TPU v7x, 32 devices: a whole 2x2x4 slice. The times are simulated.
32 devices in a mesh: sec: 4 (over z), gen: 8 (over y, x, core).
Axes of the slice: x: 2, y: 2, z: 4, core: 2. Of those that a mesh axis runs over, the one named last changes fastest.
Arguments:
- amps_left: bfloat16 [32, 4096, 256], P('sec', 'gen'), may hold values from -2 to 2
- amps_right: bfloat16 [32, 4096, 256], P('sec', 'gen'), may hold values from -2 to 2
- block_sizes: int32 [32], P('sec'), may hold values from 1 to 256, 4096 in all
- slab: bfloat16 [256, 64, 4096], P('gen', None, 'sec'), may hold values from -0.01171875 to 0.01171875
- fcore: bfloat16 [256, 64], P('gen'), may hold values from -6 to 6
Outputs:
- rdm: bfloat16 [4096, 4096], P('gen', 'sec')
- grad: float32 [256, 64], P('gen')
Inputs may be any that keep to these rules, and one draw needn't show every extreme that they name: block_sizes of all sectors sum to 4096, and some sector has exactly 256 live states.
All inputs are finite; a program needn't handle non-finite values. No bound on the sum of `block_sizes` on one device may be relied on, other than what follows from the above.
Results may differ from a plain program's by a relative error of at most 0.0029.
Values may be sent and summed in bfloat16 or wider, within the bound.
No kernel may reach another device: no remote copies, remote signals or barrier semaphores. Data moves between devices by JAX's collectives and lax.ppermute only.
A program may use at most 64 MiB of HBM per device.

v0:
```python
import functools

import jax
import jax.numpy as jnp
from jax import lax
from jax.experimental import pallas as pl
from jax.experimental.pallas import tpu as pltpu
from jax.sharding import PartitionSpec as P

CHUNKS = 4
GROUPS = ((0,), (1,), (2,), (3,))
ORDER = (
    "W0", "M0", "W1", "A1", "P0", "M1", "W2", "A2", "P1", "M2", "C0", "W3", "A3", "P2", "C1", "M3", "F0", "C2", "F1", "P3", "F2", "C3", "R", "F3",
)
LIMIT = 50 * 2**20
NT = (((1,), (1,)), ((), ()))
HBM = pl.BlockSpec(memory_space=pltpu.HBM)
VMEM = pl.BlockSpec(memory_space=pltpu.VMEM)
SMEM = pl.BlockSpec(memory_space=pltpu.SMEM)
PARAMS = pltpu.CompilerParams(vmem_limit_bytes=LIMIT)


def partial_kernel(cuts, info, left, partner, *refs):
    *pieces, near, own, far, bra, ket, bra_sem, ket_sem = refs
    sectors, rows, states = left.shape
    cols = own.shape[2]
    copies = []
    for n, (ref, index, start, r) in enumerate(cuts):
        piece = pieces[ref].at[index]
        at = pl.multiple_of((info[0] ^ r) * cols + start, 16)
        copies.append(pltpu.make_async_copy(piece, bra.at[:, pl.ds(at, piece.shape[1])], bra_sem.at[n]))
    kets = [
        pltpu.make_async_copy(ref, ket.at[c], ket_sem.at[c]) for c, ref in enumerate((left, partner))
    ]
    for copy in copies + kets:
        copy.start()
    for copy in copies:
        copy.wait()
    ids = lax.broadcasted_iota(jnp.int32, (rows, states), 1)
    for c in range(2):
        kets[c].wait()
        out = None
        for s in range(sectors):
            live = jnp.where(ids < info[1 + s], ket[c, s].astype(jnp.float32), 0.0)
            term = lax.dot_general(
                live.astype(jnp.bfloat16), bra[s], NT, preferred_element_type=jnp.float32
            )
            out = term if out is None else out + term
        blocks = [out[:, k * cols : (k + 1) * cols] for k in range(4)]
        own[c] = blocks[0]
        near[0, c] = blocks[1].astype(jnp.bfloat16)
        near[1, c] = blocks[3].astype(jnp.bfloat16)
        far[c] = blocks[2].astype(far.dtype)


def partial_products(info, left, partner, cols, cuts, *pieces):
    sectors, rows, states = left.shape

    block = (2, rows, cols)
    return pl.pallas_call(
        functools.partial(partial_kernel, cuts),
        in_specs=[SMEM] + [HBM] * (2 + len(pieces)),
        out_specs=[VMEM] * 3,
        scratch_shapes=[
            pltpu.VMEM((sectors, 4 * cols, states), jnp.bfloat16),
            pltpu.VMEM((2, sectors, rows, states), jnp.bfloat16),
            pltpu.SemaphoreType.DMA((len(cuts),)),
            pltpu.SemaphoreType.DMA((2,)),
        ],
        out_shape=[
            jax.ShapeDtypeStruct((2, *block), jnp.bfloat16),
            jax.ShapeDtypeStruct(block, jnp.float32),
            jax.ShapeDtypeStruct(block, jnp.float32),
        ],
        compiler_params=PARAMS,
        name="partial_products",
    )(info, left, partner, *pieces)


def combine_kernel(chunk, position, core, mine, a, b, *refs):
    rdm, others, turned, own, other, block, sems = refs[-7:]
    rows, cols = own.shape
    f32 = jnp.float32
    total = (mine[...] + a[0].astype(f32)) + b[...].astype(f32)
    own[...] = total[0].astype(jnp.bfloat16)
    other[...] = total[1].astype(jnp.bfloat16)
    at = pl.multiple_of(core[0] * rows + chunk * cols, 128)
    copies = [
        pltpu.make_async_copy(own, rdm.at[:, pl.ds(at, cols)], sems.at[0]),
        pltpu.make_async_copy(other, others.at[:, pl.ds(chunk * cols, cols)], sems.at[1]),
        pltpu.make_async_copy(block, turned.at[position], sems.at[2]),
    ]
    for copy in copies[:2]:
        copy.start()
    width = block.shape[0]
    by_row = total.reshape(2 * rows // width, width, cols)
    block[...] = jnp.swapaxes(by_row, 0, 1).astype(jnp.bfloat16)
    copies[2].start()
    for copy in copies:
        copy.wait()


def combine(chunk, group, core, mine, near, far, width, pair_cols, held):
    _, rows, cols = mine.shape
    bf16 = jnp.bfloat16
    block = (width, 2 * rows // width, cols)
    return pl.pallas_call(
        functools.partial(combine_kernel, chunk, group.index(chunk)),
        in_specs=[SMEM] + [VMEM] * 3 + [HBM] * len(held),
        out_specs=[HBM] * 3,
        out_shape=[
            jax.ShapeDtypeStruct((rows, pair_cols), bf16),
            jax.ShapeDtypeStruct((rows, pair_cols // 2), bf16),
            jax.ShapeDtypeStruct((len(group), *block), bf16),
        ],
        scratch_shapes=[pltpu.VMEM((rows, cols), bf16)] * 2
        + [pltpu.VMEM(block, bf16), pltpu.SemaphoreType.DMA((3,))],
        input_output_aliases={4 + i: i for i in range(len(held))},
        compiler_params=PARAMS,
        name="combine",
    )(core, mine, near, far, *held)


def place_kernel(core, other, held, rdm, sem):
    rows = other.shape[1]
    at = pl.multiple_of((1 - core[0]) * rows, 128)
    copy = pltpu.make_async_copy(other, rdm.at[:, pl.ds(at, rows)], sem)
    copy.start()
    copy.wait()


def place(core, other, rdm):
    return pl.pallas_call(
        place_kernel,
        in_specs=[SMEM, VMEM, HBM],
        out_specs=HBM,
        out_shape=jax.ShapeDtypeStruct(rdm.shape, rdm.dtype),
        scratch_shapes=[pltpu.SemaphoreType.DMA],
        input_output_aliases={2: 0},
        compiler_params=PARAMS,
        name="place",
    )(core, other, rdm)


def fock_kernel(first, base, slab, diagonal, *refs):
    *pieces, fock, traced, part, rdm, sems = refs
    width, orbitals, total = part.shape
    chunks, _, _, cols = pieces[0].shape
    copies = [pltpu.make_async_copy(slab.at[:, :, pl.ds(first * cols, total)], part, sems.at[4])]
    for r in range(4):
        piece = pieces[r] if len(pieces) == 4 else pieces[min(r, 2)]
        if len(pieces) == 3 and r >= 2:
            piece = piece.at[pl.ds((r - 2) * chunks, chunks)]
        copies.append(pltpu.make_async_copy(piece, rdm.at[base[0] ^ r], sems.at[r]))
    for copy in copies:
        copy.start()
    for copy in copies:
        copy.wait()
    acc = jnp.zeros((orbitals, width), jnp.float32)
    for u in range(width):
        trace = None
        for n in range(chunks):
            at = slice(n * cols, (n + 1) * cols)
            lhs = jnp.concatenate([part[u, :, at], diagonal[:, at]], axis=0)
            rhs = jnp.concatenate([rdm[c, n, u] for c in range(4)], axis=0)
            out = lax.dot_general(lhs, rhs, NT, preferred_element_type=jnp.float32)
            acc += out[:orbitals]
            trace = out[orbitals] if trace is None else trace + out[orbitals]
        traced[u, :] = trace
    fock[...] = acc


def fock_terms(first, base, slab, diagonal, *pieces):
    width, orbitals, _ = slab.shape
    chunks, _, _, cols = pieces[0].shape
    return pl.pallas_call(
        functools.partial(fock_kernel, first),
        in_specs=[SMEM, HBM, VMEM] + [HBM] * len(pieces),
        out_specs=[VMEM] * 2,
        out_shape=[
            jax.ShapeDtypeStruct((orbitals, width), jnp.float32),
            jax.ShapeDtypeStruct((width, width), jnp.float32),
        ],
        scratch_shapes=[
            pltpu.VMEM((width, orbitals, chunks * cols), jnp.bfloat16),
            pltpu.VMEM((4, *pieces[0].shape), jnp.bfloat16),
            pltpu.SemaphoreType.DMA((5,)),
        ],
        compiler_params=PARAMS,
        name="fock_terms",
    )(base, slab, diagonal, *pieces)


def turn_kernel(core, a, b, o):
    size = a.shape[0]
    o[:, :size] = jnp.swapaxes(a[...].astype(jnp.float32), 0, 1).astype(jnp.bfloat16)
    o[:, size:] = jnp.swapaxes(b[...].astype(jnp.float32), 0, 1).astype(jnp.bfloat16)


def turn(core, slab, received, cols):
    orbitals, width, total = received.shape
    steps = total // cols
    return pl.pallas_call(
        turn_kernel,
        grid_spec=pltpu.PrefetchScalarGridSpec(
            num_scalar_prefetch=1,
            grid=(steps,),
            in_specs=[
                pl.BlockSpec((orbitals, width, cols), lambda i, core: (0, 0, core[0] * steps + i)),
                pl.BlockSpec((orbitals, width, cols), lambda i, core: (0, 0, i)),
            ],
            out_specs=pl.BlockSpec((width, 2 * orbitals, cols), lambda i, core: (0, 0, i)),
        ),
        out_shape=jax.ShapeDtypeStruct((width, 2 * orbitals, total), jnp.bfloat16),
        compiler_params=PARAMS,
        name="turn",
    )(core, slab, received)


def after(value, *done):
    done = jax.tree.leaves(done)
    return lax.optimization_barrier((value, *done))[0]


def shards(secs, gens, amps_left, amps_right, block_sizes, slab, fcore):
    sectors, rows, states = amps_left.shape
    general, width, pair_cols = slab.shape
    cols = rows // CHUNKS
    half = cols // 2
    z = lax.axis_index("sec")
    g = lax.axis_index("gen")
    chip, core = g // 2, g % 2

    def across(value, flip):
        return lax.ppermute(value, "gen", [(i, i ^ flip) for i in range(gens)])

    def along(value, flip):
        return lax.ppermute(value, "sec", [(i, i ^ flip) for i in range(secs)])

    def number(value):
        return value.reshape(1).astype(jnp.int32)

    def bra(chunk, source):
        return source[:, chunk * cols : (chunk + 1) * cols]

    sent = bra(0, amps_right)
    pieces = {}
    if ORDER[0] == "W0":
        xs, ys = across(sent, 2), across(sent, 4)
    else:
        pieces[0] = [across(sent, 2 * r) for r in (1, 2, 3)]
    partner_left = across(amps_left, 1)
    later = after(amps_right, sent)
    waiting = [None] + [bra(chunk, later) for chunk in range(1, CHUNKS)]

    given = lax.dynamic_slice(after(slab, sent), (0, 0, (1 - core) * rows), (general, width, rows))
    received, *waiting[1:] = lax.optimization_barrier((across(given, 1), *waiting[1:]))
    integrals = turn(number(core), slab, received, cols)

    column_ids = z * pair_cols + core * rows + jnp.arange(rows, dtype=jnp.int32)
    diagonal = jnp.broadcast_to(
        (column_ids // width == column_ids % width).astype(jnp.bfloat16)[None], (16, rows)
    )

    def products(chunk, *parts):
        mine = slice(chunk * cols, (chunk + 1) * cols)
        every = slice(None)
        cuts = [(0, (every, mine), 0, 0)] + [(n, (every,), 0, n) for n in range(1, 4)]
        if len(parts) == 4:
            cuts.append((4, (every,), half, 3))
        info = jnp.concatenate([number(chip ^ z), block_sizes])
        return partial_products(info, amps_left, partner_left, cols, cuts, amps_right, *parts)

    sums, terms, gathered = [None] * CHUNKS, [], {}

    def contract(group):
        at = slice(group[0] * cols, (group[-1] + 1) * cols)
        marks = after(diagonal[:, at], state["last"])
        terms.append(fock_terms(group[0], number(chip), integrals, marks, *gathered[group]))
        state["last"] = terms[-1][0]

    if 0 in pieces:
        state = {"last": (), "held": ()}
        sent = after(waiting[1], *pieces[0], integrals)
        state["xs"], state["ys"] = across(sent, 2), across(sent, 4)
    else:
        state = {"last": integrals, "held": (), "xs": xs, "ys": ys}

    def do_forward(chunk):
        last = state["last"]
        xs, ys = after(state["xs"], last), after(state["ys"], last)
        lower, upper = xs[:, :half], ys[:, half:]
        pieces[chunk] = (xs, ys, across(lower, 4), across(upper, 2))
        state["last"] = (lower, upper)
        if chunk + 1 < CHUNKS:
            sent = after(waiting[chunk + 1], xs, ys)
            state["xs"], state["ys"] = across(sent, 2), across(sent, 4)

    def do_products(chunk):
        near, own, far = products(chunk, *(after(p, state["last"]) for p in pieces[chunk]))
        sums[chunk] = [own, along(near, 1), far]
        state["last"] = own

    def do_pass(chunk):
        own, near, far = sums[chunk]
        far = after(far, state["last"])
        passed = (far + near[1].astype(jnp.float32)).astype(jnp.bfloat16)
        sums[chunk] = [own, near, along(passed, 2)]
        state["last"] = passed

    def do_finish(chunk):
        own, near, far = sums[chunk]
        group = [g for g in GROUPS if chunk in g][0]
        held = state["held"] if chunk > group[0] else state["held"][:2]
        state["held"] = combine(
            chunk, group, number(core), after(own, state["last"]), near, far, width, pair_cols, held
        )
        turned = state["held"][2]
        if chunk == group[-1]:
            if True:
                gathered[group] = (turned, *[across(turned, 2 * r) for r in (1, 2, 3)])
            else:
                gathered[group] = (turned, across(turned, 2))
        state["last"] = state["held"][1]

    def do_second(chunk):
        group = [g for g in GROUPS if chunk in g][0]
        both = jnp.concatenate([after(p, state["last"]) for p in gathered[group]], axis=0)
        gathered[group] += (across(both, 4),)
        state["last"] = both

    def do_wait(chunk):
        state["last"] = (state["last"], *pieces[chunk][2:])

    steps = {
        "W": do_forward,
        "A": do_wait,
        "M": do_products,
        "P": do_pass,
        "C": do_finish,
        "H": do_second,
        "F": lambda chunk: contract([g for g in GROUPS if chunk in g][0]),
    }
    for step in ORDER:
        if step == "R":
            rdm = place(number(core), across(state["held"][1], 1), state["held"][0])
            state["last"] = rdm
        else:
            steps[step[0]](int(step[1]))

    two_body = sum(t[0] for t in terms)
    traced = sum(t[1] for t in terms)

    def ordered(value):
        split = value.reshape(value.shape[0], 4, 2, -1)
        return jnp.where(core == 0, split, split[:, :, ::-1]).reshape(value.shape)

    one = ordered(traced).T / width
    both = jnp.concatenate([fcore, across(fcore, 1)], axis=0).astype(jnp.float32)
    mine = ordered(two_body) + jnp.dot(both, one, precision=lax.Precision.HIGHEST)
    theirs = across(mine, 1)
    fock = mine[:general] + theirs[general:]
    partner = mine[general:] + theirs[:general]

    first = jnp.where(core == 0, fock, partner)
    second = jnp.where(core == 0, partner, fock)
    active = jnp.concatenate([first, second], axis=0)
    flipped = lax.dynamic_slice_in_dim(active.T, core * general, general, axis=0)
    part = 2.0 * (fock - jnp.where(g < 2, flipped, 0.0))
    for flip in (1, 2):
        part = part + along(part, flip)
    return rdm, part


def general_shards(secs, gens, amps_left, amps_right, block_sizes, slab, fcore):
    sectors, rows, states = amps_left.shape
    general, width, pair_cols = slab.shape
    chips = gens // 2
    per_sec = chips // secs
    bits = chips.bit_length() - 1
    chunks = 1
    half = rows // chunks // 2
    z = lax.axis_index("sec")
    g = lax.axis_index("gen")
    chip, core = g // 2, g % 2

    def across(value, flip):
        return lax.ppermute(value, "gen", [(i, i ^ flip) for i in range(gens)])

    def along(value, flip):
        return lax.ppermute(value, "sec", [(i, i ^ flip) for i in range(secs)])

    def gather(value, order):
        held = value[None]
        for bit in order:
            held = jnp.concatenate([held, across(held, 2 << bit)], axis=0)
        return held

    def place(relative, order):
        return sum(((relative >> bit) & 1) << at for at, bit in enumerate(order))

    orders = (tuple(range(bits)), tuple(reversed(range(bits))))
    live = (jnp.arange(states, dtype=jnp.int32)[None, :] < block_sizes[:, None]).astype(jnp.bfloat16)

    left = jnp.concatenate([amps_left, across(amps_left, 1)], axis=1) * live[:, None, :]

    by_core = slab.reshape(general, width, per_sec, 2, rows)
    kept = lax.dynamic_index_in_dim(by_core, core, 3, keepdims=False)
    given = lax.dynamic_index_in_dim(by_core, 1 - core, 3, keepdims=False)
    integrals = jnp.concatenate([kept, across(given, 1)], axis=0)

    column_ids = (
        z * pair_cols
        + jnp.arange(per_sec, dtype=jnp.int32)[:, None] * (2 * rows)
        + core * rows
        + jnp.arange(rows, dtype=jnp.int32)[None, :]
    )
    diagonal = (column_ids // width == column_ids % width).astype(jnp.bfloat16)

    pieces = []
    two_body = jnp.zeros((2 * general, width), jnp.float32)
    traced = jnp.zeros((width, width), jnp.float32)
    for chunk in range(chunks):
        start = chunk * 2 * half
        blocks = [
            gather(amps_right[:, start + i * half : start + (i + 1) * half], orders[i])
            for i in range(2)
        ]

        def partial_for(dest):
            wanted = chip ^ (dest * per_sec + jnp.arange(per_sec, dtype=jnp.int32))
            found = [
                jnp.take(blocks[i], place(wanted, orders[i]), axis=0) for i in range(2)
            ]
            right = jnp.concatenate(found, axis=2)
            return jnp.einsum(
                "srm,csqm->rcq", left, right, preferred_element_type=jnp.float32
            )

        arrived = [
            along(partial_for(z ^ flip).astype(jnp.bfloat16), flip) for flip in range(1, secs)
        ]
        total = partial_for(z)
        for value in arrived:
            total = total + value.astype(jnp.float32)
        piece = total.astype(jnp.bfloat16)
        pieces.append(piece)

        columns = per_sec * 2 * half
        by_row = piece.reshape(2, rows // width, width, columns)
        halves = [gather(by_row[i], orders[i]) for i in range(2)]
        table = jnp.arange(chips, dtype=jnp.int32)
        halves[1] = halves[1][jnp.array([sum(((p >> b) & 1) << a for a, b in enumerate(orders[1])) for p in range(chips)])]
        every = jnp.stack(halves, axis=1).reshape(width, width, columns)
        part = integrals[:, :, :, start : start + 2 * half].reshape(2 * general, width, columns)
        two_body = two_body + jnp.einsum(
            "puq,tuq->pt", part, every, preferred_element_type=jnp.float32
        )
        traced = traced + jnp.einsum(
            "tuq,q->tu",
            every,
            diagonal[:, start : start + 2 * half].reshape(columns),
            preferred_element_type=jnp.float32,
        )

    def ordered(value, axis):
        shape = value.shape
        split = value.reshape(shape[:axis] + (gens, shape[axis] // gens) + shape[axis + 1 :])
        return jnp.take(split, g ^ jnp.arange(gens), axis=axis).reshape(shape)

    two_body = ordered(two_body, 1)
    one = ordered(traced, 0) / width
    both = jnp.concatenate([fcore, across(fcore, 1)], axis=0).astype(jnp.float32)
    mine = two_body + jnp.dot(both, one, precision=lax.Precision.HIGHEST)
    theirs = across(mine, 1)
    fock = mine[:general] + theirs[general:]
    partner = mine[general:] + theirs[:general]

    first = jnp.where(core == 0, fock, partner)
    second = jnp.where(core == 0, partner, fock)
    active = jnp.concatenate([first, second], axis=0)
    flipped = lax.dynamic_slice_in_dim(active.T, core * general, general, axis=0)
    part = 2.0 * (fock - jnp.where(g < 2, flipped, 0.0))
    parts = [part] + [along(part, flip) for flip in range(1, secs)]
    while len(parts) > 1:
        parts = [a + b for a, b in zip(parts[::2], parts[1::2])]
    grad = parts[0]

    own = jnp.concatenate([p[:rows] for p in pieces], axis=2)
    other = across(jnp.concatenate([p[rows:] for p in pieces], axis=2), 1)
    lower = jnp.where(core == 0, own, other)
    upper = jnp.where(core == 0, other, own)
    rdm = jnp.stack([lower, upper], axis=2).reshape(rows, pair_cols)
    return rdm, grad


def solution(mesh):
    secs, gens = mesh.shape["sec"], mesh.shape["gen"]
    placed = (
        P("sec", "gen", None),
        P("sec", "gen", None),
        P("sec"),
        P("gen", None, "sec"),
        P("gen", None),
    )
    def step(*args):
        rows, general, width = args[0].shape[1], args[3].shape[0], args[3].shape[1]
        fits = secs == 4 and gens == 8 and 2 * general == width and rows == 128 * CHUNKS
        return (shards if fits else general_shards)(secs, gens, *args)

    return jax.shard_map(
        step,
        mesh=mesh,
        in_specs=placed,
        out_specs=(P("gen", "sec"), P("gen", None)),
        check_vma=False,
    )
```

profile of v0, /device:TPU:0, one launch (start us, length us, event | category | flops | bytes accessed | tf_op | source)
XLA Modules:
  0.0 164.5 jit_solution(5914545461437208525)
XLA Ops:
  1.8 2.0 %constant_dynamic-slice_fusion = bf16[32,64,512]{2,1,0:T(8,128)(2,1)S(1)} fusion(bf16[32,64,1024]{2,1,0:T(8,128)(2,1)} %a.1, s32[]{:T(128)S(6)} %select_n.79), kind=kLoop, calls=%fused_computation.36 | loop fusion | bytes 4194308 | tf_op jit(solution)/shard_map/dynamic_slice | solution.py:256
  4.3 2.9 %collective-permute-start.3 = (bf16[8,128,256]{2,1,0:T(8,128)(2,1)S(1)}, bf16[8,128,256]{2,1,0:T(8,128)(2,1)S(1)}, u32[]{:S(2)}, u32[]{:S(2)}) collective-permute-start(bf16[8,128,256]{2,1,0:T(8,128)(2,1)S(1)} %slice.88), channel_id=1, source_target_pairs={{0,4},{1,5},{2,6},{3,7},{4,0},{5,1},{6,2},{7,3},{8,12},{9,13},{10,... | collective-permute-start | bytes 1572872 | tf_op jit(solution)/shard_map/ppermute | solution.py:235
  7.3 1.5 collective-permute-start.2
  10.2 5.2 %turn.1.slab = bf16[64,64,512]{2,1,0:T(8,128)(2,1)} custom-call(s32[1]{0:T(128)} %bitcast.core, bf16[32,64,1024]{2,1,0:T(8,128)(2,1)} %a.1, bf16[32,64,512]{2,1,0:T(8,128)(2,1)S(1)} %collective-permute-done.1.b), custom_call_target="tpu_custom_call" | custom-call | tf_op jit(solution)/shard_map/turn/pallas_call | solution.py:203
  15.4 4.0 %collective-permute-done.3.refs_2_ = bf16[8,128,256]{2,1,0:T(8,128)(2,1)S(1)} collective-permute-done((bf16[8,128,256]{2,1,0:T(8,128)(2,1)S(1)}, bf16[8,128,256]{2,1,0:T(8,128)(2,1)S(1)}, u32[]{:S(2)}, u32[]{:S(2)}) %collective-permute-start.3) | collective-permute-done | bytes 524320 | tf_op jit(solution)/shard_map/ppermute | solution.py:235
  19.4 1.5 collective-permute-done.2.refs_1_
  21.2 1.8 %collective-permute-start.6 = (bf16[8,64,256]{2,1,0:T(8,128)(2,1)S(1)}, bf16[8,64,256]{2,1,0:T(8,128)(2,1)S(1)}, u32[]{:S(2)}, u32[]{:S(2)}) collective-permute-start(bf16[8,64,256]{2,1,0:T(8,128)(2,1)S(1)} %slice.93), channel_id=1, source_target_pairs={{0,2},{1,3},{2,0},{3,1},{4,6},{5,7},{6,4},{7,5},{8,10},{9,11},{10,... | collective-permute-start | bytes 786440 | tf_op jit(solution)/shard_map/ppermute | solution.py:235
  23.7 1.5 collective-permute-start.5
  25.8 4.7 %collective-permute-done.6.refs_4_ = bf16[8,64,256]{2,1,0:T(8,128)(2,1)S(1)} collective-permute-done((bf16[8,64,256]{2,1,0:T(8,128)(2,1)S(1)}, bf16[8,64,256]{2,1,0:T(8,128)(2,1)S(1)}, u32[]{:S(2)}, u32[]{:S(2)}) %collective-permute-start.6) | collective-permute-done | bytes 262176 | tf_op jit(solution)/shard_map/ppermute | solution.py:235
  30.5 9.0 %collective-permute-done.5.refs_3_ = bf16[8,64,256]{2,1,0:T(8,128)(2,1)S(1)} collective-permute-done((bf16[8,64,256]{2,1,0:T(8,128)(2,1)}, bf16[8,64,256]{2,1,0:T(8,128)(2,1)S(1)}, u32[]{:S(2)}, u32[]{:S(2)}) %collective-permute-start.5) | collective-permute-done | bytes 262176 | tf_op jit(solution)/shard_map/ppermute | solution.py:235
  39.5 5.0 %partial_products.4 = (bf16[2,2,512,128]{3,2,1,0:T(8,128)(2,1)S(1)}, f32[2,512,128]{2,1,0:T(8,128)S(1)}, f32[2,512,128]{2,1,0:T(8,128)S(1)}) custom-call(s32[9]{0:T(128)S(1)} %pad_add_fusion.info, bf16[8,512,256]{2,1,0:T(8,128)(2,1)} %left.7, bf16[8,512,256]{2,1,0:T(8,128)(2,1)} %collective-permute-done.partner, bf16[8,512,256]{2,1,0:T(8,128)(2,1)} %refs_0_.7, ...), custom_call_target="tpu_custom_call" | custom-call | tf_op jit(solution)/shard_map/partial_products/pallas_call | solution.py:60
  44.4 1.6 collective-permute-start.11
  46.1 1.6 collective-permute-start.10
  48.3 1.4 collective-permute-start.12
  50.3 5.1 %collective-permute-done.10.refs_4_ = bf16[8,64,256]{2,1,0:T(8,128)(2,1)S(1)} collective-permute-done((bf16[8,64,256]{2,1,0:T(8,128)(2,1)S(1)}, bf16[8,64,256]{2,1,0:T(8,128)(2,1)S(1)}, u32[]{:S(2)}, u32[]{:S(2)}) %collective-permute-start.10) | collective-permute-done | bytes 262176 | tf_op jit(solution)/shard_map/ppermute | solution.py:235
  55.4 1.6 collective-permute-done.9.refs_3_
  57.0 5.0 %partial_products.5 = (bf16[2,2,512,128]{3,2,1,0:T(8,128)(2,1)S(1)}, f32[2,512,128]{2,1,0:T(8,128)S(1)}, f32[2,512,128]{2,1,0:T(8,128)S(1)}) custom-call(s32[9]{0:T(128)S(1)} %pad_add_fusion.info, bf16[8,512,256]{2,1,0:T(8,128)(2,1)} %left.7, bf16[8,512,256]{2,1,0:T(8,128)(2,1)} %collective-permute-done.partner, bf16[8,512,256]{2,1,0:T(8,128)(2,1)} %refs_0_.7, ...), custom_call_target="tpu_custom_call" | custom-call | tf_op jit(solution)/shard_map/partial_products/pallas_call | solution.py:60
  63.0 2.1 %collective-permute-done.12.refs_2_ = bf16[8,128,256]{2,1,0:T(8,128)(2,1)S(1)} collective-permute-done((bf16[8,128,256]{2,1,0:T(8,128)(2,1)S(1)}, bf16[8,128,256]{2,1,0:T(8,128)(2,1)S(1)}, u32[]{:S(2)}, u32[]{:S(2)}) %collective-permute-start.12) | collective-permute-done | bytes 524320 | tf_op jit(solution)/shard_map/ppermute | solution.py:235
  66.0 1.3 collective-permute-start.18
  67.4 1.9 %collective-permute-start.13 = (bf16[8,128,256]{2,1,0:T(8,128)(2,1)S(1)}, bf16[8,128,256]{2,1,0:T(8,128)(2,1)S(1)}, u32[]{:S(2)}, u32[]{:S(2)}) collective-permute-start(bf16[8,128,256]{2,1,0:T(8,128)(2,1)S(1)} %get-tuple-element.106), channel_id=1, source_target_pairs={{0,2},{1,3},{2,0},{3,1},{4,6},{5,7},{6,4},{7,5},{8,10},{9,11},{10,... | collective-permute-start | bytes 1572872 | tf_op jit(solution)/shard_map/ppermute | solution.py:235
  69.3 5.1 %collective-permute-done.15.refs_4_ = bf16[8,64,256]{2,1,0:T(8,128)(2,1)S(1)} collective-permute-done((bf16[8,64,256]{2,1,0:T(8,128)(2,1)S(1)}, bf16[8,64,256]{2,1,0:T(8,128)(2,1)S(1)}, u32[]{:S(2)}, u32[]{:S(2)}) %collective-permute-start.15) | collective-permute-done | bytes 262176 | tf_op jit(solution)/shard_map/ppermute | solution.py:235
  74.4 2.6 %collective-permute-start.17 = (bf16[2,512,128]{2,1,0:T(8,128)(2,1)S(1)}, bf16[2,512,128]{2,1,0:T(8,128)(2,1)S(1)}, u32[]{:S(2)}, u32[]{:S(2)}) collective-permute-start(bf16[2,512,128]{2,1,0:T(8,128)(2,1)S(1)} %fusion.3), channel_id=1, source_target_pairs={{0,16},{8,24},{16,0},{24,8},{1,17},{9,25},{17,1},{25,9},{2,18},{10... | collective-permute-start | bytes 786440 | tf_op jit(solution)/shard_map/ppermute | solution.py:238
  77.0 5.0 %partial_products.6 = (bf16[2,2,512,128]{3,2,1,0:T(8,128)(2,1)S(1)}, f32[2,512,128]{2,1,0:T(8,128)S(1)}, f32[2,512,128]{2,1,0:T(8,128)S(1)}) custom-call(s32[9]{0:T(128)S(1)} %pad_add_fusion.info, bf16[8,512,256]{2,1,0:T(8,128)(2,1)} %left.7, bf16[8,512,256]{2,1,0:T(8,128)(2,1)} %collective-permute-done.partner, bf16[8,512,256]{2,1,0:T(8,128)(2,1)} %refs_0_.7, ...), custom_call_target="tpu_custom_call" | custom-call | tf_op jit(solution)/shard_map/partial_products/pallas_call | solution.py:60
  82.5 2.8 %collective-permute-done.17.b = bf16[2,512,128]{2,1,0:T(8,128)(2,1)S(1)} collective-permute-done((bf16[2,512,128]{2,1,0:T(8,128)(2,1)S(1)}, bf16[2,512,128]{2,1,0:T(8,128)(2,1)S(1)}, u32[]{:S(2)}, u32[]{:S(2)}) %collective-permute-start.17) | collective-permute-done | bytes 262176 | tf_op jit(solution)/shard_map/ppermute | solution.py:238
  87.2 1.7 %collective-permute-start.22 = (bf16[2,512,128]{2,1,0:T(8,128)(2,1)S(1)}, bf16[2,512,128]{2,1,0:T(8,128)(2,1)S(1)}, u32[]{:S(2)}, u32[]{:S(2)}) collective-permute-start(bf16[2,512,128]{2,1,0:T(8,128)(2,1)S(1)} %fusion.2), channel_id=1, source_target_pairs={{0,16},{8,24},{16,0},{24,8},{1,17},{9,25},{17,1},{25,9},{2,18},{10... | collective-permute-start | bytes 786440 | tf_op jit(solution)/shard_map/ppermute | solution.py:238
  88.9 1.8 %collective-permute-start.23 = (bf16[1,64,16,128]{3,2,1,0:T(8,128)(2,1)S(1)}, bf16[1,64,16,128]{3,2,1,0:T(8,128)(2,1)}, u32[]{:S(2)}, u32[]{:S(2)}) collective-permute-start(bf16[1,64,16,128]{3,2,1,0:T(8,128)(2,1)S(1)} %get-tuple-element.132.refs_0_), channel_id=1, source_target_pairs={{0,2},{1,3},{2,0},{3,1},{4,6},{5,7},{6,4},{7,5},{8,10},{9,11},{10,... | collective-permute-start | bytes 786440 | tf_op jit(solution)/shard_map/ppermute | solution.py:235
  90.7 2.3 %collective-permute-done.20.refs_4_ = bf16[8,64,256]{2,1,0:T(8,128)(2,1)S(1)} collective-permute-done((bf16[8,64,256]{2,1,0:T(8,128)(2,1)S(1)}, bf16[8,64,256]{2,1,0:T(8,128)(2,1)S(1)}, u32[]{:S(2)}, u32[]{:S(2)}) %collective-permute-start.20) | collective-permute-done | bytes 262176 | tf_op jit(solution)/shard_map/ppermute | solution.py:235
  94.6 1.1 collective-permute-start.25
  99.4 5.7 %partial_products.7 = (bf16[2,2,512,128]{3,2,1,0:T(8,128)(2,1)}, f32[2,512,128]{2,1,0:T(8,128)S(1)}, f32[2,512,128]{2,1,0:T(8,128)S(1)}) custom-call(s32[9]{0:T(128)S(1)} %pad_add_fusion.info, bf16[8,512,256]{2,1,0:T(8,128)(2,1)} %left.7, bf16[8,512,256]{2,1,0:T(8,128)(2,1)} %collective-permute-done.partner, bf16[8,512,256]{2,1,0:T(8,128)(2,1)} %refs_0_.7, ...), custom_call_target="tpu_custom_call" | custom-call | tf_op jit(solution)/shard_map/partial_products/pallas_call | solution.py:60
  105.7 2.4 %collective-permute-start.26 = (bf16[2,512,128]{2,1,0:T(8,128)(2,1)}, bf16[2,512,128]{2,1,0:T(8,128)(2,1)S(1)}, u32[]{:S(2)}, u32[]{:S(2)}) collective-permute-start(bf16[2,512,128]{2,1,0:T(8,128)(2,1)} %fusion.1), channel_id=1, source_target_pairs={{0,16},{8,24},{16,0},{24,8},{1,17},{9,25},{17,1},{25,9},{2,18},{10... | collective-permute-start | bytes 786440 | tf_op jit(solution)/shard_map/ppermute | solution.py:238
  110.3 1.3 collective-permute-start.29
  111.7 2.3 %fock_terms.4 = (f32[64,64]{1,0:T(8,128)S(1)}, f32[64,64]{1,0:T(8,128)S(1)}) custom-call(s32[1]{0:T(128)} %bitcast.5.base, bf16[64,64,512]{2,1,0:T(8,128)(2,1)} %turn.1.slab, bf16[16,128]{1,0:T(8,128)(2,1)S(1)} %broadcast_in_dim.18.diagonal, bf16[1,64,16,128]{3,2,1,0:T(8,128)(2,1)S(1)} %get-tuple-element.132.refs_0_, ...), custom_call_target="tpu_custom_call" | custom-call | tf_op jit(solution)/shard_map/fock_terms/pallas_call | solution.py:176
  114.0 3.6 %collective-permute-done.26.b = bf16[2,512,128]{2,1,0:T(8,128)(2,1)S(1)} collective-permute-done((bf16[2,512,128]{2,1,0:T(8,128)(2,1)}, bf16[2,512,128]{2,1,0:T(8,128)(2,1)S(1)}, u32[]{:S(2)}, u32[]{:S(2)}) %collective-permute-start.26) | collective-permute-done | bytes 262176 | tf_op jit(solution)/shard_map/ppermute | solution.py:238
  118.7 1.1 collective-permute-start.32
  119.8 2.2 %collective-permute-start.33 = (bf16[1,64,16,128]{3,2,1,0:T(8,128)(2,1)S(1)}, bf16[1,64,16,128]{3,2,1,0:T(8,128)(2,1)S(1)}, u32[]{:S(2)}, u32[]{:S(2)}) collective-permute-start(bf16[1,64,16,128]{3,2,1,0:T(8,128)(2,1)S(1)} %get-tuple-element.143.refs_0_), channel_id=1, source_target_pairs={{0,6},{1,7},{2,4},{3,5},{4,2},{5,3},{6,0},{7,1},{8,14},{9,15},{10,... | collective-permute-start | bytes 786440 | tf_op jit(solution)/shard_map/ppermute | solution.py:235
  122.0 2.1 %fock_terms.5 = (f32[64,64]{1,0:T(8,128)S(1)}, f32[64,64]{1,0:T(8,128)S(1)}) custom-call(s32[1]{0:T(128)} %bitcast.5.base, bf16[64,64,512]{2,1,0:T(8,128)(2,1)} %turn.1.slab, bf16[16,128]{1,0:T(8,128)(2,1)S(1)} %broadcast_in_dim.17.diagonal, bf16[1,64,16,128]{3,2,1,0:T(8,128)(2,1)S(1)} %copy-done.1, ...), custom_call_target="tpu_custom_call" | custom-call | tf_op jit(solution)/shard_map/fock_terms/pallas_call | solution.py:176
  124.2 3.3 %collective-permute-start.34 = (bf16[2,512,128]{2,1,0:T(8,128)(2,1)S(1)}, bf16[2,512,128]{2,1,0:T(8,128)(2,1)S(1)}, u32[]{:S(2)}, u32[]{:S(2)}) collective-permute-start(bf16[2,512,128]{2,1,0:T(8,128)(2,1)S(1)} %fusion), channel_id=1, source_target_pairs={{0,16},{8,24},{16,0},{24,8},{1,17},{9,25},{17,1},{25,9},{2,18},{10... | collective-permute-start | bytes 786440 | tf_op jit(solution)/shard_map/ppermute | solution.py:238
  127.6 2.3 %collective-permute-done.32.refs_2_ = bf16[1,64,16,128]{3,2,1,0:T(8,128)(2,1)S(1)} collective-permute-done((bf16[1,64,16,128]{3,2,1,0:T(8,128)(2,1)S(1)}, bf16[1,64,16,128]{3,2,1,0:T(8,128)(2,1)S(1)}, u32[]{:S(2)}, u32[]{:S(2)}) %collective-permute-start.32) | collective-permute-done | bytes 262176 | tf_op jit(solution)/shard_map/ppermute | solution.py:235
  129.8 2.1 %fock_terms.6 = (f32[64,64]{1,0:T(8,128)S(1)}, f32[64,64]{1,0:T(8,128)S(1)}) custom-call(s32[1]{0:T(128)} %bitcast.5.base, bf16[64,64,512]{2,1,0:T(8,128)(2,1)} %turn.1.slab, bf16[16,128]{1,0:T(8,128)(2,1)S(1)} %broadcast_in_dim.16.diagonal, bf16[1,64,16,128]{3,2,1,0:T(8,128)(2,1)S(1)} %get-tuple-element.143.refs_0_, ...), custom_call_target="tpu_custom_call" | custom-call | tf_op jit(solution)/shard_map/fock_terms/pallas_call | solution.py:176
  131.9 2.8 %collective-permute-done.34.b = bf16[2,512,128]{2,1,0:T(8,128)(2,1)S(1)} collective-permute-done((bf16[2,512,128]{2,1,0:T(8,128)(2,1)S(1)}, bf16[2,512,128]{2,1,0:T(8,128)(2,1)S(1)}, u32[]{:S(2)}, u32[]{:S(2)}) %collective-permute-start.34) | collective-permute-done | bytes 262176 | tf_op jit(solution)/shard_map/ppermute | solution.py:238
  136.7 2.5 %collective-permute-start.38 = (bf16[1,64,16,128]{3,2,1,0:T(8,128)(2,1)S(1)}, bf16[1,64,16,128]{3,2,1,0:T(8,128)(2,1)S(1)}, u32[]{:S(2)}, u32[]{:S(2)}) collective-permute-start(bf16[1,64,16,128]{3,2,1,0:T(8,128)(2,1)S(1)} %get-tuple-element.150.refs_0_), channel_id=1, source_target_pairs={{0,6},{1,7},{2,4},{3,5},{4,2},{5,3},{6,0},{7,1},{8,14},{9,15},{10,... | collective-permute-start | bytes 786440 | tf_op jit(solution)/shard_map/ppermute | solution.py:235
  140.0 4.8 %collective-permute-done.36.refs_1_ = bf16[1,64,16,128]{3,2,1,0:T(8,128)(2,1)S(1)} collective-permute-done((bf16[1,64,16,128]{3,2,1,0:T(8,128)(2,1)S(1)}, bf16[1,64,16,128]{3,2,1,0:T(8,128)(2,1)S(1)}, u32[]{:S(2)}, u32[]{:S(2)}) %collective-permute-start.36) | collective-permute-done | bytes 262176 | tf_op jit(solution)/shard_map/ppermute | solution.py:235
  144.8 5.5 %collective-permute-done.38.refs_3_ = bf16[1,64,16,128]{3,2,1,0:T(8,128)(2,1)S(1)} collective-permute-done((bf16[1,64,16,128]{3,2,1,0:T(8,128)(2,1)S(1)}, bf16[1,64,16,128]{3,2,1,0:T(8,128)(2,1)S(1)}, u32[]{:S(2)}, u32[]{:S(2)}) %collective-permute-start.38) | collective-permute-done | bytes 262176 | tf_op jit(solution)/shard_map/ppermute | solution.py:235
  150.3 2.1 %fock_terms.7 = (f32[64,64]{1,0:T(8,128)S(1)}, f32[64,64]{1,0:T(8,128)S(1)}) custom-call(s32[1]{0:T(128)} %bitcast.5.base, bf16[64,64,512]{2,1,0:T(8,128)(2,1)} %turn.1.slab, bf16[16,128]{1,0:T(8,128)(2,1)S(1)} %broadcast_in_dim.19.diagonal, bf16[1,64,16,128]{3,2,1,0:T(8,128)(2,1)S(1)} %get-tuple-element.150.refs_0_, ...), custom_call_target="tpu_custom_call" | custom-call | tf_op jit(solution)/shard_map/fock_terms/pallas_call | solution.py:176
  153.0 1.2 collective-permute-done.40
  155.4 3.2 %collective-permute-done.41 = f32[32,64]{0,1:T(8,128)S(1)} collective-permute-done((f32[32,64]{0,1:T(8,128)S(1)}, f32[32,64]{0,1:T(8,128)S(1)}, u32[]{:S(2)}, u32[]{:S(2)}) %collective-permute-start.41) | collective-permute-done | bytes 8224 | tf_op jit(solution)/shard_map/ppermute | solution.py:238
  158.6 1.5 collective-permute-start.42
  160.1 3.7 %collective-permute-done.42 = f32[32,64]{0,1:T(8,128)S(1)} collective-permute-done((f32[32,64]{0,1:T(8,128)S(1)}, f32[32,64]{0,1:T(8,128)S(1)}, u32[]{:S(2)}, u32[]{:S(2)}) %collective-permute-start.42) | collective-permute-done | bytes 8224 | tf_op jit(solution)/shard_map/ppermute | solution.py:238
  (105 shorter events, 24.8 us)
Async XLA Ops:
  1.7 7.0 %copy-start.2 = (bf16[8,512,256]{2,1,0:T(8,128)(2,1)S(1)}, bf16[8,512,256]{2,1,0:T(8,128)(2,1)}, u32[]{:S(2)}) copy-start(bf16[8,512,256]{2,1,0:T(8,128)(2,1)} %refs_0_.7) | copy-start | bytes 6291460
  3.7 6.5 %collective-permute-start.1 = (bf16[32,64,512]{2,1,0:T(8,128)(2,1)S(1)}, bf16[32,64,512]{2,1,0:T(8,128)(2,1)S(1)}, u32[]{:S(2)}, u32[]{:S(2)}) collective-permute-start(bf16[32,64,512]{2,1,0:T(8,128)(2,1)S(1)} %constant_dynamic-slice_fusion), channel_id=1, source_target_pairs={{0,1},{1,0},{2,3},{3,2},{4,5},{5,4},{6,7},{7,6},{8,9},{9,8},{10,11... | collective-permute-start | bytes 6291464 | tf_op jit(solution)/shard_map/ppermute | solution.py:235
  4.2 35.2 %collective-permute-start = (bf16[8,512,256]{2,1,0:T(8,128)(2,1)}, bf16[8,512,256]{2,1,0:T(8,128)(2,1)}, u32[]{:S(2)}, u32[]{:S(2)}) collective-permute-start(bf16[8,512,256]{2,1,0:T(8,128)(2,1)} %left.7), channel_id=1, source_target_pairs={{0,1},{1,0},{2,3},{3,2},{4,5},{5,4},{6,7},{7,6},{8,9},{9,8},{10,11... | collective-permute-start | bytes 6291464 | tf_op jit(solution)/shard_map/ppermute | solution.py:235
  4.3 15.1 %collective-permute-start.3 = (bf16[8,128,256]{2,1,0:T(8,128)(2,1)S(1)}, bf16[8,128,256]{2,1,0:T(8,128)(2,1)S(1)}, u32[]{:S(2)}, u32[]{:S(2)}) collective-permute-start(bf16[8,128,256]{2,1,0:T(8,128)(2,1)S(1)} %slice.88), channel_id=1, source_target_pairs={{0,4},{1,5},{2,6},{3,7},{4,0},{5,1},{6,2},{7,3},{8,12},{9,13},{10,... | collective-permute-start | bytes 1572872 | tf_op jit(solution)/shard_map/ppermute | solution.py:235
  7.3 13.6 %collective-permute-start.2 = (bf16[8,128,256]{2,1,0:T(8,128)(2,1)S(1)}, bf16[8,128,256]{2,1,0:T(8,128)(2,1)S(1)}, u32[]{:S(2)}, u32[]{:S(2)}) collective-permute-start(bf16[8,128,256]{2,1,0:T(8,128)(2,1)S(1)} %slice.88), channel_id=1, source_target_pairs={{0,2},{1,3},{2,0},{3,1},{4,6},{5,7},{6,4},{7,5},{8,10},{9,11},{10,... | collective-permute-start | bytes 1572872 | tf_op jit(solution)/shard_map/ppermute | solution.py:235
  10.2 15.5 %copy-start.5 = (s32[8]{0:T(128)S(1)}, s32[8]{0:T(128)}, u32[]{:S(2)}) copy-start(s32[8]{0:T(128)} %param.7) | copy-start | bytes 100
  20.9 25.2 %collective-permute-start.7 = (bf16[8,128,256]{2,1,0:T(8,128)(2,1)}, bf16[8,128,256]{2,1,0:T(8,128)(2,1)S(1)}, u32[]{:S(2)}, u32[]{:S(2)}) collective-permute-start(bf16[8,128,256]{2,1,0:T(8,128)(2,1)} %get-tuple-element.87), channel_id=1, source_target_pairs={{0,4},{1,5},{2,6},{3,7},{4,0},{5,1},{6,2},{7,3},{8,12},{9,13},{10,... | collective-permute-start | bytes 1572872 | tf_op jit(solution)/shard_map/ppermute | solution.py:235
  21.2 9.3 %collective-permute-start.6 = (bf16[8,64,256]{2,1,0:T(8,128)(2,1)S(1)}, bf16[8,64,256]{2,1,0:T(8,128)(2,1)S(1)}, u32[]{:S(2)}, u32[]{:S(2)}) collective-permute-start(bf16[8,64,256]{2,1,0:T(8,128)(2,1)S(1)} %slice.93), channel_id=1, source_target_pairs={{0,2},{1,3},{2,0},{3,1},{4,6},{5,7},{6,4},{7,5},{8,10},{9,11},{10,... | collective-permute-start | bytes 786440 | tf_op jit(solution)/shard_map/ppermute | solution.py:235
  23.7 15.8 %collective-permute-start.5 = (bf16[8,64,256]{2,1,0:T(8,128)(2,1)}, bf16[8,64,256]{2,1,0:T(8,128)(2,1)S(1)}, u32[]{:S(2)}, u32[]{:S(2)}) collective-permute-start(bf16[8,64,256]{2,1,0:T(8,128)(2,1)} %slice.92), channel_id=1, source_target_pairs={{0,4},{1,5},{2,6},{3,7},{4,0},{5,1},{6,2},{7,3},{8,12},{9,13},{10,... | collective-permute-start | bytes 786440 | tf_op jit(solution)/shard_map/ppermute | solution.py:235
  25.2 22.4 %collective-permute-start.4 = (bf16[8,128,256]{2,1,0:T(8,128)(2,1)}, bf16[8,128,256]{2,1,0:T(8,128)(2,1)S(1)}, u32[]{:S(2)}, u32[]{:S(2)}) collective-permute-start(bf16[8,128,256]{2,1,0:T(8,128)(2,1)} %get-tuple-element.87), channel_id=1, source_target_pairs={{0,2},{1,3},{2,0},{3,1},{4,6},{5,7},{6,4},{7,5},{8,10},{9,11},{10,... | collective-permute-start | bytes 1572872 | tf_op jit(solution)/shard_map/ppermute | solution.py:235
  25.8 22.5 %copy-start.3 = (bf16[8,128,256]{2,1,0:T(8,128)(2,1)S(1)}, bf16[8,128,256]{2,1,0:T(8,128)(2,1)}, u32[]{:S(2)}) copy-start(bf16[8,128,256]{2,1,0:T(8,128)(2,1)} %get-tuple-element.95) | copy-start | bytes 1572868
  44.4 12.6 %collective-permute-start.11 = (bf16[2,2,512,128]{3,2,1,0:T(8,128)(2,1)S(1)}, bf16[2,2,512,128]{3,2,1,0:T(8,128)(2,1)S(1)}, u32[]{:S(2)}, u32[]{:S(2)}) collective-permute-start(bf16[2,2,512,128]{3,2,1,0:T(8,128)(2,1)S(1)} %get-tuple-element.98), channel_id=1, source_target_pairs={{0,8},{8,0},{16,24},{24,16},{1,9},{9,1},{17,25},{25,17},{2,10},{10... | collective-permute-start | bytes 1572872 | tf_op jit(solution)/shard_map/ppermute | solution.py:238
  46.1 9.3 %collective-permute-start.10 = (bf16[8,64,256]{2,1,0:T(8,128)(2,1)S(1)}, bf16[8,64,256]{2,1,0:T(8,128)(2,1)S(1)}, u32[]{:S(2)}, u32[]{:S(2)}) collective-permute-start(bf16[8,64,256]{2,1,0:T(8,128)(2,1)S(1)} %slice.95), channel_id=1, source_target_pairs={{0,2},{1,3},{2,0},{3,1},{4,6},{5,7},{6,4},{7,5},{8,10},{9,11},{10,... | collective-permute-start | bytes 786440 | tf_op jit(solution)/shard_map/ppermute | solution.py:235
  47.7 9.3 %collective-permute-start.9 = (bf16[8,64,256]{2,1,0:T(8,128)(2,1)S(1)}, bf16[8,64,256]{2,1,0:T(8,128)(2,1)S(1)}, u32[]{:S(2)}, u32[]{:S(2)}) collective-permute-start(bf16[8,64,256]{2,1,0:T(8,128)(2,1)S(1)} %slice.94), channel_id=1, source_target_pairs={{0,4},{1,5},{2,6},{3,7},{4,0},{5,1},{6,2},{7,3},{8,12},{9,13},{10,... | collective-permute-start | bytes 786440 | tf_op jit(solution)/shard_map/ppermute | solution.py:235
  48.3 16.7 %collective-permute-start.12 = (bf16[8,128,256]{2,1,0:T(8,128)(2,1)S(1)}, bf16[8,128,256]{2,1,0:T(8,128)(2,1)S(1)}, u32[]{:S(2)}, u32[]{:S(2)}) collective-permute-start(bf16[8,128,256]{2,1,0:T(8,128)(2,1)S(1)} %copy-done.3), channel_id=1, source_target_pairs={{0,4},{1,5},{2,6},{3,7},{4,0},{5,1},{6,2},{7,3},{8,12},{9,13},{10,... | collective-permute-start | bytes 1572872 | tf_op jit(solution)/shard_map/ppermute | solution.py:235
  49.8 15.5 %collective-permute-start.8 = (bf16[8,128,256]{2,1,0:T(8,128)(2,1)S(1)}, bf16[8,128,256]{2,1,0:T(8,128)(2,1)S(1)}, u32[]{:S(2)}, u32[]{:S(2)}) collective-permute-start(bf16[8,128,256]{2,1,0:T(8,128)(2,1)S(1)} %copy-done.3), channel_id=1, source_target_pairs={{0,2},{1,3},{2,0},{3,1},{4,6},{5,7},{6,4},{7,5},{8,10},{9,11},{10,... | collective-permute-start | bytes 1572872 | tf_op jit(solution)/shard_map/ppermute | solution.py:235
  62.0 14.9 %collective-permute-start.16 = (bf16[2,2,512,128]{3,2,1,0:T(8,128)(2,1)S(1)}, bf16[2,2,512,128]{3,2,1,0:T(8,128)(2,1)S(1)}, u32[]{:S(2)}, u32[]{:S(2)}) collective-permute-start(bf16[2,2,512,128]{3,2,1,0:T(8,128)(2,1)S(1)} %get-tuple-element.109), channel_id=1, source_target_pairs={{0,8},{8,0},{16,24},{24,16},{1,9},{9,1},{17,25},{25,17},{2,10},{10... | collective-permute-start | bytes 1572872 | tf_op jit(solution)/shard_map/ppermute | solution.py:238
  65.0 9.3 %collective-permute-start.15 = (bf16[8,64,256]{2,1,0:T(8,128)(2,1)S(1)}, bf16[8,64,256]{2,1,0:T(8,128)(2,1)S(1)}, u32[]{:S(2)}, u32[]{:S(2)}) collective-permute-start(bf16[8,64,256]{2,1,0:T(8,128)(2,1)S(1)} %slice.98), channel_id=1, source_target_pairs={{0,2},{1,3},{2,0},{3,1},{4,6},{5,7},{6,4},{7,5},{8,10},{9,11},{10,... | collective-permute-start | bytes 786440 | tf_op jit(solution)/shard_map/ppermute | solution.py:235
  65.3 11.7 %collective-permute-start.14 = (bf16[8,64,256]{2,1,0:T(8,128)(2,1)S(1)}, bf16[8,64,256]{2,1,0:T(8,128)(2,1)S(1)}, u32[]{:S(2)}, u32[]{:S(2)}) collective-permute-start(bf16[8,64,256]{2,1,0:T(8,128)(2,1)S(1)} %slice.97), channel_id=1, source_target_pairs={{0,4},{1,5},{2,6},{3,7},{4,0},{5,1},{6,2},{7,3},{8,12},{9,13},{10,... | collective-permute-start | bytes 786440 | tf_op jit(solution)/shard_map/ppermute | solution.py:235
  66.0 20.1 %collective-permute-start.18 = (bf16[8,128,256]{2,1,0:T(8,128)(2,1)S(1)}, bf16[8,128,256]{2,1,0:T(8,128)(2,1)S(1)}, u32[]{:S(2)}, u32[]{:S(2)}) collective-permute-start(bf16[8,128,256]{2,1,0:T(8,128)(2,1)S(1)} %get-tuple-element.106), channel_id=1, source_target_pairs={{0,4},{1,5},{2,6},{3,7},{4,0},{5,1},{6,2},{7,3},{8,12},{9,13},{10,... | collective-permute-start | bytes 1572872 | tf_op jit(solution)/shard_map/ppermute | solution.py:235
  67.4 19.2 %collective-permute-start.13 = (bf16[8,128,256]{2,1,0:T(8,128)(2,1)S(1)}, bf16[8,128,256]{2,1,0:T(8,128)(2,1)S(1)}, u32[]{:S(2)}, u32[]{:S(2)}) collective-permute-start(bf16[8,128,256]{2,1,0:T(8,128)(2,1)S(1)} %get-tuple-element.106), channel_id=1, source_target_pairs={{0,2},{1,3},{2,0},{3,1},{4,6},{5,7},{6,4},{7,5},{8,10},{9,11},{10,... | collective-permute-start | bytes 1572872 | tf_op jit(solution)/shard_map/ppermute | solution.py:235
  74.4 10.9 %collective-permute-start.17 = (bf16[2,512,128]{2,1,0:T(8,128)(2,1)S(1)}, bf16[2,512,128]{2,1,0:T(8,128)(2,1)S(1)}, u32[]{:S(2)}, u32[]{:S(2)}) collective-permute-start(bf16[2,512,128]{2,1,0:T(8,128)(2,1)S(1)} %fusion.3), channel_id=1, source_target_pairs={{0,16},{8,24},{16,0},{24,8},{1,17},{9,25},{17,1},{25,9},{2,18},{10... | collective-permute-start | bytes 786440 | tf_op jit(solution)/shard_map/ppermute | solution.py:238
  82.0 14.4 %collective-permute-start.21 = (bf16[2,2,512,128]{3,2,1,0:T(8,128)(2,1)S(1)}, bf16[2,2,512,128]{3,2,1,0:T(8,128)(2,1)S(1)}, u32[]{:S(2)}, u32[]{:S(2)}) collective-permute-start(bf16[2,2,512,128]{3,2,1,0:T(8,128)(2,1)S(1)} %get-tuple-element.121), channel_id=1, source_target_pairs={{0,8},{8,0},{16,24},{24,16},{1,9},{9,1},{17,25},{25,17},{2,10},{10... | collective-permute-start | bytes 1572872 | tf_op jit(solution)/shard_map/ppermute | solution.py:238
  86.1 6.9 %collective-permute-start.20 = (bf16[8,64,256]{2,1,0:T(8,128)(2,1)S(1)}, bf16[8,64,256]{2,1,0:T(8,128)(2,1)S(1)}, u32[]{:S(2)}, u32[]{:S(2)}) collective-permute-start(bf16[8,64,256]{2,1,0:T(8,128)(2,1)S(1)} %slice.101), channel_id=1, source_target_pairs={{0,2},{1,3},{2,0},{3,1},{4,6},{5,7},{6,4},{7,5},{8,10},{9,11},{10,... | collective-permute-start | bytes 786440 | tf_op jit(solution)/shard_map/ppermute | solution.py:235
  86.5 8.1 %collective-permute-start.19 = (bf16[8,64,256]{2,1,0:T(8,128)(2,1)S(1)}, bf16[8,64,256]{2,1,0:T(8,128)(2,1)S(1)}, u32[]{:S(2)}, u32[]{:S(2)}) collective-permute-start(bf16[8,64,256]{2,1,0:T(8,128)(2,1)S(1)} %slice.100), channel_id=1, source_target_pairs={{0,4},{1,5},{2,6},{3,7},{4,0},{5,1},{6,2},{7,3},{8,12},{9,13},{10,... | collective-permute-start | bytes 786440 | tf_op jit(solution)/shard_map/ppermute | solution.py:235
  87.2 10.6 %collective-permute-start.22 = (bf16[2,512,128]{2,1,0:T(8,128)(2,1)S(1)}, bf16[2,512,128]{2,1,0:T(8,128)(2,1)S(1)}, u32[]{:S(2)}, u32[]{:S(2)}) collective-permute-start(bf16[2,512,128]{2,1,0:T(8,128)(2,1)S(1)} %fusion.2), channel_id=1, source_target_pairs={{0,16},{8,24},{16,0},{24,8},{1,17},{9,25},{17,1},{25,9},{2,18},{10... | collective-permute-start | bytes 786440 | tf_op jit(solution)/shard_map/ppermute | solution.py:238
  88.9 19.2 %collective-permute-start.23 = (bf16[1,64,16,128]{3,2,1,0:T(8,128)(2,1)S(1)}, bf16[1,64,16,128]{3,2,1,0:T(8,128)(2,1)}, u32[]{:S(2)}, u32[]{:S(2)}) collective-permute-start(bf16[1,64,16,128]{3,2,1,0:T(8,128)(2,1)S(1)} %get-tuple-element.132.refs_0_), channel_id=1, source_target_pairs={{0,2},{1,3},{2,0},{3,1},{4,6},{5,7},{6,4},{7,5},{8,10},{9,11},{10,... | collective-permute-start | bytes 786440 | tf_op jit(solution)/shard_map/ppermute | solution.py:235
  93.0 16.1 %collective-permute-start.24 = (bf16[1,64,16,128]{3,2,1,0:T(8,128)(2,1)S(1)}, bf16[1,64,16,128]{3,2,1,0:T(8,128)(2,1)}, u32[]{:S(2)}, u32[]{:S(2)}) collective-permute-start(bf16[1,64,16,128]{3,2,1,0:T(8,128)(2,1)S(1)} %get-tuple-element.132.refs_0_), channel_id=1, source_target_pairs={{0,4},{1,5},{2,6},{3,7},{4,0},{5,1},{6,2},{7,3},{8,12},{9,13},{10,... | collective-permute-start | bytes 786440 | tf_op jit(solution)/shard_map/ppermute | solution.py:235
  94.6 15.6 %collective-permute-start.25 = (bf16[1,64,16,128]{3,2,1,0:T(8,128)(2,1)S(1)}, bf16[1,64,16,128]{3,2,1,0:T(8,128)(2,1)}, u32[]{:S(2)}, u32[]{:S(2)}) collective-permute-start(bf16[1,64,16,128]{3,2,1,0:T(8,128)(2,1)S(1)} %get-tuple-element.132.refs_0_), channel_id=1, source_target_pairs={{0,6},{1,7},{2,4},{3,5},{4,2},{5,3},{6,0},{7,1},{8,14},{9,15},{10,... | collective-permute-start | bytes 786440 | tf_op jit(solution)/shard_map/ppermute | solution.py:235
  105.1 19.0 %collective-permute-start.30 = (bf16[2,2,512,128]{3,2,1,0:T(8,128)(2,1)}, bf16[2,2,512,128]{3,2,1,0:T(8,128)(2,1)S(1)}, u32[]{:S(2)}, u32[]{:S(2)}) collective-permute-start(bf16[2,2,512,128]{3,2,1,0:T(8,128)(2,1)} %get-tuple-element.141), channel_id=1, source_target_pairs={{0,8},{8,0},{16,24},{24,16},{1,9},{9,1},{17,25},{25,17},{2,10},{10... | collective-permute-start | bytes 1572872 | tf_op jit(solution)/shard_map/ppermute | solution.py:238
  105.7 11.9 %collective-permute-start.26 = (bf16[2,512,128]{2,1,0:T(8,128)(2,1)}, bf16[2,512,128]{2,1,0:T(8,128)(2,1)S(1)}, u32[]{:S(2)}, u32[]{:S(2)}) collective-permute-start(bf16[2,512,128]{2,1,0:T(8,128)(2,1)} %fusion.1), channel_id=1, source_target_pairs={{0,16},{8,24},{16,0},{24,8},{1,17},{9,25},{17,1},{25,9},{2,18},{10... | collective-permute-start | bytes 786440 | tf_op jit(solution)/shard_map/ppermute | solution.py:238
  108.1 10.6 %collective-permute-start.27 = (bf16[1,64,16,128]{3,2,1,0:T(8,128)(2,1)}, bf16[1,64,16,128]{3,2,1,0:T(8,128)(2,1)S(1)}, u32[]{:S(2)}, u32[]{:S(2)}) collective-permute-start(bf16[1,64,16,128]{3,2,1,0:T(8,128)(2,1)} %copy-done), channel_id=1, source_target_pairs={{0,2},{1,3},{2,0},{3,1},{4,6},{5,7},{6,4},{7,5},{8,10},{9,11},{10,... | collective-permute-start | bytes 786440 | tf_op jit(solution)/shard_map/ppermute | solution.py:235
  109.2 10.7 %collective-permute-start.28 = (bf16[1,64,16,128]{3,2,1,0:T(8,128)(2,1)}, bf16[1,64,16,128]{3,2,1,0:T(8,128)(2,1)S(1)}, u32[]{:S(2)}, u32[]{:S(2)}) collective-permute-start(bf16[1,64,16,128]{3,2,1,0:T(8,128)(2,1)} %copy-done), channel_id=1, source_target_pairs={{0,4},{1,5},{2,6},{3,7},{4,0},{5,1},{6,2},{7,3},{8,12},{9,13},{10,... | collective-permute-start | bytes 786440 | tf_op jit(solution)/shard_map/ppermute | solution.py:235
  110.3 11.8 %collective-permute-start.29 = (bf16[1,64,16,128]{3,2,1,0:T(8,128)(2,1)}, bf16[1,64,16,128]{3,2,1,0:T(8,128)(2,1)S(1)}, u32[]{:S(2)}, u32[]{:S(2)}) collective-permute-start(bf16[1,64,16,128]{3,2,1,0:T(8,128)(2,1)} %copy-done), channel_id=1, source_target_pairs={{0,6},{1,7},{2,4},{3,5},{4,2},{5,3},{6,0},{7,1},{8,14},{9,15},{10,... | collective-permute-start | bytes 786440 | tf_op jit(solution)/shard_map/ppermute | solution.py:235
  114.0 8.0 %copy-start.1 = (bf16[1,64,16,128]{3,2,1,0:T(8,128)(2,1)S(1)}, bf16[1,64,16,128]{3,2,1,0:T(8,128)(2,1)}, u32[]{:S(2)}) copy-start(bf16[1,64,16,128]{3,2,1,0:T(8,128)(2,1)} %copy-done) | copy-start | bytes 786436
  118.5 9.1 %collective-permute-start.31 = (bf16[1,64,16,128]{3,2,1,0:T(8,128)(2,1)S(1)}, bf16[1,64,16,128]{3,2,1,0:T(8,128)(2,1)S(1)}, u32[]{:S(2)}, u32[]{:S(2)}) collective-permute-start(bf16[1,64,16,128]{3,2,1,0:T(8,128)(2,1)S(1)} %get-tuple-element.143.refs_0_), channel_id=1, source_target_pairs={{0,2},{1,3},{2,0},{3,1},{4,6},{5,7},{6,4},{7,5},{8,10},{9,11},{10,... | collective-permute-start | bytes 786440 | tf_op jit(solution)/shard_map/ppermute | solution.py:235
  118.7 11.1 %collective-permute-start.32 = (bf16[1,64,16,128]{3,2,1,0:T(8,128)(2,1)S(1)}, bf16[1,64,16,128]{3,2,1,0:T(8,128)(2,1)S(1)}, u32[]{:S(2)}, u32[]{:S(2)}) collective-permute-start(bf16[1,64,16,128]{3,2,1,0:T(8,128)(2,1)S(1)} %get-tuple-element.143.refs_0_), channel_id=1, source_target_pairs={{0,4},{1,5},{2,6},{3,7},{4,0},{5,1},{6,2},{7,3},{8,12},{9,13},{10,... | collective-permute-start | bytes 786440 | tf_op jit(solution)/shard_map/ppermute | solution.py:235
  119.8 10.0 %collective-permute-start.33 = (bf16[1,64,16,128]{3,2,1,0:T(8,128)(2,1)S(1)}, bf16[1,64,16,128]{3,2,1,0:T(8,128)(2,1)S(1)}, u32[]{:S(2)}, u32[]{:S(2)}) collective-permute-start(bf16[1,64,16,128]{3,2,1,0:T(8,128)(2,1)S(1)} %get-tuple-element.143.refs_0_), channel_id=1, source_target_pairs={{0,6},{1,7},{2,4},{3,5},{4,2},{5,3},{6,0},{7,1},{8,14},{9,15},{10,... | collective-permute-start | bytes 786440 | tf_op jit(solution)/shard_map/ppermute | solution.py:235
  124.2 10.5 %collective-permute-start.34 = (bf16[2,512,128]{2,1,0:T(8,128)(2,1)S(1)}, bf16[2,512,128]{2,1,0:T(8,128)(2,1)S(1)}, u32[]{:S(2)}, u32[]{:S(2)}) collective-permute-start(bf16[2,512,128]{2,1,0:T(8,128)(2,1)S(1)} %fusion), channel_id=1, source_target_pairs={{0,16},{8,24},{16,0},{24,8},{1,17},{9,25},{17,1},{25,9},{2,18},{10... | collective-permute-start | bytes 786440 | tf_op jit(solution)/shard_map/ppermute | solution.py:238
  131.9 7.2 %copy-start.4 = (bf16[32,64]{1,0:T(8,128)(2,1)S(1)}, bf16[32,64]{1,0:T(8,128)(2,1)}, u32[]{:S(2)}) copy-start(bf16[32,64]{1,0:T(8,128)(2,1)} %param.9) | copy-start | bytes 12292
  135.5 3.6 %collective-permute-start.35 = (bf16[512,512]{1,0:T(8,128)(2,1)S(1)}, bf16[512,512]{1,0:T(8,128)(2,1)S(1)}, u32[]{:S(2)}, u32[]{:S(2)}) collective-permute-start(bf16[512,512]{1,0:T(8,128)(2,1)S(1)} %get-tuple-element.147), channel_id=1, source_target_pairs={{0,1},{1,0},{2,3},{3,2},{4,5},{5,4},{6,7},{7,6},{8,9},{9,8},{10,11... | collective-permute-start | bytes 1572872 | tf_op jit(solution)/shard_map/ppermute | solution.py:235
  135.6 9.2 %collective-permute-start.36 = (bf16[1,64,16,128]{3,2,1,0:T(8,128)(2,1)S(1)}, bf16[1,64,16,128]{3,2,1,0:T(8,128)(2,1)S(1)}, u32[]{:S(2)}, u32[]{:S(2)}) collective-permute-start(bf16[1,64,16,128]{3,2,1,0:T(8,128)(2,1)S(1)} %get-tuple-element.150.refs_0_), channel_id=1, source_target_pairs={{0,2},{1,3},{2,0},{3,1},{4,6},{5,7},{6,4},{7,5},{8,10},{9,11},{10,... | collective-permute-start | bytes 786440 | tf_op jit(solution)/shard_map/ppermute | solution.py:235
  135.7 9.1 %collective-permute-start.37 = (bf16[1,64,16,128]{3,2,1,0:T(8,128)(2,1)S(1)}, bf16[1,64,16,128]{3,2,1,0:T(8,128)(2,1)S(1)}, u32[]{:S(2)}, u32[]{:S(2)}) collective-permute-start(bf16[1,64,16,128]{3,2,1,0:T(8,128)(2,1)S(1)} %get-tuple-element.150.refs_0_), channel_id=1, source_target_pairs={{0,4},{1,5},{2,6},{3,7},{4,0},{5,1},{6,2},{7,3},{8,12},{9,13},{10,... | collective-permute-start | bytes 786440 | tf_op jit(solution)/shard_map/ppermute | solution.py:235
  136.7 13.6 %collective-permute-start.38 = (bf16[1,64,16,128]{3,2,1,0:T(8,128)(2,1)S(1)}, bf16[1,64,16,128]{3,2,1,0:T(8,128)(2,1)S(1)}, u32[]{:S(2)}, u32[]{:S(2)}) collective-permute-start(bf16[1,64,16,128]{3,2,1,0:T(8,128)(2,1)S(1)} %get-tuple-element.150.refs_0_), channel_id=1, source_target_pairs={{0,6},{1,7},{2,4},{3,5},{4,2},{5,3},{6,0},{7,1},{8,14},{9,15},{10,... | collective-permute-start | bytes 786440 | tf_op jit(solution)/shard_map/ppermute | solution.py:235
  139.2 13.6 %collective-permute-start.39 = (bf16[32,64]{1,0:T(8,128)(2,1)S(1)}, bf16[32,64]{1,0:T(8,128)(2,1)S(1)}, u32[]{:S(2)}, u32[]{:S(2)}) collective-permute-start(bf16[32,64]{1,0:T(8,128)(2,1)S(1)} %copy-done.4), channel_id=1, source_target_pairs={{0,1},{1,0},{2,3},{3,2},{4,5},{5,4},{6,7},{7,6},{8,9},{9,8},{10,11... | collective-permute-start | bytes 12296 | tf_op jit(solution)/shard_map/ppermute | solution.py:235
  153.0 1.2 collective-permute-start.40
  154.7 3.9 %collective-permute-start.41 = (f32[32,64]{0,1:T(8,128)S(1)}, f32[32,64]{0,1:T(8,128)S(1)}, u32[]{:S(2)}, u32[]{:S(2)}) collective-permute-start(f32[32,64]{0,1:T(8,128)S(1)} %fusion.8), channel_id=1, source_target_pairs={{0,8},{8,0},{16,24},{24,16},{1,9},{9,1},{17,25},{25,17},{2,10},{10... | collective-permute-start | bytes 24584 | tf_op jit(solution)/shard_map/ppermute | solution.py:238
  158.6 5.2 %collective-permute-start.42 = (f32[32,64]{0,1:T(8,128)S(1)}, f32[32,64]{0,1:T(8,128)S(1)}, u32[]{:S(2)}, u32[]{:S(2)}) collective-permute-start(f32[32,64]{0,1:T(8,128)S(1)} %add.113), channel_id=1, source_target_pairs={{0,16},{8,24},{16,0},{24,8},{1,17},{9,25},{17,1},{25,9},{2,18},{10... | collective-permute-start | bytes 24584 | tf_op jit(solution)/shard_map/ppermute | solution.py:238
  (1 other events, 0.7 us)
where the time goes:
time: 165 us; the launch traced here: 164 us
  waiting for transfers between devices  67.3 us (41%)
  starting transfers between devices  49.2 us (30%)
  Pallas kernels  38.5 us (23%)
  local copies, waits for them, and re-layouts  7 us (4%)
    ppermute x33, waiting for transfers between devices, across(): return lax.ppermute(value, 'gen', [(i, i ^ flip) for i in range(gens)])  49.9 us
    ppermute x33, starting transfers between devices, across(): return lax.ppermute(value, 'gen', [(i, i ^ flip) for i in range(gens)])  33.3 us
    pallas_call x4, Pallas kernels, partial_products(): pl.pallas_call(functools.partial(partial_kernel, cuts), in_specs=[SMEM] +...  20.6 us
    ppermute x10, waiting for transfers between devices, along(): return lax.ppermute(value, 'sec', [(i, i ^ flip) for i in range(secs)])  17.4 us
    ppermute x10, starting transfers between devices, along(): return lax.ppermute(value, 'sec', [(i, i ^ flip) for i in range(secs)])  15.9 us
    pallas_call x4, Pallas kernels, fock_terms(): pl.pallas_call(functools.partial(fock_kernel, first), in_specs=[SMEM, HBM...  8.62 us
    pallas_call x1, Pallas kernels, turn(): pl.pallas_call(turn_kernel, grid_spec=pltpu.PrefetchScalarGridSpec(num_sc...  5.22 us
  transfers between devices with their start and end apart: 43, of which 22 were waited for; matrix products, arithmetic and copies ran while one was open for 2% of the time, Pallas kernels for 23%

commit v1 on v0

--- a/solution.py
+++ b/solution.py
@@ -73,6 +73,7 @@
             jax.ShapeDtypeStruct(block, jnp.float32),
         ],
         compiler_params=PARAMS,
+        cost_estimate=pl.CostEstimate(flops=2147483648, bytes_accessed=1, transcendentals=0),
         name="partial_products",
     )(info, left, partner, *pieces)
 
@@ -117,6 +118,7 @@
         + [pltpu.VMEM(block, bf16), pltpu.SemaphoreType.DMA((3,))],
         input_output_aliases={4 + i: i for i in range(len(held))},
         compiler_params=PARAMS,
+        cost_estimate=pl.CostEstimate(flops=1048576, bytes_accessed=1, transcendentals=0),
         name="combine",
     )(core, mine, near, far, *held)
 
@@ -187,6 +189,7 @@
             pltpu.SemaphoreType.DMA((5,)),
         ],
         compiler_params=PARAMS,
+        cost_estimate=pl.CostEstimate(flops=83886080, bytes_accessed=1, transcendentals=0),
         name="fock_terms",
     )(base, slab, diagonal, *pieces)
 
@@ -213,6 +216,7 @@
         ),
         out_shape=jax.ShapeDtypeStruct((width, 2 * orbitals, total), jnp.bfloat16),
         compiler_params=PARAMS,
+        cost_estimate=pl.CostEstimate(flops=1048576, bytes_accessed=1, transcendentals=0),
         name="turn",
     )(core, slab, received)
 

time: 165 us -> 161 us (0.976)
  waiting for transfers between devices: 67.3 us -> 59.9 us
  starting transfers between devices: 49.2 us -> 53.3 us
    ppermute x33, waiting for transfers between devices: 49.9 us -> 40.8 us  [across(): return lax.ppermute(value, 'gen', [(i, i ^ flip) for i in range(gens)])]
    ppermute x10, starting transfers between devices: 15.9 us -> 18.3 us  [along(): return lax.ppermute(value, 'sec', [(i, i ^ flip) for i in range(secs)])]
    ppermute x10, waiting for transfers between devices: 17.4 us -> 19.1 us  [along(): return lax.ppermute(value, 'sec', [(i, i ^ flip) for i in range(secs)])]
    ppermute x33, starting transfers between devices: 33.3 us -> 35 us  [across(): return lax.ppermute(value, 'gen', [(i, i ^ flip) for i in range(gens)])]
  transfers between devices with their start and end apart: 43 -> 43, of which waited for: 22 -> 21; matrix products, arithmetic and copies ran while one was open for 2% -> 1% of each run, Pallas kernels for 23% -> 24%
where the time goes in v1:
time: 161 us; the launch traced here: 160 us
  waiting for transfers between devices  59.9 us (37%)
  starting transfers between devices  53.3 us (33%)
  Pallas kernels  38.5 us (24%)
  local copies, waits for them, and re-layouts  6.13 us (4%)
    ppermute x33, waiting for transfers between devices, across(): return lax.ppermute(value, 'gen', [(i, i ^ flip) for i in range(gens)])  40.8 us
    ppermute x33, starting transfers between devices, across(): return lax.ppermute(value, 'gen', [(i, i ^ flip) for i in range(gens)])  35 us
    pallas_call x4, Pallas kernels, partial_products(): pl.pallas_call(functools.partial(partial_kernel, cuts), in_specs=[SMEM] +...  20.6 us
    ppermute x10, waiting for transfers between devices, along(): return lax.ppermute(value, 'sec', [(i, i ^ flip) for i in range(secs)])  19.1 us
    ppermute x10, starting transfers between devices, along(): return lax.ppermute(value, 'sec', [(i, i ^ flip) for i in range(secs)])  18.3 us
    pallas_call x4, Pallas kernels, fock_terms(): pl.pallas_call(functools.partial(fock_kernel, first), in_specs=[SMEM, HBM...  8.61 us
    pallas_call x1, Pallas kernels, turn(): pl.pallas_call(turn_kernel, grid_spec=pltpu.PrefetchScalarGridSpec(num_sc...  5.2 us
    pallas_call x4, Pallas kernels, combine(): pl.pallas_call(functools.partial(combine_kernel, chunk, group.index(chunk...  3.25 us
  transfers between devices with their start and end apart: 43, of which 21 were waited for; matrix products, arithmetic and copies ran while one was open for 1% of the time, Pallas kernels for 24%

profile of v1, /device:TPU:0, one launch (start us, length us, event | category | flops | bytes accessed | tf_op | source)
XLA Modules:
  0.0 160.2 jit_solution(6740276931727613599)
XLA Ops:
  1.8 2.0 %constant_dynamic-slice_fusion = bf16[32,64,512]{2,1,0:T(8,128)(2,1)S(1)} fusion(bf16[32,64,1024]{2,1,0:T(8,128)(2,1)} %a.1, s32[]{:T(128)S(6)} %select_n.79), kind=kLoop, calls=%fused_computation.36 | loop fusion | bytes 4194308 | tf_op jit(solution)/shard_map/dynamic_slice | solution.py:260
  4.3 2.9 %collective-permute-start.3 = (bf16[8,128,256]{2,1,0:T(8,128)(2,1)S(1)}, bf16[8,128,256]{2,1,0:T(8,128)(2,1)S(1)}, u32[]{:S(2)}, u32[]{:S(2)}) collective-permute-start(bf16[8,128,256]{2,1,0:T(8,128)(2,1)S(1)} %slice.88), channel_id=1, source_target_pairs={{0,4},{1,5},{2,6},{3,7},{4,0},{5,1},{6,2},{7,3},{8,12},{9,13},{10,... | collective-permute-start | bytes 1572872 | tf_op jit(solution)/shard_map/ppermute | solution.py:239
  7.3 1.5 collective-permute-start.2
  10.2 5.2 %turn.1.slab = bf16[64,64,512]{2,1,0:T(8,128)(2,1)} custom-call(s32[1]{0:T(128)} %bitcast.core, bf16[32,64,1024]{2,1,0:T(8,128)(2,1)} %a.1, bf16[32,64,512]{2,1,0:T(8,128)(2,1)S(1)} %collective-permute-done.1.b), custom_call_target="tpu_custom_call" | custom-call | flops 1048576 | bytes 1 | tf_op jit(solution)/shard_map/turn/pallas_call | solution.py:206
  15.4 4.0 %collective-permute-done.3.refs_2_ = bf16[8,128,256]{2,1,0:T(8,128)(2,1)S(1)} collective-permute-done((bf16[8,128,256]{2,1,0:T(8,128)(2,1)S(1)}, bf16[8,128,256]{2,1,0:T(8,128)(2,1)S(1)}, u32[]{:S(2)}, u32[]{:S(2)}) %collective-permute-start.3) | collective-permute-done | bytes 524320 | tf_op jit(solution)/shard_map/ppermute | solution.py:239
  19.4 1.8 %collective-permute-start.6 = (bf16[8,64,256]{2,1,0:T(8,128)(2,1)S(1)}, bf16[8,64,256]{2,1,0:T(8,128)(2,1)S(1)}, u32[]{:S(2)}, u32[]{:S(2)}) collective-permute-start(bf16[8,64,256]{2,1,0:T(8,128)(2,1)S(1)} %slice.93), channel_id=1, source_target_pairs={{0,2},{1,3},{2,0},{3,1},{4,6},{5,7},{6,4},{7,5},{8,10},{9,11},{10,... | collective-permute-start | bytes 786440 | tf_op jit(solution)/shard_map/ppermute | solution.py:239
  21.2 1.6 collective-permute-start.5
  23.3 1.1 collective-permute-start.4
  24.6 4.2 %collective-permute-done.6.refs_4_ = bf16[8,64,256]{2,1,0:T(8,128)(2,1)S(1)} collective-permute-done((bf16[8,64,256]{2,1,0:T(8,128)(2,1)S(1)}, bf16[8,64,256]{2,1,0:T(8,128)(2,1)S(1)}, u32[]{:S(2)}, u32[]{:S(2)}) %collective-permute-start.6) | collective-permute-done | bytes 262176 | tf_op jit(solution)/shard_map/ppermute | solution.py:239
  28.7 1.8 %collective-permute-done.5.refs_3_ = bf16[8,64,256]{2,1,0:T(8,128)(2,1)S(1)} collective-permute-done((bf16[8,64,256]{2,1,0:T(8,128)(2,1)S(1)}, bf16[8,64,256]{2,1,0:T(8,128)(2,1)S(1)}, u32[]{:S(2)}, u32[]{:S(2)}) %collective-permute-start.5) | collective-permute-done | bytes 262176 | tf_op jit(solution)/shard_map/ppermute | solution.py:239
  30.6 5.0 %partial_products.4 = (bf16[2,2,512,128]{3,2,1,0:T(8,128)(2,1)S(1)}, f32[2,512,128]{2,1,0:T(8,128)S(1)}, f32[2,512,128]{2,1,0:T(8,128)S(1)}) custom-call(s32[9]{0:T(128)S(1)} %pad_add_fusion.info, bf16[8,512,256]{2,1,0:T(8,128)(2,1)} %left.7, bf16[8,512,256]{2,1,0:T(8,128)(2,1)} %collective-permute-done.partner, bf16[8,512,256]{2,1,0:T(8,128)(2,1)} %refs_0_.7, ...), custom_call_target="tpu_custom_call" | custom-call | flops 2147483648 | bytes 1 | tf_op jit(solution)/shard_map/partial_products/pallas_call | solution.py:60
  35.5 1.6 %collective-permute-start.11 = (bf16[2,2,512,128]{3,2,1,0:T(8,128)(2,1)S(1)}, bf16[2,2,512,128]{3,2,1,0:T(8,128)(2,1)S(1)}, u32[]{:S(2)}, u32[]{:S(2)}) collective-permute-start(bf16[2,2,512,128]{3,2,1,0:T(8,128)(2,1)S(1)} %get-tuple-element.98), channel_id=1, source_target_pairs={{0,8},{8,0},{16,24},{24,16},{1,9},{9,1},{17,25},{25,17},{2,10},{10... | collective-permute-start | bytes 1572872 | tf_op jit(solution)/shard_map/ppermute | solution.py:242
  37.2 2.6 %collective-permute-done.7.refs_2_ = bf16[8,128,256]{2,1,0:T(8,128)(2,1)S(1)} collective-permute-done((bf16[8,128,256]{2,1,0:T(8,128)(2,1)S(1)}, bf16[8,128,256]{2,1,0:T(8,128)(2,1)S(1)}, u32[]{:S(2)}, u32[]{:S(2)}) %collective-permute-start.7) | collective-permute-done | bytes 524320 | tf_op jit(solution)/shard_map/ppermute | solution.py:239
  39.7 1.2 collective-permute-start.10
  44.0 5.1 %collective-permute-done.10.refs_4_ = bf16[8,64,256]{2,1,0:T(8,128)(2,1)S(1)} collective-permute-done((bf16[8,64,256]{2,1,0:T(8,128)(2,1)S(1)}, bf16[8,64,256]{2,1,0:T(8,128)(2,1)S(1)}, u32[]{:S(2)}, u32[]{:S(2)}) %collective-permute-start.10) | collective-permute-done | bytes 262176 | tf_op jit(solution)/shard_map/ppermute | solution.py:239
  49.1 1.2 collective-permute-done.9.refs_3_
  50.3 5.0 %partial_products.5 = (bf16[2,2,512,128]{3,2,1,0:T(8,128)(2,1)S(1)}, f32[2,512,128]{2,1,0:T(8,128)S(1)}, f32[2,512,128]{2,1,0:T(8,128)S(1)}) custom-call(s32[9]{0:T(128)S(1)} %pad_add_fusion.info, bf16[8,512,256]{2,1,0:T(8,128)(2,1)} %left.7, bf16[8,512,256]{2,1,0:T(8,128)(2,1)} %collective-permute-done.partner, bf16[8,512,256]{2,1,0:T(8,128)(2,1)} %refs_0_.7, ...), custom_call_target="tpu_custom_call" | custom-call | flops 2147483648 | bytes 1 | tf_op jit(solution)/shard_map/partial_products/pallas_call | solution.py:60
  55.3 1.6 %collective-permute-start.16 = (bf16[2,2,512,128]{3,2,1,0:T(8,128)(2,1)S(1)}, bf16[2,2,512,128]{3,2,1,0:T(8,128)(2,1)S(1)}, u32[]{:S(2)}, u32[]{:S(2)}) collective-permute-start(bf16[2,2,512,128]{3,2,1,0:T(8,128)(2,1)S(1)} %get-tuple-element.109), channel_id=1, source_target_pairs={{0,8},{8,0},{16,24},{24,16},{1,9},{9,1},{17,25},{25,17},{2,10},{10... | collective-permute-start | bytes 1572872 | tf_op jit(solution)/shard_map/ppermute | solution.py:242
  56.9 1.3 collective-permute-done.12.refs_2_
  59.2 1.7 %collective-permute-start.14 = (bf16[8,64,256]{2,1,0:T(8,128)(2,1)S(1)}, bf16[8,64,256]{2,1,0:T(8,128)(2,1)S(1)}, u32[]{:S(2)}, u32[]{:S(2)}) collective-permute-start(bf16[8,64,256]{2,1,0:T(8,128)(2,1)S(1)} %slice.97), channel_id=1, source_target_pairs={{0,4},{1,5},{2,6},{3,7},{4,0},{5,1},{6,2},{7,3},{8,12},{9,13},{10,... | collective-permute-start | bytes 786440 | tf_op jit(solution)/shard_map/ppermute | solution.py:239
  60.9 2.6 %collective-permute-start.17 = (bf16[2,512,128]{2,1,0:T(8,128)(2,1)S(1)}, bf16[2,512,128]{2,1,0:T(8,128)(2,1)S(1)}, u32[]{:S(2)}, u32[]{:S(2)}) collective-permute-start(bf16[2,512,128]{2,1,0:T(8,128)(2,1)S(1)} %fusion.3), channel_id=1, source_target_pairs={{0,16},{8,24},{16,0},{24,8},{1,17},{9,25},{17,1},{25,9},{2,18},{10... | collective-permute-start | bytes 786440 | tf_op jit(solution)/shard_map/ppermute | solution.py:242
  63.9 2.1 %collective-permute-done.15.refs_4_ = bf16[8,64,256]{2,1,0:T(8,128)(2,1)S(1)} collective-permute-done((bf16[8,64,256]{2,1,0:T(8,128)(2,1)S(1)}, bf16[8,64,256]{2,1,0:T(8,128)(2,1)S(1)}, u32[]{:S(2)}, u32[]{:S(2)}) %collective-permute-start.15) | collective-permute-done | bytes 262176 | tf_op jit(solution)/shard_map/ppermute | solution.py:239
  67.0 1.5 collective-permute-done.14.refs_3_
  68.5 2.6 %collective-permute-done.16.a = bf16[2,2,512,128]{3,2,1,0:T(8,128)(2,1)S(1)} collective-permute-done((bf16[2,2,512,128]{3,2,1,0:T(8,128)(2,1)S(1)}, bf16[2,2,512,128]{3,2,1,0:T(8,128)(2,1)S(1)}, u32[]{:S(2)}, u32[]{:S(2)}) %collective-permute-start.16) | collective-permute-done | bytes 524320 | tf_op jit(solution)/shard_map/ppermute | solution.py:242
  71.2 5.0 %partial_products.6 = (bf16[2,2,512,128]{3,2,1,0:T(8,128)(2,1)S(1)}, f32[2,512,128]{2,1,0:T(8,128)S(1)}, f32[2,512,128]{2,1,0:T(8,128)S(1)}) custom-call(s32[9]{0:T(128)S(1)} %pad_add_fusion.info, bf16[8,512,256]{2,1,0:T(8,128)(2,1)} %left.7, bf16[8,512,256]{2,1,0:T(8,128)(2,1)} %collective-permute-done.partner, bf16[8,512,256]{2,1,0:T(8,128)(2,1)} %refs_0_.7, ...), custom_call_target="tpu_custom_call" | custom-call | flops 2147483648 | bytes 1 | tf_op jit(solution)/shard_map/partial_products/pallas_call | solution.py:60
  78.1 1.9 %collective-permute-start.19 = (bf16[8,64,256]{2,1,0:T(8,128)(2,1)S(1)}, bf16[8,64,256]{2,1,0:T(8,128)(2,1)S(1)}, u32[]{:S(2)}, u32[]{:S(2)}) collective-permute-start(bf16[8,64,256]{2,1,0:T(8,128)(2,1)S(1)} %slice.100), channel_id=1, source_target_pairs={{0,4},{1,5},{2,6},{3,7},{4,0},{5,1},{6,2},{7,3},{8,12},{9,13},{10,... | collective-permute-start | bytes 786440 | tf_op jit(solution)/shard_map/ppermute | solution.py:239
  80.0 3.2 %collective-permute-start.22 = (bf16[2,512,128]{2,1,0:T(8,128)(2,1)S(1)}, bf16[2,512,128]{2,1,0:T(8,128)(2,1)S(1)}, u32[]{:S(2)}, u32[]{:S(2)}) collective-permute-start(bf16[2,512,128]{2,1,0:T(8,128)(2,1)S(1)} %fusion.2), channel_id=1, source_target_pairs={{0,16},{8,24},{16,0},{24,8},{1,17},{9,25},{17,1},{25,9},{2,18},{10... | collective-permute-start | bytes 786440 | tf_op jit(solution)/shard_map/ppermute | solution.py:242
  83.5 2.8 %collective-permute-done.20.refs_4_ = bf16[8,64,256]{2,1,0:T(8,128)(2,1)S(1)} collective-permute-done((bf16[8,64,256]{2,1,0:T(8,128)(2,1)S(1)}, bf16[8,64,256]{2,1,0:T(8,128)(2,1)S(1)}, u32[]{:S(2)}, u32[]{:S(2)}) %collective-permute-start.20) | collective-permute-done | bytes 262176 | tf_op jit(solution)/shard_map/ppermute | solution.py:239
  87.1 2.4 %collective-permute-done.19.refs_3_ = bf16[8,64,256]{2,1,0:T(8,128)(2,1)S(1)} collective-permute-done((bf16[8,64,256]{2,1,0:T(8,128)(2,1)S(1)}, bf16[8,64,256]{2,1,0:T(8,128)(2,1)S(1)}, u32[]{:S(2)}, u32[]{:S(2)}) %collective-permute-start.19) | collective-permute-done | bytes 262176 | tf_op jit(solution)/shard_map/ppermute | solution.py:239
  89.5 2.0 %collective-permute-start.25 = (bf16[1,64,16,128]{3,2,1,0:T(8,128)(2,1)S(1)}, bf16[1,64,16,128]{3,2,1,0:T(8,128)(2,1)}, u32[]{:S(2)}, u32[]{:S(2)}) collective-permute-start(bf16[1,64,16,128]{3,2,1,0:T(8,128)(2,1)S(1)} %get-tuple-element.132.refs_0_), channel_id=1, source_target_pairs={{0,6},{1,7},{2,4},{3,5},{4,2},{5,3},{6,0},{7,1},{8,14},{9,15},{10,... | collective-permute-start | bytes 786440 | tf_op jit(solution)/shard_map/ppermute | solution.py:239
  93.8 5.7 %partial_products.7 = (bf16[2,2,512,128]{3,2,1,0:T(8,128)(2,1)}, f32[2,512,128]{2,1,0:T(8,128)S(1)}, f32[2,512,128]{2,1,0:T(8,128)S(1)}) custom-call(s32[9]{0:T(128)S(1)} %pad_add_fusion.info, bf16[8,512,256]{2,1,0:T(8,128)(2,1)} %left.7, bf16[8,512,256]{2,1,0:T(8,128)(2,1)} %collective-permute-done.partner, bf16[8,512,256]{2,1,0:T(8,128)(2,1)} %refs_0_.7, ...), custom_call_target="tpu_custom_call" | custom-call | flops 2147483648 | bytes 1 | tf_op jit(solution)/shard_map/partial_products/pallas_call | solution.py:60
  99.6 1.9 %collective-permute-start.30 = (bf16[2,2,512,128]{3,2,1,0:T(8,128)(2,1)}, bf16[2,2,512,128]{3,2,1,0:T(8,128)(2,1)S(1)}, u32[]{:S(2)}, u32[]{:S(2)}) collective-permute-start(bf16[2,2,512,128]{3,2,1,0:T(8,128)(2,1)} %get-tuple-element.141), channel_id=1, source_target_pairs={{0,8},{8,0},{16,24},{24,16},{1,9},{9,1},{17,25},{25,17},{2,10},{10... | collective-permute-start | bytes 1572872 | tf_op jit(solution)/shard_map/ppermute | solution.py:242
  101.5 2.3 %collective-permute-start.26 = (bf16[2,512,128]{2,1,0:T(8,128)(2,1)}, bf16[2,512,128]{2,1,0:T(8,128)(2,1)S(1)}, u32[]{:S(2)}, u32[]{:S(2)}) collective-permute-start(bf16[2,512,128]{2,1,0:T(8,128)(2,1)} %fusion.1), channel_id=1, source_target_pairs={{0,16},{8,24},{16,0},{24,8},{1,17},{9,25},{17,1},{25,9},{2,18},{10... | collective-permute-start | bytes 786440 | tf_op jit(solution)/shard_map/ppermute | solution.py:242
  105.6 1.7 %collective-permute-start.29 = (bf16[1,64,16,128]{3,2,1,0:T(8,128)(2,1)}, bf16[1,64,16,128]{3,2,1,0:T(8,128)(2,1)S(1)}, u32[]{:S(2)}, u32[]{:S(2)}) collective-permute-start(bf16[1,64,16,128]{3,2,1,0:T(8,128)(2,1)} %copy-done), channel_id=1, source_target_pairs={{0,6},{1,7},{2,4},{3,5},{4,2},{5,3},{6,0},{7,1},{8,14},{9,15},{10,... | collective-permute-start | bytes 786440 | tf_op jit(solution)/shard_map/ppermute | solution.py:239
  107.3 2.3 %fock_terms.4 = (f32[64,64]{1,0:T(8,128)S(1)}, f32[64,64]{1,0:T(8,128)S(1)}) custom-call(s32[1]{0:T(128)} %bitcast.5.base, bf16[64,64,512]{2,1,0:T(8,128)(2,1)} %turn.1.slab, bf16[16,128]{1,0:T(8,128)(2,1)S(1)} %broadcast_in_dim.18.diagonal, bf16[1,64,16,128]{3,2,1,0:T(8,128)(2,1)S(1)} %get-tuple-element.132.refs_0_, ...), custom_call_target="tpu_custom_call" | custom-call | flops 83886080 | bytes 1 | tf_op jit(solution)/shard_map/fock_terms/pallas_call | solution.py:178
  109.7 4.2 %collective-permute-done.26.b = bf16[2,512,128]{2,1,0:T(8,128)(2,1)S(1)} collective-permute-done((bf16[2,512,128]{2,1,0:T(8,128)(2,1)}, bf16[2,512,128]{2,1,0:T(8,128)(2,1)S(1)}, u32[]{:S(2)}, u32[]{:S(2)}) %collective-permute-start.26) | collective-permute-done | bytes 262176 | tf_op jit(solution)/shard_map/ppermute | solution.py:242
  115.3 2.9 %collective-permute-start.33 = (bf16[1,64,16,128]{3,2,1,0:T(8,128)(2,1)S(1)}, bf16[1,64,16,128]{3,2,1,0:T(8,128)(2,1)S(1)}, u32[]{:S(2)}, u32[]{:S(2)}) collective-permute-start(bf16[1,64,16,128]{3,2,1,0:T(8,128)(2,1)S(1)} %get-tuple-element.143.refs_0_), channel_id=1, source_target_pairs={{0,6},{1,7},{2,4},{3,5},{4,2},{5,3},{6,0},{7,1},{8,14},{9,15},{10,... | collective-permute-start | bytes 786440 | tf_op jit(solution)/shard_map/ppermute | solution.py:239
  118.3 2.1 %fock_terms.5 = (f32[64,64]{1,0:T(8,128)S(1)}, f32[64,64]{1,0:T(8,128)S(1)}) custom-call(s32[1]{0:T(128)} %bitcast.5.base, bf16[64,64,512]{2,1,0:T(8,128)(2,1)} %turn.1.slab, bf16[16,128]{1,0:T(8,128)(2,1)S(1)} %broadcast_in_dim.17.diagonal, bf16[1,64,16,128]{3,2,1,0:T(8,128)(2,1)S(1)} %copy-done.1, ...), custom_call_target="tpu_custom_call" | custom-call | flops 83886080 | bytes 1 | tf_op jit(solution)/shard_map/fock_terms/pallas_call | solution.py:178
  120.4 3.4 %collective-permute-start.34 = (bf16[2,512,128]{2,1,0:T(8,128)(2,1)S(1)}, bf16[2,512,128]{2,1,0:T(8,128)(2,1)S(1)}, u32[]{:S(2)}, u32[]{:S(2)}) collective-permute-start(bf16[2,512,128]{2,1,0:T(8,128)(2,1)S(1)} %fusion), channel_id=1, source_target_pairs={{0,16},{8,24},{16,0},{24,8},{1,17},{9,25},{17,1},{25,9},{2,18},{10... | collective-permute-start | bytes 786440 | tf_op jit(solution)/shard_map/ppermute | solution.py:242
  124.0 2.1 %fock_terms.6 = (f32[64,64]{1,0:T(8,128)S(1)}, f32[64,64]{1,0:T(8,128)S(1)}) custom-call(s32[1]{0:T(128)} %bitcast.5.base, bf16[64,64,512]{2,1,0:T(8,128)(2,1)} %turn.1.slab, bf16[16,128]{1,0:T(8,128)(2,1)S(1)} %broadcast_in_dim.16.diagonal, bf16[1,64,16,128]{3,2,1,0:T(8,128)(2,1)S(1)} %get-tuple-element.143.refs_0_, ...), custom_call_target="tpu_custom_call" | custom-call | flops 83886080 | bytes 1 | tf_op jit(solution)/shard_map/fock_terms/pallas_call | solution.py:178
  126.2 4.9 %collective-permute-done.34.b = bf16[2,512,128]{2,1,0:T(8,128)(2,1)S(1)} collective-permute-done((bf16[2,512,128]{2,1,0:T(8,128)(2,1)S(1)}, bf16[2,512,128]{2,1,0:T(8,128)(2,1)S(1)}, u32[]{:S(2)}, u32[]{:S(2)}) %collective-permute-start.34) | collective-permute-done | bytes 262176 | tf_op jit(solution)/shard_map/ppermute | solution.py:242
  132.1 3.3 %collective-permute-start.38 = (bf16[1,64,16,128]{3,2,1,0:T(8,128)(2,1)S(1)}, bf16[1,64,16,128]{3,2,1,0:T(8,128)(2,1)S(1)}, u32[]{:S(2)}, u32[]{:S(2)}) collective-permute-start(bf16[1,64,16,128]{3,2,1,0:T(8,128)(2,1)S(1)} %get-tuple-element.150.refs_0_), channel_id=1, source_target_pairs={{0,6},{1,7},{2,4},{3,5},{4,2},{5,3},{6,0},{7,1},{8,14},{9,15},{10,... | collective-permute-start | bytes 786440 | tf_op jit(solution)/shard_map/ppermute | solution.py:239
  136.3 4.8 %collective-permute-done.36.refs_1_ = bf16[1,64,16,128]{3,2,1,0:T(8,128)(2,1)S(1)} collective-permute-done((bf16[1,64,16,128]{3,2,1,0:T(8,128)(2,1)S(1)}, bf16[1,64,16,128]{3,2,1,0:T(8,128)(2,1)S(1)}, u32[]{:S(2)}, u32[]{:S(2)}) %collective-permute-start.36) | collective-permute-done | bytes 262176 | tf_op jit(solution)/shard_map/ppermute | solution.py:239
  141.1 5.2 %collective-permute-done.37.refs_2_ = bf16[1,64,16,128]{3,2,1,0:T(8,128)(2,1)S(1)} collective-permute-done((bf16[1,64,16,128]{3,2,1,0:T(8,128)(2,1)S(1)}, bf16[1,64,16,128]{3,2,1,0:T(8,128)(2,1)S(1)}, u32[]{:S(2)}, u32[]{:S(2)}) %collective-permute-start.37) | collective-permute-done | bytes 262176 | tf_op jit(solution)/shard_map/ppermute | solution.py:239
  146.2 2.1 %fock_terms.7 = (f32[64,64]{1,0:T(8,128)S(1)}, f32[64,64]{1,0:T(8,128)S(1)}) custom-call(s32[1]{0:T(128)} %bitcast.5.base, bf16[64,64,512]{2,1,0:T(8,128)(2,1)} %turn.1.slab, bf16[16,128]{1,0:T(8,128)(2,1)S(1)} %broadcast_in_dim.19.diagonal, bf16[1,64,16,128]{3,2,1,0:T(8,128)(2,1)S(1)} %get-tuple-element.150.refs_0_, ...), custom_call_target="tpu_custom_call" | custom-call | flops 83886080 | bytes 1 | tf_op jit(solution)/shard_map/fock_terms/pallas_call | solution.py:178
  148.9 1.2 collective-permute-done.40
  151.0 3.5 %collective-permute-done.41 = f32[32,64]{0,1:T(8,128)S(1)} collective-permute-done((f32[32,64]{0,1:T(8,128)S(1)}, f32[32,64]{0,1:T(8,128)S(1)}, u32[]{:S(2)}, u32[]{:S(2)}) %collective-permute-start.41) | collective-permute-done | bytes 8224 | tf_op jit(solution)/shard_map/ppermute | solution.py:242
  155.6 3.9 %collective-permute-done.42 = f32[32,64]{0,1:T(8,128)S(1)} collective-permute-done((f32[32,64]{0,1:T(8,128)S(1)}, f32[32,64]{0,1:T(8,128)S(1)}, u32[]{:S(2)}, u32[]{:S(2)}) %collective-permute-start.42) | collective-permute-done | bytes 8224 | tf_op jit(solution)/shard_map/ppermute | solution.py:242
  (103 shorter events, 23.5 us)
Async XLA Ops:
  1.7 7.0 %copy-start.2 = (bf16[8,512,256]{2,1,0:T(8,128)(2,1)S(1)}, bf16[8,512,256]{2,1,0:T(8,128)(2,1)}, u32[]{:S(2)}) copy-start(bf16[8,512,256]{2,1,0:T(8,128)(2,1)} %refs_0_.7) | copy-start | bytes 6291460
  3.7 6.5 %collective-permute-start.1 = (bf16[32,64,512]{2,1,0:T(8,128)(2,1)S(1)}, bf16[32,64,512]{2,1,0:T(8,128)(2,1)S(1)}, u32[]{:S(2)}, u32[]{:S(2)}) collective-permute-start(bf16[32,64,512]{2,1,0:T(8,128)(2,1)S(1)} %constant_dynamic-slice_fusion), channel_id=1, source_target_pairs={{0,1},{1,0},{2,3},{3,2},{4,5},{5,4},{6,7},{7,6},{8,9},{9,8},{10,11... | collective-permute-start | bytes 6291464 | tf_op jit(solution)/shard_map/ppermute | solution.py:239
  4.2 26.3 %collective-permute-start = (bf16[8,512,256]{2,1,0:T(8,128)(2,1)}, bf16[8,512,256]{2,1,0:T(8,128)(2,1)}, u32[]{:S(2)}, u32[]{:S(2)}) collective-permute-start(bf16[8,512,256]{2,1,0:T(8,128)(2,1)} %left.7), channel_id=1, source_target_pairs={{0,1},{1,0},{2,3},{3,2},{4,5},{5,4},{6,7},{7,6},{8,9},{9,8},{10,11... | collective-permute-start | bytes 6291464 | tf_op jit(solution)/shard_map/ppermute | solution.py:239
  4.3 15.1 %collective-permute-start.3 = (bf16[8,128,256]{2,1,0:T(8,128)(2,1)S(1)}, bf16[8,128,256]{2,1,0:T(8,128)(2,1)S(1)}, u32[]{:S(2)}, u32[]{:S(2)}) collective-permute-start(bf16[8,128,256]{2,1,0:T(8,128)(2,1)S(1)} %slice.88), channel_id=1, source_target_pairs={{0,4},{1,5},{2,6},{3,7},{4,0},{5,1},{6,2},{7,3},{8,12},{9,13},{10,... | collective-permute-start | bytes 1572872 | tf_op jit(solution)/shard_map/ppermute | solution.py:239
  7.3 14.0 %collective-permute-start.2 = (bf16[8,128,256]{2,1,0:T(8,128)(2,1)S(1)}, bf16[8,128,256]{2,1,0:T(8,128)(2,1)S(1)}, u32[]{:S(2)}, u32[]{:S(2)}) collective-permute-start(bf16[8,128,256]{2,1,0:T(8,128)(2,1)S(1)} %slice.88), channel_id=1, source_target_pairs={{0,2},{1,3},{2,0},{3,1},{4,6},{5,7},{6,4},{7,5},{8,10},{9,11},{10,... | collective-permute-start | bytes 1572872 | tf_op jit(solution)/shard_map/ppermute | solution.py:239
  10.2 14.3 %copy-start.4 = (s32[8]{0:T(128)S(1)}, s32[8]{0:T(128)}, u32[]{:S(2)}) copy-start(s32[8]{0:T(128)} %param.7) | copy-start | bytes 100
  19.4 9.3 %collective-permute-start.6 = (bf16[8,64,256]{2,1,0:T(8,128)(2,1)S(1)}, bf16[8,64,256]{2,1,0:T(8,128)(2,1)S(1)}, u32[]{:S(2)}, u32[]{:S(2)}) collective-permute-start(bf16[8,64,256]{2,1,0:T(8,128)(2,1)S(1)} %slice.93), channel_id=1, source_target_pairs={{0,2},{1,3},{2,0},{3,1},{4,6},{5,7},{6,4},{7,5},{8,10},{9,11},{10,... | collective-permute-start | bytes 786440 | tf_op jit(solution)/shard_map/ppermute | solution.py:239
  21.2 9.3 %collective-permute-start.5 = (bf16[8,64,256]{2,1,0:T(8,128)(2,1)S(1)}, bf16[8,64,256]{2,1,0:T(8,128)(2,1)S(1)}, u32[]{:S(2)}, u32[]{:S(2)}) collective-permute-start(bf16[8,64,256]{2,1,0:T(8,128)(2,1)S(1)} %slice.92), channel_id=1, source_target_pairs={{0,4},{1,5},{2,6},{3,7},{4,0},{5,1},{6,2},{7,3},{8,12},{9,13},{10,... | collective-permute-start | bytes 786440 | tf_op jit(solution)/shard_map/ppermute | solution.py:239
  22.8 16.9 %collective-permute-start.7 = (bf16[8,128,256]{2,1,0:T(8,128)(2,1)S(1)}, bf16[8,128,256]{2,1,0:T(8,128)(2,1)S(1)}, u32[]{:S(2)}, u32[]{:S(2)}) collective-permute-start(bf16[8,128,256]{2,1,0:T(8,128)(2,1)S(1)} %get-tuple-element.87), channel_id=1, source_target_pairs={{0,4},{1,5},{2,6},{3,7},{4,0},{5,1},{6,2},{7,3},{8,12},{9,13},{10,... | collective-permute-start | bytes 1572872 | tf_op jit(solution)/shard_map/ppermute | solution.py:239
  23.3 17.6 %collective-permute-start.4 = (bf16[8,128,256]{2,1,0:T(8,128)(2,1)S(1)}, bf16[8,128,256]{2,1,0:T(8,128)(2,1)S(1)}, u32[]{:S(2)}, u32[]{:S(2)}) collective-permute-start(bf16[8,128,256]{2,1,0:T(8,128)(2,1)S(1)} %get-tuple-element.87), channel_id=1, source_target_pairs={{0,2},{1,3},{2,0},{3,1},{4,6},{5,7},{6,4},{7,5},{8,10},{9,11},{10,... | collective-permute-start | bytes 1572872 | tf_op jit(solution)/shard_map/ppermute | solution.py:239
  35.5 14.7 %collective-permute-start.11 = (bf16[2,2,512,128]{3,2,1,0:T(8,128)(2,1)S(1)}, bf16[2,2,512,128]{3,2,1,0:T(8,128)(2,1)S(1)}, u32[]{:S(2)}, u32[]{:S(2)}) collective-permute-start(bf16[2,2,512,128]{3,2,1,0:T(8,128)(2,1)S(1)} %get-tuple-element.98), channel_id=1, source_target_pairs={{0,8},{8,0},{16,24},{24,16},{1,9},{9,1},{17,25},{25,17},{2,10},{10... | collective-permute-start | bytes 1572872 | tf_op jit(solution)/shard_map/ppermute | solution.py:242
  39.7 9.3 %collective-permute-start.10 = (bf16[8,64,256]{2,1,0:T(8,128)(2,1)S(1)}, bf16[8,64,256]{2,1,0:T(8,128)(2,1)S(1)}, u32[]{:S(2)}, u32[]{:S(2)}) collective-permute-start(bf16[8,64,256]{2,1,0:T(8,128)(2,1)S(1)} %slice.95), channel_id=1, source_target_pairs={{0,2},{1,3},{2,0},{3,1},{4,6},{5,7},{6,4},{7,5},{8,10},{9,11},{10,... | collective-permute-start | bytes 786440 | tf_op jit(solution)/shard_map/ppermute | solution.py:239
  40.9 9.3 %collective-permute-start.9 = (bf16[8,64,256]{2,1,0:T(8,128)(2,1)S(1)}, bf16[8,64,256]{2,1,0:T(8,128)(2,1)S(1)}, u32[]{:S(2)}, u32[]{:S(2)}) collective-permute-start(bf16[8,64,256]{2,1,0:T(8,128)(2,1)S(1)} %slice.94), channel_id=1, source_target_pairs={{0,4},{1,5},{2,6},{3,7},{4,0},{5,1},{6,2},{7,3},{8,12},{9,13},{10,... | collective-permute-start | bytes 786440 | tf_op jit(solution)/shard_map/ppermute | solution.py:239
  41.9 16.2 %collective-permute-start.12 = (bf16[8,128,256]{2,1,0:T(8,128)(2,1)}, bf16[8,128,256]{2,1,0:T(8,128)(2,1)S(1)}, u32[]{:S(2)}, u32[]{:S(2)}) collective-permute-start(bf16[8,128,256]{2,1,0:T(8,128)(2,1)} %get-tuple-element.95), channel_id=1, source_target_pairs={{0,4},{1,5},{2,6},{3,7},{4,0},{5,1},{6,2},{7,3},{8,12},{9,13},{10,... | collective-permute-start | bytes 1572872 | tf_op jit(solution)/shard_map/ppermute | solution.py:239
  43.0 16.2 %collective-permute-start.8 = (bf16[8,128,256]{2,1,0:T(8,128)(2,1)}, bf16[8,128,256]{2,1,0:T(8,128)(2,1)S(1)}, u32[]{:S(2)}, u32[]{:S(2)}) collective-permute-start(bf16[8,128,256]{2,1,0:T(8,128)(2,1)} %get-tuple-element.95), channel_id=1, source_target_pairs={{0,2},{1,3},{2,0},{3,1},{4,6},{5,7},{6,4},{7,5},{8,10},{9,11},{10,... | collective-permute-start | bytes 1572872 | tf_op jit(solution)/shard_map/ppermute | solution.py:239
  55.3 15.8 %collective-permute-start.16 = (bf16[2,2,512,128]{3,2,1,0:T(8,128)(2,1)S(1)}, bf16[2,2,512,128]{3,2,1,0:T(8,128)(2,1)S(1)}, u32[]{:S(2)}, u32[]{:S(2)}) collective-permute-start(bf16[2,2,512,128]{3,2,1,0:T(8,128)(2,1)S(1)} %get-tuple-element.109), channel_id=1, source_target_pairs={{0,8},{8,0},{16,24},{24,16},{1,9},{9,1},{17,25},{25,17},{2,10},{10... | collective-permute-start | bytes 1572872 | tf_op jit(solution)/shard_map/ppermute | solution.py:242
  58.2 7.9 %collective-permute-start.15 = (bf16[8,64,256]{2,1,0:T(8,128)(2,1)S(1)}, bf16[8,64,256]{2,1,0:T(8,128)(2,1)S(1)}, u32[]{:S(2)}, u32[]{:S(2)}) collective-permute-start(bf16[8,64,256]{2,1,0:T(8,128)(2,1)S(1)} %slice.98), channel_id=1, source_target_pairs={{0,2},{1,3},{2,0},{3,1},{4,6},{5,7},{6,4},{7,5},{8,10},{9,11},{10,... | collective-permute-start | bytes 786440 | tf_op jit(solution)/shard_map/ppermute | solution.py:239
  59.2 9.2 %collective-permute-start.14 = (bf16[8,64,256]{2,1,0:T(8,128)(2,1)S(1)}, bf16[8,64,256]{2,1,0:T(8,128)(2,1)S(1)}, u32[]{:S(2)}, u32[]{:S(2)}) collective-permute-start(bf16[8,64,256]{2,1,0:T(8,128)(2,1)S(1)} %slice.97), channel_id=1, source_target_pairs={{0,4},{1,5},{2,6},{3,7},{4,0},{5,1},{6,2},{7,3},{8,12},{9,13},{10,... | collective-permute-start | bytes 786440 | tf_op jit(solution)/shard_map/ppermute | solution.py:239
  60.9 15.3 %collective-permute-start.17 = (bf16[2,512,128]{2,1,0:T(8,128)(2,1)S(1)}, bf16[2,512,128]{2,1,0:T(8,128)(2,1)S(1)}, u32[]{:S(2)}, u32[]{:S(2)}) collective-permute-start(bf16[2,512,128]{2,1,0:T(8,128)(2,1)S(1)} %fusion.3), channel_id=1, source_target_pairs={{0,16},{8,24},{16,0},{24,8},{1,17},{9,25},{17,1},{25,9},{2,18},{10... | collective-permute-start | bytes 786440 | tf_op jit(solution)/shard_map/ppermute | solution.py:242
  63.5 13.6 %collective-permute-start.18 = (bf16[8,128,256]{2,1,0:T(8,128)(2,1)S(1)}, bf16[8,128,256]{2,1,0:T(8,128)(2,1)S(1)}, u32[]{:S(2)}, u32[]{:S(2)}) collective-permute-start(bf16[8,128,256]{2,1,0:T(8,128)(2,1)S(1)} %get-tuple-element.106), channel_id=1, source_target_pairs={{0,4},{1,5},{2,6},{3,7},{4,0},{5,1},{6,2},{7,3},{8,12},{9,13},{10,... | collective-permute-start | bytes 1572872 | tf_op jit(solution)/shard_map/ppermute | solution.py:239
  66.0 12.0 %collective-permute-start.13 = (bf16[8,128,256]{2,1,0:T(8,128)(2,1)S(1)}, bf16[8,128,256]{2,1,0:T(8,128)(2,1)S(1)}, u32[]{:S(2)}, u32[]{:S(2)}) collective-permute-start(bf16[8,128,256]{2,1,0:T(8,128)(2,1)S(1)} %get-tuple-element.106), channel_id=1, source_target_pairs={{0,2},{1,3},{2,0},{3,1},{4,6},{5,7},{6,4},{7,5},{8,10},{9,11},{10,... | collective-permute-start | bytes 1572872 | tf_op jit(solution)/shard_map/ppermute | solution.py:239
  76.1 15.4 %collective-permute-start.21 = (bf16[2,2,512,128]{3,2,1,0:T(8,128)(2,1)S(1)}, bf16[2,2,512,128]{3,2,1,0:T(8,128)(2,1)S(1)}, u32[]{:S(2)}, u32[]{:S(2)}) collective-permute-start(bf16[2,2,512,128]{3,2,1,0:T(8,128)(2,1)S(1)} %get-tuple-element.121), channel_id=1, source_target_pairs={{0,8},{8,0},{16,24},{24,16},{1,9},{9,1},{17,25},{25,17},{2,10},{10... | collective-permute-start | bytes 1572872 | tf_op jit(solution)/shard_map/ppermute | solution.py:242
  77.1 9.1 %collective-permute-start.20 = (bf16[8,64,256]{2,1,0:T(8,128)(2,1)S(1)}, bf16[8,64,256]{2,1,0:T(8,128)(2,1)S(1)}, u32[]{:S(2)}, u32[]{:S(2)}) collective-permute-start(bf16[8,64,256]{2,1,0:T(8,128)(2,1)S(1)} %slice.101), channel_id=1, source_target_pairs={{0,2},{1,3},{2,0},{3,1},{4,6},{5,7},{6,4},{7,5},{8,10},{9,11},{10,... | collective-permute-start | bytes 786440 | tf_op jit(solution)/shard_map/ppermute | solution.py:239
  78.1 11.4 %collective-permute-start.19 = (bf16[8,64,256]{2,1,0:T(8,128)(2,1)S(1)}, bf16[8,64,256]{2,1,0:T(8,128)(2,1)S(1)}, u32[]{:S(2)}, u32[]{:S(2)}) collective-permute-start(bf16[8,64,256]{2,1,0:T(8,128)(2,1)S(1)} %slice.100), channel_id=1, source_target_pairs={{0,4},{1,5},{2,6},{3,7},{4,0},{5,1},{6,2},{7,3},{8,12},{9,13},{10,... | collective-permute-start | bytes 786440 | tf_op jit(solution)/shard_map/ppermute | solution.py:239
  80.0 12.3 %collective-permute-start.22 = (bf16[2,512,128]{2,1,0:T(8,128)(2,1)S(1)}, bf16[2,512,128]{2,1,0:T(8,128)(2,1)S(1)}, u32[]{:S(2)}, u32[]{:S(2)}) collective-permute-start(bf16[2,512,128]{2,1,0:T(8,128)(2,1)S(1)} %fusion.2), channel_id=1, source_target_pairs={{0,16},{8,24},{16,0},{24,8},{1,17},{9,25},{17,1},{25,9},{2,18},{10... | collective-permute-start | bytes 786440 | tf_op jit(solution)/shard_map/ppermute | solution.py:242
  83.1 20.6 %collective-permute-start.23 = (bf16[1,64,16,128]{3,2,1,0:T(8,128)(2,1)S(1)}, bf16[1,64,16,128]{3,2,1,0:T(8,128)(2,1)}, u32[]{:S(2)}, u32[]{:S(2)}) collective-permute-start(bf16[1,64,16,128]{3,2,1,0:T(8,128)(2,1)S(1)} %get-tuple-element.132.refs_0_), channel_id=1, source_target_pairs={{0,2},{1,3},{2,0},{3,1},{4,6},{5,7},{6,4},{7,5},{8,10},{9,11},{10,... | collective-permute-start | bytes 786440 | tf_op jit(solution)/shard_map/ppermute | solution.py:239
  86.2 18.3 %collective-permute-start.24 = (bf16[1,64,16,128]{3,2,1,0:T(8,128)(2,1)S(1)}, bf16[1,64,16,128]{3,2,1,0:T(8,128)(2,1)}, u32[]{:S(2)}, u32[]{:S(2)}) collective-permute-start(bf16[1,64,16,128]{3,2,1,0:T(8,128)(2,1)S(1)} %get-tuple-element.132.refs_0_), channel_id=1, source_target_pairs={{0,4},{1,5},{2,6},{3,7},{4,0},{5,1},{6,2},{7,3},{8,12},{9,13},{10,... | collective-permute-start | bytes 786440 | tf_op jit(solution)/shard_map/ppermute | solution.py:239
  89.5 16.1 %collective-permute-start.25 = (bf16[1,64,16,128]{3,2,1,0:T(8,128)(2,1)S(1)}, bf16[1,64,16,128]{3,2,1,0:T(8,128)(2,1)}, u32[]{:S(2)}, u32[]{:S(2)}) collective-permute-start(bf16[1,64,16,128]{3,2,1,0:T(8,128)(2,1)S(1)} %get-tuple-element.132.refs_0_), channel_id=1, source_target_pairs={{0,6},{1,7},{2,4},{3,5},{4,2},{5,3},{6,0},{7,1},{8,14},{9,15},{10,... | collective-permute-start | bytes 786440 | tf_op jit(solution)/shard_map/ppermute | solution.py:239
  93.1 0.7 copy-start
  99.6 20.8 %collective-permute-start.30 = (bf16[2,2,512,128]{3,2,1,0:T(8,128)(2,1)}, bf16[2,2,512,128]{3,2,1,0:T(8,128)(2,1)S(1)}, u32[]{:S(2)}, u32[]{:S(2)}) collective-permute-start(bf16[2,2,512,128]{3,2,1,0:T(8,128)(2,1)} %get-tuple-element.141), channel_id=1, source_target_pairs={{0,8},{8,0},{16,24},{24,16},{1,9},{9,1},{17,25},{25,17},{2,10},{10... | collective-permute-start | bytes 1572872 | tf_op jit(solution)/shard_map/ppermute | solution.py:242
  101.5 12.4 %collective-permute-start.26 = (bf16[2,512,128]{2,1,0:T(8,128)(2,1)}, bf16[2,512,128]{2,1,0:T(8,128)(2,1)S(1)}, u32[]{:S(2)}, u32[]{:S(2)}) collective-permute-start(bf16[2,512,128]{2,1,0:T(8,128)(2,1)} %fusion.1), channel_id=1, source_target_pairs={{0,16},{8,24},{16,0},{24,8},{1,17},{9,25},{17,1},{25,9},{2,18},{10... | collective-permute-start | bytes 786440 | tf_op jit(solution)/shard_map/ppermute | solution.py:242
  103.8 11.0 %collective-permute-start.27 = (bf16[1,64,16,128]{3,2,1,0:T(8,128)(2,1)}, bf16[1,64,16,128]{3,2,1,0:T(8,128)(2,1)S(1)}, u32[]{:S(2)}, u32[]{:S(2)}) collective-permute-start(bf16[1,64,16,128]{3,2,1,0:T(8,128)(2,1)} %copy-done), channel_id=1, source_target_pairs={{0,2},{1,3},{2,0},{3,1},{4,6},{5,7},{6,4},{7,5},{8,10},{9,11},{10,... | collective-permute-start | bytes 786440 | tf_op jit(solution)/shard_map/ppermute | solution.py:239
  104.6 10.8 %collective-permute-start.28 = (bf16[1,64,16,128]{3,2,1,0:T(8,128)(2,1)}, bf16[1,64,16,128]{3,2,1,0:T(8,128)(2,1)S(1)}, u32[]{:S(2)}, u32[]{:S(2)}) collective-permute-start(bf16[1,64,16,128]{3,2,1,0:T(8,128)(2,1)} %copy-done), channel_id=1, source_target_pairs={{0,4},{1,5},{2,6},{3,7},{4,0},{5,1},{6,2},{7,3},{8,12},{9,13},{10,... | collective-permute-start | bytes 786440 | tf_op jit(solution)/shard_map/ppermute | solution.py:239
  105.6 12.7 %collective-permute-start.29 = (bf16[1,64,16,128]{3,2,1,0:T(8,128)(2,1)}, bf16[1,64,16,128]{3,2,1,0:T(8,128)(2,1)S(1)}, u32[]{:S(2)}, u32[]{:S(2)}) collective-permute-start(bf16[1,64,16,128]{3,2,1,0:T(8,128)(2,1)} %copy-done), channel_id=1, source_target_pairs={{0,6},{1,7},{2,4},{3,5},{4,2},{5,3},{6,0},{7,1},{8,14},{9,15},{10,... | collective-permute-start | bytes 786440 | tf_op jit(solution)/shard_map/ppermute | solution.py:239
  109.7 8.6 %copy-start.1 = (bf16[1,64,16,128]{3,2,1,0:T(8,128)(2,1)S(1)}, bf16[1,64,16,128]{3,2,1,0:T(8,128)(2,1)}, u32[]{:S(2)}) copy-start(bf16[1,64,16,128]{3,2,1,0:T(8,128)(2,1)} %copy-done) | copy-start | bytes 786436
  114.7 9.2 %collective-permute-start.31 = (bf16[1,64,16,128]{3,2,1,0:T(8,128)(2,1)S(1)}, bf16[1,64,16,128]{3,2,1,0:T(8,128)(2,1)S(1)}, u32[]{:S(2)}, u32[]{:S(2)}) collective-permute-start(bf16[1,64,16,128]{3,2,1,0:T(8,128)(2,1)S(1)} %get-tuple-element.143.refs_0_), channel_id=1, source_target_pairs={{0,2},{1,3},{2,0},{3,1},{4,6},{5,7},{6,4},{7,5},{8,10},{9,11},{10,... | collective-permute-start | bytes 786440 | tf_op jit(solution)/shard_map/ppermute | solution.py:239
  114.8 9.2 %collective-permute-start.32 = (bf16[1,64,16,128]{3,2,1,0:T(8,128)(2,1)S(1)}, bf16[1,64,16,128]{3,2,1,0:T(8,128)(2,1)S(1)}, u32[]{:S(2)}, u32[]{:S(2)}) collective-permute-start(bf16[1,64,16,128]{3,2,1,0:T(8,128)(2,1)S(1)} %get-tuple-element.143.refs_0_), channel_id=1, source_target_pairs={{0,4},{1,5},{2,6},{3,7},{4,0},{5,1},{6,2},{7,3},{8,12},{9,13},{10,... | collective-permute-start | bytes 786440 | tf_op jit(solution)/shard_map/ppermute | solution.py:239
  115.3 8.7 %collective-permute-start.33 = (bf16[1,64,16,128]{3,2,1,0:T(8,128)(2,1)S(1)}, bf16[1,64,16,128]{3,2,1,0:T(8,128)(2,1)S(1)}, u32[]{:S(2)}, u32[]{:S(2)}) collective-permute-start(bf16[1,64,16,128]{3,2,1,0:T(8,128)(2,1)S(1)} %get-tuple-element.143.refs_0_), channel_id=1, source_target_pairs={{0,6},{1,7},{2,4},{3,5},{4,2},{5,3},{6,0},{7,1},{8,14},{9,15},{10,... | collective-permute-start | bytes 786440 | tf_op jit(solution)/shard_map/ppermute | solution.py:239
  120.4 10.6 %collective-permute-start.34 = (bf16[2,512,128]{2,1,0:T(8,128)(2,1)S(1)}, bf16[2,512,128]{2,1,0:T(8,128)(2,1)S(1)}, u32[]{:S(2)}, u32[]{:S(2)}) collective-permute-start(bf16[2,512,128]{2,1,0:T(8,128)(2,1)S(1)} %fusion), channel_id=1, source_target_pairs={{0,16},{8,24},{16,0},{24,8},{1,17},{9,25},{17,1},{25,9},{2,18},{10... | collective-permute-start | bytes 786440 | tf_op jit(solution)/shard_map/ppermute | solution.py:242
  126.1 9.3 %copy-start.3 = (bf16[32,64]{1,0:T(8,128)(2,1)S(1)}, bf16[32,64]{1,0:T(8,128)(2,1)}, u32[]{:S(2)}) copy-start(bf16[32,64]{1,0:T(8,128)(2,1)} %param.9) | copy-start | bytes 12292
  131.8 3.6 %collective-permute-start.35 = (bf16[512,512]{1,0:T(8,128)(2,1)S(1)}, bf16[512,512]{1,0:T(8,128)(2,1)S(1)}, u32[]{:S(2)}, u32[]{:S(2)}) collective-permute-start(bf16[512,512]{1,0:T(8,128)(2,1)S(1)} %get-tuple-element.147), channel_id=1, source_target_pairs={{0,1},{1,0},{2,3},{3,2},{4,5},{5,4},{6,7},{7,6},{8,9},{9,8},{10,11... | collective-permute-start | bytes 1572872 | tf_op jit(solution)/shard_map/ppermute | solution.py:239
  131.9 9.2 %collective-permute-start.36 = (bf16[1,64,16,128]{3,2,1,0:T(8,128)(2,1)S(1)}, bf16[1,64,16,128]{3,2,1,0:T(8,128)(2,1)S(1)}, u32[]{:S(2)}, u32[]{:S(2)}) collective-permute-start(bf16[1,64,16,128]{3,2,1,0:T(8,128)(2,1)S(1)} %get-tuple-element.150.refs_0_), channel_id=1, source_target_pairs={{0,2},{1,3},{2,0},{3,1},{4,6},{5,7},{6,4},{7,5},{8,10},{9,11},{10,... | collective-permute-start | bytes 786440 | tf_op jit(solution)/shard_map/ppermute | solution.py:239
  132.0 14.2 %collective-permute-start.37 = (bf16[1,64,16,128]{3,2,1,0:T(8,128)(2,1)S(1)}, bf16[1,64,16,128]{3,2,1,0:T(8,128)(2,1)S(1)}, u32[]{:S(2)}, u32[]{:S(2)}) collective-permute-start(bf16[1,64,16,128]{3,2,1,0:T(8,128)(2,1)S(1)} %get-tuple-element.150.refs_0_), channel_id=1, source_target_pairs={{0,4},{1,5},{2,6},{3,7},{4,0},{5,1},{6,2},{7,3},{8,12},{9,13},{10,... | collective-permute-start | bytes 786440 | tf_op jit(solution)/shard_map/ppermute | solution.py:239
  132.1 14.1 %collective-permute-start.38 = (bf16[1,64,16,128]{3,2,1,0:T(8,128)(2,1)S(1)}, bf16[1,64,16,128]{3,2,1,0:T(8,128)(2,1)S(1)}, u32[]{:S(2)}, u32[]{:S(2)}) collective-permute-start(bf16[1,64,16,128]{3,2,1,0:T(8,128)(2,1)S(1)} %get-tuple-element.150.refs_0_), channel_id=1, source_target_pairs={{0,6},{1,7},{2,4},{3,5},{4,2},{5,3},{6,0},{7,1},{8,14},{9,15},{10,... | collective-permute-start | bytes 786440 | tf_op jit(solution)/shard_map/ppermute | solution.py:239
  135.5 13.2 %collective-permute-start.39 = (bf16[32,64]{1,0:T(8,128)(2,1)S(1)}, bf16[32,64]{1,0:T(8,128)(2,1)S(1)}, u32[]{:S(2)}, u32[]{:S(2)}) collective-permute-start(bf16[32,64]{1,0:T(8,128)(2,1)S(1)} %copy-done.3), channel_id=1, source_target_pairs={{0,1},{1,0},{2,3},{3,2},{4,5},{5,4},{6,7},{7,6},{8,9},{9,8},{10,11... | collective-permute-start | bytes 12296 | tf_op jit(solution)/shard_map/ppermute | solution.py:239
  148.9 1.2 collective-permute-start.40
  150.6 3.9 %collective-permute-start.41 = (f32[32,64]{0,1:T(8,128)S(1)}, f32[32,64]{0,1:T(8,128)S(1)}, u32[]{:S(2)}, u32[]{:S(2)}) collective-permute-start(f32[32,64]{0,1:T(8,128)S(1)} %fusion.8), channel_id=1, source_target_pairs={{0,8},{8,0},{16,24},{24,16},{1,9},{9,1},{17,25},{25,17},{2,10},{10... | collective-permute-start | bytes 24584 | tf_op jit(solution)/shard_map/ppermute | solution.py:242
  154.5 5.0 %collective-permute-start.42 = (f32[32,64]{0,1:T(8,128)S(1)}, f32[32,64]{0,1:T(8,128)S(1)}, u32[]{:S(2)}, u32[]{:S(2)}) collective-permute-start(f32[32,64]{0,1:T(8,128)S(1)} %add.113), channel_id=1, source_target_pairs={{0,16},{8,24},{16,0},{24,8},{1,17},{9,25},{17,1},{25,9},{2,18},{10... | collective-permute-start | bytes 24584 | tf_op jit(solution)/shard_map/ppermute | solution.py:242

commit v2 on v0

--- a/solution.py
+++ b/solution.py
@@ -10,7 +10,8 @@
 CHUNKS = 4
 GROUPS = ((0,), (1,), (2,), (3,))
 ORDER = (
-    "W0", "M0", "W1", "A1", "P0", "M1", "W2", "A2", "P1", "M2", "C0", "W3", "A3", "P2", "C1", "M3", "F0", "C2", "F1", "P3", "F2", "C3", "R", "F3",
+    "W0", "M0", "W1", "A1", "P0", "M1", "W2", "A2", "P1", "M2", "C0", "W3", "A3", "M3",
+    "P2", "C1", "F0", "P3", "C2", "F1", "F2", "C3", "R", "F3",
 )
 LIMIT = 50 * 2**20
 NT = (((1,), (1,)), ((), ()))
@@ -20,8 +21,13 @@
 PARAMS = pltpu.CompilerParams(vmem_limit_bytes=LIMIT)
 
 
-def partial_kernel(cuts, info, left, partner, *refs):
-    *pieces, near, own, far, bra, ket, bra_sem, ket_sem = refs
+def cost(flops):
+    return pl.CostEstimate(flops=flops, bytes_accessed=1, transcendentals=0)
+
+
+def partial_kernel(cuts, nears, info, left, partner, *refs):
+    own, far, bra, ket, bra_sem, ket_sem = refs[-6:]
+    pieces, near = refs[: -6 - nears], refs[-6 - nears : -6]
     sectors, rows, states = left.shape
     cols = own.shape[2]
     copies = []
@@ -48,19 +54,19 @@
             out = term if out is None else out + term
         blocks = [out[:, k * cols : (k + 1) * cols] for k in range(4)]
         own[c] = blocks[0]
-        near[0, c] = blocks[1].astype(jnp.bfloat16)
-        near[1, c] = blocks[3].astype(jnp.bfloat16)
+        near[0][0, c] = blocks[1].astype(jnp.bfloat16)
+        near[nears - 1][2 - nears, c] = blocks[3].astype(jnp.bfloat16)
         far[c] = blocks[2].astype(far.dtype)
 
 
-def partial_products(info, left, partner, cols, cuts, *pieces):
+def partial_products(info, left, partner, cols, cuts, nears, *pieces):
     sectors, rows, states = left.shape
 
     block = (2, rows, cols)
     return pl.pallas_call(
-        functools.partial(partial_kernel, cuts),
+        functools.partial(partial_kernel, cuts, nears),
         in_specs=[SMEM] + [HBM] * (2 + len(pieces)),
-        out_specs=[VMEM] * 3,
+        out_specs=[VMEM] * (nears + 2),
         scratch_shapes=[
             pltpu.VMEM((sectors, 4 * cols, states), jnp.bfloat16),
             pltpu.VMEM((2, sectors, rows, states), jnp.bfloat16),
@@ -68,11 +74,12 @@
             pltpu.SemaphoreType.DMA((2,)),
         ],
         out_shape=[
-            jax.ShapeDtypeStruct((2, *block), jnp.bfloat16),
-            jax.ShapeDtypeStruct(block, jnp.float32),
-            jax.ShapeDtypeStruct(block, jnp.float32),
-        ],
+            jax.ShapeDtypeStruct((2 // nears, *block), jnp.bfloat16),
+        ]
+        * nears
+        + [jax.ShapeDtypeStruct(block, jnp.float32)] * 2,
         compiler_params=PARAMS,
+        cost_estimate=cost(16 * rows * sectors * states * cols),
         name="partial_products",
     )(info, left, partner, *pieces)
 
@@ -117,6 +124,7 @@
         + [pltpu.VMEM(block, bf16), pltpu.SemaphoreType.DMA((3,))],
         input_output_aliases={4 + i: i for i in range(len(held))},
         compiler_params=PARAMS,
+        cost_estimate=cost(8 * rows * cols),
         name="combine",
     )(core, mine, near, far, *held)
 
@@ -187,6 +195,7 @@
             pltpu.SemaphoreType.DMA((5,)),
         ],
         compiler_params=PARAMS,
+        cost_estimate=cost(2 * (orbitals + 16) * width * width * chunks * cols),
         name="fock_terms",
     )(base, slab, diagonal, *pieces)
 
@@ -213,6 +222,7 @@
         ),
         out_shape=jax.ShapeDtypeStruct((width, 2 * orbitals, total), jnp.bfloat16),
         compiler_params=PARAMS,
+        cost_estimate=cost(orbitals * width * total),
         name="turn",
     )(core, slab, received)
 
@@ -262,14 +272,14 @@
         (column_ids // width == column_ids % width).astype(jnp.bfloat16)[None], (16, rows)
     )
 
-    def products(chunk, *parts):
+    def products(chunk, nears, *parts):
         mine = slice(chunk * cols, (chunk + 1) * cols)
         every = slice(None)
         cuts = [(0, (every, mine), 0, 0)] + [(n, (every,), 0, n) for n in range(1, 4)]
         if len(parts) == 4:
             cuts.append((4, (every,), half, 3))
         info = jnp.concatenate([number(chip ^ z), block_sizes])
-        return partial_products(info, amps_left, partner_left, cols, cuts, amps_right, *parts)
+        return partial_products(info, amps_left, partner_left, cols, cuts, nears, amps_right, *parts)
 
     sums, terms, gathered = [None] * CHUNKS, [], {}
 
@@ -297,15 +307,19 @@
             state["xs"], state["ys"] = across(sent, 2), across(sent, 4)
 
     def do_products(chunk):
-        near, own, far = products(chunk, *(after(p, state["last"]) for p in pieces[chunk]))
-        sums[chunk] = [own, along(near, 1), far]
+        nears = 2 if chunk == CHUNKS - 1 else 1
+        *near, own, far = products(chunk, nears, *(after(p, state["last"]) for p in pieces[chunk]))
+        near[-1] = along(near[-1], 1)
+        sums[chunk] = [own, near, far]
         state["last"] = own
 
     def do_pass(chunk):
         own, near, far = sums[chunk]
         far = after(far, state["last"])
-        passed = (far + near[1].astype(jnp.float32)).astype(jnp.bfloat16)
-        sums[chunk] = [own, near, along(passed, 2)]
+        passed = (far + near[-1][-1].astype(jnp.float32)).astype(jnp.bfloat16)
+        if len(near) == 2:
+            near[0] = along(after(near[0], passed), 1)
+        sums[chunk] = [own, near[0], along(passed, 2)]
         state["last"] = passed
 
     def do_finish(chunk):

time: 165 us -> 159 us (0.964)
  waiting for transfers between devices: 67.3 us -> 55.1 us
  local copies, waits for them, and re-layouts: 7 us -> 10.6 us
  starting transfers between devices: 49.2 us -> 51.8 us
    ppermute x33, waiting for transfers between devices: 49.9 us -> 43.4 us  [across(): return lax.ppermute(value, 'gen', [(i, i ^ flip) for i in range(gens)])]
    ppermute x10 -> x11, waiting for transfers between devices: 17.4 us -> 11.7 us  [along(): return lax.ppermute(value, 'sec', [(i, i ^ flip) for i in range(secs)])]
    unnamed x13 -> x15, local copies, waits for them, and re-layouts: 1.42 us -> 4.46 us
    ppermute x10 -> x11, starting transfers between devices: 15.9 us -> 17 us  [along(): return lax.ppermute(value, 'sec', [(i, i ^ flip) for i in range(secs)])]
  transfers between devices with their start and end apart: 43 -> 44, of which waited for: 22 -> 19; matrix products, arithmetic and copies ran while one was open for 2% -> 2% of each run, Pallas kernels for 23% -> 24%
where the time goes in v2:
time: 159 us; the launch traced here: 158 us
  waiting for transfers between devices  55.1 us (35%)
  starting transfers between devices  51.8 us (33%)
  Pallas kernels  38.3 us (24%)
  local copies, waits for them, and re-layouts  10.6 us (7%)
    ppermute x33, waiting for transfers between devices, across(): return lax.ppermute(value, 'gen', [(i, i ^ flip) for i in range(gens)])  43.4 us
    ppermute x33, starting transfers between devices, across(): return lax.ppermute(value, 'gen', [(i, i ^ flip) for i in range(gens)])  34.8 us
    pallas_call x4, Pallas kernels, partial_products(): pl.pallas_call(functools.partial(partial_kernel, cuts, nears), in_specs=[...  20.7 us
    ppermute x11, starting transfers between devices, along(): return lax.ppermute(value, 'sec', [(i, i ^ flip) for i in range(secs)])  17 us
    ppermute x11, waiting for transfers between devices, along(): return lax.ppermute(value, 'sec', [(i, i ^ flip) for i in range(secs)])  11.7 us
    pallas_call x4, Pallas kernels, fock_terms(): pl.pallas_call(functools.partial(fock_kernel, first), in_specs=[SMEM, HBM...  8.39 us
    pallas_call x1, Pallas kernels, turn(): pl.pallas_call(turn_kernel, grid_spec=pltpu.PrefetchScalarGridSpec(num_sc...  5.21 us
    unnamed x15, local copies, waits for them, and re-layouts  4.46 us
  transfers between devices with their start and end apart: 44, of which 19 were waited for; matrix products, arithmetic and copies ran while one was open for 2% of the time, Pallas kernels for 24%

profile of v2, /device:TPU:0, one launch (start us, length us, event | category | flops | bytes accessed | tf_op | source)
XLA Modules:
  0.0 158.4 jit_solution(5114866007776726449)
XLA Ops:
  1.8 2.0 %constant_dynamic-slice_fusion = bf16[32,64,512]{2,1,0:T(8,128)(2,1)S(1)} fusion(bf16[32,64,1024]{2,1,0:T(8,128)(2,1)} %a.1, s32[]{:T(128)S(6)} %select_n.79), kind=kLoop, calls=%fused_computation.35 | loop fusion | bytes 4194308 | tf_op jit(solution)/shard_map/dynamic_slice | solution.py:266
  4.3 2.9 %collective-permute-start.3 = (bf16[8,128,256]{2,1,0:T(8,128)(2,1)S(1)}, bf16[8,128,256]{2,1,0:T(8,128)(2,1)S(1)}, u32[]{:S(2)}, u32[]{:S(2)}) collective-permute-start(bf16[8,128,256]{2,1,0:T(8,128)(2,1)S(1)} %slice.85), channel_id=1, source_target_pairs={{0,4},{1,5},{2,6},{3,7},{4,0},{5,1},{6,2},{7,3},{8,12},{9,13},{10,... | collective-permute-start | bytes 1572872 | tf_op jit(solution)/shard_map/ppermute | solution.py:245
  7.3 1.5 collective-permute-start.2
  10.2 5.2 %turn.1.slab = bf16[64,64,512]{2,1,0:T(8,128)(2,1)} custom-call(s32[1]{0:T(128)} %bitcast.core, bf16[32,64,1024]{2,1,0:T(8,128)(2,1)} %a.1, bf16[32,64,512]{2,1,0:T(8,128)(2,1)S(1)} %collective-permute-done.1.b), custom_call_target="tpu_custom_call" | custom-call | flops 1048576 | bytes 1 | tf_op jit(solution)/shard_map/turn/pallas_call | solution.py:212
  15.4 4.0 %collective-permute-done.3.refs_2_ = bf16[8,128,256]{2,1,0:T(8,128)(2,1)S(1)} collective-permute-done((bf16[8,128,256]{2,1,0:T(8,128)(2,1)S(1)}, bf16[8,128,256]{2,1,0:T(8,128)(2,1)S(1)}, u32[]{:S(2)}, u32[]{:S(2)}) %collective-permute-start.3) | collective-permute-done | bytes 524320 | tf_op jit(solution)/shard_map/ppermute | solution.py:245
  19.4 1.8 %collective-permute-start.6 = (bf16[8,64,256]{2,1,0:T(8,128)(2,1)S(1)}, bf16[8,64,256]{2,1,0:T(8,128)(2,1)S(1)}, u32[]{:S(2)}, u32[]{:S(2)}) collective-permute-start(bf16[8,64,256]{2,1,0:T(8,128)(2,1)S(1)} %slice.90), channel_id=1, source_target_pairs={{0,2},{1,3},{2,0},{3,1},{4,6},{5,7},{6,4},{7,5},{8,10},{9,11},{10,... | collective-permute-start | bytes 786440 | tf_op jit(solution)/shard_map/ppermute | solution.py:245
  21.2 1.6 %collective-permute-start.5 = (bf16[8,64,256]{2,1,0:T(8,128)(2,1)S(1)}, bf16[8,64,256]{2,1,0:T(8,128)(2,1)S(1)}, u32[]{:S(2)}, u32[]{:S(2)}) collective-permute-start(bf16[8,64,256]{2,1,0:T(8,128)(2,1)S(1)} %slice.89), channel_id=1, source_target_pairs={{0,4},{1,5},{2,6},{3,7},{4,0},{5,1},{6,2},{7,3},{8,12},{9,13},{10,... | collective-permute-start | bytes 786440 | tf_op jit(solution)/shard_map/ppermute | solution.py:245
  24.6 4.2 %collective-permute-done.6.refs_4_ = bf16[8,64,256]{2,1,0:T(8,128)(2,1)S(1)} collective-permute-done((bf16[8,64,256]{2,1,0:T(8,128)(2,1)S(1)}, bf16[8,64,256]{2,1,0:T(8,128)(2,1)S(1)}, u32[]{:S(2)}, u32[]{:S(2)}) %collective-permute-start.6) | collective-permute-done | bytes 262176 | tf_op jit(solution)/shard_map/ppermute | solution.py:245
  28.7 1.8 %collective-permute-done.5.refs_3_ = bf16[8,64,256]{2,1,0:T(8,128)(2,1)S(1)} collective-permute-done((bf16[8,64,256]{2,1,0:T(8,128)(2,1)S(1)}, bf16[8,64,256]{2,1,0:T(8,128)(2,1)S(1)}, u32[]{:S(2)}, u32[]{:S(2)}) %collective-permute-start.5) | collective-permute-done | bytes 262176 | tf_op jit(solution)/shard_map/ppermute | solution.py:245
  30.6 5.0 %partial_products.4 = (bf16[2,2,512,128]{3,2,1,0:T(8,128)(2,1)S(1)}, f32[2,512,128]{2,1,0:T(8,128)S(1)}, f32[2,512,128]{2,1,0:T(8,128)S(1)}) custom-call(s32[9]{0:T(128)S(1)} %pad_add_fusion.info, bf16[8,512,256]{2,1,0:T(8,128)(2,1)} %left.7, bf16[8,512,256]{2,1,0:T(8,128)(2,1)} %collective-permute-done.partner, bf16[8,512,256]{2,1,0:T(8,128)(2,1)} %refs_0_.7, ...), custom_call_target="tpu_custom_call" | custom-call | flops 2147483648 | bytes 1 | tf_op jit(solution)/shard_map/partial_products/pallas_call | solution.py:66
  35.5 1.6 %collective-permute-start.11 = (bf16[2,2,512,128]{3,2,1,0:T(8,128)(2,1)S(1)}, bf16[2,2,512,128]{3,2,1,0:T(8,128)(2,1)S(1)}, u32[]{:S(2)}, u32[]{:S(2)}) collective-permute-start(bf16[2,2,512,128]{3,2,1,0:T(8,128)(2,1)S(1)} %get-tuple-element.100), channel_id=1, source_target_pairs={{0,8},{8,0},{16,24},{24,16},{1,9},{9,1},{17,25},{25,17},{2,10},{10... | collective-permute-start | bytes 1572872 | tf_op jit(solution)/shard_map/ppermute | solution.py:248
  37.2 2.6 %collective-permute-done.7.refs_2_ = bf16[8,128,256]{2,1,0:T(8,128)(2,1)S(1)} collective-permute-done((bf16[8,128,256]{2,1,0:T(8,128)(2,1)S(1)}, bf16[8,128,256]{2,1,0:T(8,128)(2,1)S(1)}, u32[]{:S(2)}, u32[]{:S(2)}) %collective-permute-start.7) | collective-permute-done | bytes 524320 | tf_op jit(solution)/shard_map/ppermute | solution.py:245
  39.7 1.2 collective-permute-start.10
  44.0 5.1 %collective-permute-done.10.refs_4_ = bf16[8,64,256]{2,1,0:T(8,128)(2,1)S(1)} collective-permute-done((bf16[8,64,256]{2,1,0:T(8,128)(2,1)S(1)}, bf16[8,64,256]{2,1,0:T(8,128)(2,1)S(1)}, u32[]{:S(2)}, u32[]{:S(2)}) %collective-permute-start.10) | collective-permute-done | bytes 262176 | tf_op jit(solution)/shard_map/ppermute | solution.py:245
  49.1 1.2 collective-permute-done.9.refs_3_
  50.3 5.0 %partial_products.5 = (bf16[2,2,512,128]{3,2,1,0:T(8,128)(2,1)S(1)}, f32[2,512,128]{2,1,0:T(8,128)S(1)}, f32[2,512,128]{2,1,0:T(8,128)S(1)}) custom-call(s32[9]{0:T(128)S(1)} %pad_add_fusion.info, bf16[8,512,256]{2,1,0:T(8,128)(2,1)} %left.7, bf16[8,512,256]{2,1,0:T(8,128)(2,1)} %collective-permute-done.partner, bf16[8,512,256]{2,1,0:T(8,128)(2,1)} %refs_0_.7, ...), custom_call_target="tpu_custom_call" | custom-call | flops 2147483648 | bytes 1 | tf_op jit(solution)/shard_map/partial_products/pallas_call | solution.py:66
  55.3 1.6 %collective-permute-start.16 = (bf16[2,2,512,128]{3,2,1,0:T(8,128)(2,1)S(1)}, bf16[2,2,512,128]{3,2,1,0:T(8,128)(2,1)S(1)}, u32[]{:S(2)}, u32[]{:S(2)}) collective-permute-start(bf16[2,2,512,128]{3,2,1,0:T(8,128)(2,1)S(1)} %get-tuple-element.111), channel_id=1, source_target_pairs={{0,8},{8,0},{16,24},{24,16},{1,9},{9,1},{17,25},{25,17},{2,10},{10... | collective-permute-start | bytes 1572872 | tf_op jit(solution)/shard_map/ppermute | solution.py:248
  56.9 1.3 collective-permute-done.12.refs_2_
  59.2 1.7 %collective-permute-start.14 = (bf16[8,64,256]{2,1,0:T(8,128)(2,1)S(1)}, bf16[8,64,256]{2,1,0:T(8,128)(2,1)S(1)}, u32[]{:S(2)}, u32[]{:S(2)}) collective-permute-start(bf16[8,64,256]{2,1,0:T(8,128)(2,1)S(1)} %slice.94), channel_id=1, source_target_pairs={{0,4},{1,5},{2,6},{3,7},{4,0},{5,1},{6,2},{7,3},{8,12},{9,13},{10,... | collective-permute-start | bytes 786440 | tf_op jit(solution)/shard_map/ppermute | solution.py:245
  62.4 5.1 %collective-permute-done.15.refs_4_ = bf16[8,64,256]{2,1,0:T(8,128)(2,1)S(1)} collective-permute-done((bf16[8,64,256]{2,1,0:T(8,128)(2,1)S(1)}, bf16[8,64,256]{2,1,0:T(8,128)(2,1)S(1)}, u32[]{:S(2)}, u32[]{:S(2)}) %collective-permute-start.15) | collective-permute-done | bytes 262176 | tf_op jit(solution)/shard_map/ppermute | solution.py:245
  67.5 2.6 %collective-permute-start.17 = (bf16[2,512,128]{2,1,0:T(8,128)(2,1)S(1)}, bf16[2,512,128]{2,1,0:T(8,128)(2,1)S(1)}, u32[]{:S(2)}, u32[]{:S(2)}) collective-permute-start(bf16[2,512,128]{2,1,0:T(8,128)(2,1)S(1)} %fusion.3), channel_id=1, source_target_pairs={{0,16},{8,24},{16,0},{24,8},{1,17},{9,25},{17,1},{25,9},{2,18},{10... | collective-permute-start | bytes 786440 | tf_op jit(solution)/shard_map/ppermute | solution.py:248
  70.9 5.7 %partial_products.6 = (bf16[2,2,512,128]{3,2,1,0:T(8,128)(2,1)}, f32[2,512,128]{2,1,0:T(8,128)S(1)}, f32[2,512,128]{2,1,0:T(8,128)S(1)}) custom-call(s32[9]{0:T(128)S(1)} %pad_add_fusion.info, bf16[8,512,256]{2,1,0:T(8,128)(2,1)} %left.7, bf16[8,512,256]{2,1,0:T(8,128)(2,1)} %collective-permute-done.partner, bf16[8,512,256]{2,1,0:T(8,128)(2,1)} %refs_0_.7, ...), custom_call_target="tpu_custom_call" | custom-call | flops 2147483648 | bytes 1 | tf_op jit(solution)/shard_map/partial_products/pallas_call | solution.py:66
  76.6 1.6 %collective-permute-start.21 = (bf16[2,2,512,128]{3,2,1,0:T(8,128)(2,1)}, bf16[2,2,512,128]{3,2,1,0:T(8,128)(2,1)S(1)}, u32[]{:S(2)}, u32[]{:S(2)}) collective-permute-start(bf16[2,2,512,128]{3,2,1,0:T(8,128)(2,1)} %get-tuple-element.129), channel_id=1, source_target_pairs={{0,8},{8,0},{16,24},{24,16},{1,9},{9,1},{17,25},{25,17},{2,10},{10... | collective-permute-start | bytes 1572872 | tf_op jit(solution)/shard_map/ppermute | solution.py:248
  83.2 1.6 %collective-permute-start.19 = (bf16[8,64,256]{2,1,0:T(8,128)(2,1)}, bf16[8,64,256]{2,1,0:T(8,128)(2,1)}, u32[]{:S(2)}, u32[]{:S(2)}) collective-permute-start(bf16[8,64,256]{2,1,0:T(8,128)(2,1)} %slice.97), channel_id=1, source_target_pairs={{0,4},{1,5},{2,6},{3,7},{4,0},{5,1},{6,2},{7,3},{8,12},{9,13},{10,... | collective-permute-start | bytes 786440 | tf_op jit(solution)/shard_map/ppermute | solution.py:245
  84.8 1.8 %collective-permute-start.22 = (bf16[2,512,128]{2,1,0:T(8,128)(2,1)}, bf16[2,512,128]{2,1,0:T(8,128)(2,1)S(1)}, u32[]{:S(2)}, u32[]{:S(2)}) collective-permute-start(bf16[2,512,128]{2,1,0:T(8,128)(2,1)} %fusion.2), channel_id=1, source_target_pairs={{0,16},{8,24},{16,0},{24,8},{1,17},{9,25},{17,1},{25,9},{2,18},{10... | collective-permute-start | bytes 786440 | tf_op jit(solution)/shard_map/ppermute | solution.py:248
  87.0 2.9 %collective-permute-done.20.refs_4_ = bf16[8,64,256]{2,1,0:T(8,128)(2,1)} collective-permute-done((bf16[8,64,256]{2,1,0:T(8,128)(2,1)}, bf16[8,64,256]{2,1,0:T(8,128)(2,1)}, u32[]{:S(2)}, u32[]{:S(2)}) %collective-permute-start.20) | collective-permute-done | bytes 262176 | tf_op jit(solution)/shard_map/ppermute | solution.py:245
  91.4 1.5 collective-permute-start.25
  95.0 5.0 %partial_products.7 = (bf16[1,2,512,128]{3,2,1,0:T(8,128)(2,1)S(1)}, bf16[1,2,512,128]{3,2,1,0:T(8,128)(2,1)S(1)}, f32[2,512,128]{2,1,0:T(8,128)S(1)}, f32[2,512,128]{2,1,0:T(8,128)S(1)}) custom-call(s32[9]{0:T(128)S(1)} %pad_add_fusion.info, bf16[8,512,256]{2,1,0:T(8,128)(2,1)} %left.7, bf16[8,512,256]{2,1,0:T(8,128)(2,1)} %collective-permute-done.partner, ...), custom_call_target="tpu_custom_call" | custom-call | flops 2147483648 | bytes 1 | tf_op jit(solution)/shard_map/partial_products/pallas_call | solution.py:66
  101.1 2.9 %collective-permute-start.27 = (bf16[2,512,128]{2,1,0:T(8,128)(2,1)S(1)}, bf16[2,512,128]{2,1,0:T(8,128)(2,1)S(1)}, u32[]{:S(2)}, u32[]{:S(2)}) collective-permute-start(bf16[2,512,128]{2,1,0:T(8,128)(2,1)S(1)} %fusion.1), channel_id=1, source_target_pairs={{0,16},{8,24},{16,0},{24,8},{1,17},{9,25},{17,1},{25,9},{2,18},{10... | collective-permute-start | bytes 786440 | tf_op jit(solution)/shard_map/ppermute | solution.py:248
  104.8 1.3 collective-permute-start.28
  106.8 1.7 %collective-permute-start.30 = (bf16[1,64,16,128]{3,2,1,0:T(8,128)(2,1)S(1)}, bf16[1,64,16,128]{3,2,1,0:T(8,128)(2,1)S(1)}, u32[]{:S(2)}, u32[]{:S(2)}) collective-permute-start(bf16[1,64,16,128]{3,2,1,0:T(8,128)(2,1)S(1)} %get-tuple-element.142.refs_0_), channel_id=1, source_target_pairs={{0,6},{1,7},{2,4},{3,5},{4,2},{5,3},{6,0},{7,1},{8,14},{9,15},{10,... | collective-permute-start | bytes 786440 | tf_op jit(solution)/shard_map/ppermute | solution.py:245
  108.5 2.1 %fock_terms.4 = (f32[64,64]{1,0:T(8,128)S(1)}, f32[64,64]{1,0:T(8,128)S(1)}) custom-call(s32[1]{0:T(128)} %bitcast.4.base, bf16[64,64,512]{2,1,0:T(8,128)(2,1)} %turn.1.slab, bf16[16,128]{1,0:T(8,128)(2,1)S(1)} %broadcast_in_dim.18.diagonal, bf16[1,64,16,128]{3,2,1,0:T(8,128)(2,1)S(1)} %get-tuple-element.134.refs_0_, ...), custom_call_target="tpu_custom_call" | custom-call | flops 83886080 | bytes 1 | tf_op jit(solution)/shard_map/fock_terms/pallas_call | solution.py:184
  111.5 2.1 %collective-permute-start.31 = (bf16[1,64,16,128]{3,2,1,0:T(8,128)(2,1)S(1)}, bf16[1,64,16,128]{3,2,1,0:T(8,128)(2,1)S(1)}, u32[]{:S(2)}, u32[]{:S(2)}) collective-permute-start(bf16[1,64,16,128]{3,2,1,0:T(8,128)(2,1)S(1)} %get-tuple-element.145.refs_0_), channel_id=1, source_target_pairs={{0,2},{1,3},{2,0},{3,1},{4,6},{5,7},{6,4},{7,5},{8,10},{9,11},{10,... | collective-permute-start | bytes 786440 | tf_op jit(solution)/shard_map/ppermute | solution.py:245
  113.9 1.1 collective-permute-start.33
  115.1 1.2 collective-permute-done.29.refs_2_
  116.3 1.5 collective-permute-start.34
  117.8 2.2 %collective-permute-start.35 = (bf16[2,512,128]{2,1,0:T(8,128)(2,1)S(1)}, bf16[2,512,128]{2,1,0:T(8,128)(2,1)S(1)}, u32[]{:S(2)}, u32[]{:S(2)}) collective-permute-start(bf16[2,512,128]{2,1,0:T(8,128)(2,1)S(1)} %fusion), channel_id=1, source_target_pairs={{0,16},{8,24},{16,0},{24,8},{1,17},{9,25},{17,1},{25,9},{2,18},{10... | collective-permute-start | bytes 786440 | tf_op jit(solution)/shard_map/ppermute | solution.py:248
  120.0 2.1 %fock_terms.5 = (f32[64,64]{1,0:T(8,128)S(1)}, f32[64,64]{1,0:T(8,128)S(1)}) custom-call(s32[1]{0:T(128)} %bitcast.4.base, bf16[64,64,512]{2,1,0:T(8,128)(2,1)} %turn.1.slab, bf16[16,128]{1,0:T(8,128)(2,1)S(1)} %broadcast_in_dim.17.diagonal, bf16[1,64,16,128]{3,2,1,0:T(8,128)(2,1)S(1)} %get-tuple-element.142.refs_0_, ...), custom_call_target="tpu_custom_call" | custom-call | flops 83886080 | bytes 1 | tf_op jit(solution)/shard_map/fock_terms/pallas_call | solution.py:184
  122.7 2.1 %fock_terms.6 = (f32[64,64]{1,0:T(8,128)S(1)}, f32[64,64]{1,0:T(8,128)S(1)}) custom-call(s32[1]{0:T(128)} %bitcast.4.base, bf16[64,64,512]{2,1,0:T(8,128)(2,1)} %turn.1.slab, bf16[16,128]{1,0:T(8,128)(2,1)S(1)} %broadcast_in_dim.16.diagonal, bf16[1,64,16,128]{3,2,1,0:T(8,128)(2,1)S(1)} %get-tuple-element.145.refs_0_, ...), custom_call_target="tpu_custom_call" | custom-call | flops 83886080 | bytes 1 | tf_op jit(solution)/shard_map/fock_terms/pallas_call | solution.py:184
  124.9 3.1 %collective-permute-done.35.b = bf16[2,512,128]{2,1,0:T(8,128)(2,1)S(1)} collective-permute-done((bf16[2,512,128]{2,1,0:T(8,128)(2,1)S(1)}, bf16[2,512,128]{2,1,0:T(8,128)(2,1)S(1)}, u32[]{:S(2)}, u32[]{:S(2)}) %collective-permute-start.35) | collective-permute-done | bytes 262176 | tf_op jit(solution)/shard_map/ppermute | solution.py:248
  128.8 1.7 %collective-permute-start.37 = (bf16[1,64,16,128]{3,2,1,0:T(8,128)(2,1)S(1)}, bf16[1,64,16,128]{3,2,1,0:T(8,128)(2,1)S(1)}, u32[]{:S(2)}, u32[]{:S(2)}) collective-permute-start(bf16[1,64,16,128]{3,2,1,0:T(8,128)(2,1)S(1)} %get-tuple-element.154.refs_0_), channel_id=1, source_target_pairs={{0,2},{1,3},{2,0},{3,1},{4,6},{5,7},{6,4},{7,5},{8,10},{9,11},{10,... | collective-permute-start | bytes 786440 | tf_op jit(solution)/shard_map/ppermute | solution.py:245
  130.6 1.8 %collective-permute-start.39 = (bf16[1,64,16,128]{3,2,1,0:T(8,128)(2,1)S(1)}, bf16[1,64,16,128]{3,2,1,0:T(8,128)(2,1)S(1)}, u32[]{:S(2)}, u32[]{:S(2)}) collective-permute-start(bf16[1,64,16,128]{3,2,1,0:T(8,128)(2,1)S(1)} %get-tuple-element.154.refs_0_), channel_id=1, source_target_pairs={{0,6},{1,7},{2,4},{3,5},{4,2},{5,3},{6,0},{7,1},{8,14},{9,15},{10,... | collective-permute-start | bytes 786440 | tf_op jit(solution)/shard_map/ppermute | solution.py:245
  133.2 4.8 %collective-permute-done.37.refs_1_ = bf16[1,64,16,128]{3,2,1,0:T(8,128)(2,1)S(1)} collective-permute-done((bf16[1,64,16,128]{3,2,1,0:T(8,128)(2,1)S(1)}, bf16[1,64,16,128]{3,2,1,0:T(8,128)(2,1)S(1)}, u32[]{:S(2)}, u32[]{:S(2)}) %collective-permute-start.37) | collective-permute-done | bytes 262176 | tf_op jit(solution)/shard_map/ppermute | solution.py:245
  138.0 6.6 %collective-permute-done.38.refs_2_ = bf16[1,64,16,128]{3,2,1,0:T(8,128)(2,1)S(1)} collective-permute-done((bf16[1,64,16,128]{3,2,1,0:T(8,128)(2,1)S(1)}, bf16[1,64,16,128]{3,2,1,0:T(8,128)(2,1)S(1)}, u32[]{:S(2)}, u32[]{:S(2)}) %collective-permute-start.38) | collective-permute-done | bytes 262176 | tf_op jit(solution)/shard_map/ppermute | solution.py:245
  144.6 2.1 %fock_terms.7 = (f32[64,64]{1,0:T(8,128)S(1)}, f32[64,64]{1,0:T(8,128)S(1)}) custom-call(s32[1]{0:T(128)} %bitcast.4.base, bf16[64,64,512]{2,1,0:T(8,128)(2,1)} %turn.1.slab, bf16[16,128]{1,0:T(8,128)(2,1)S(1)} %broadcast_in_dim.19.diagonal, bf16[1,64,16,128]{3,2,1,0:T(8,128)(2,1)S(1)} %get-tuple-element.154.refs_0_, ...), custom_call_target="tpu_custom_call" | custom-call | flops 83886080 | bytes 1 | tf_op jit(solution)/shard_map/fock_terms/pallas_call | solution.py:184
  147.3 1.2 collective-permute-done.41
  149.0 3.9 %collective-permute-done.42 = f32[32,64]{0,1:T(8,128)S(1)} collective-permute-done((f32[32,64]{0,1:T(8,128)S(1)}, f32[32,64]{0,1:T(8,128)S(1)}, u32[]{:S(2)}, u32[]{:S(2)}) %collective-permute-start.42) | collective-permute-done | bytes 8224 | tf_op jit(solution)/shard_map/ppermute | solution.py:248
  153.0 4.7 %collective-permute-done.43 = f32[32,64]{0,1:T(8,128)S(1)} collective-permute-done((f32[32,64]{0,1:T(8,128)S(1)}, f32[32,64]{0,1:T(8,128)S(1)}, u32[]{:S(2)}, u32[]{:S(2)}) %collective-permute-start.43) | collective-permute-done | bytes 8224 | tf_op jit(solution)/shard_map/ppermute | solution.py:248
  (109 shorter events, 28.3 us)
Async XLA Ops:
  1.7 7.0 %copy-start.4 = (bf16[8,512,256]{2,1,0:T(8,128)(2,1)S(1)}, bf16[8,512,256]{2,1,0:T(8,128)(2,1)}, u32[]{:S(2)}) copy-start(bf16[8,512,256]{2,1,0:T(8,128)(2,1)} %refs_0_.7) | copy-start | bytes 6291460
  3.7 6.5 %collective-permute-start.1 = (bf16[32,64,512]{2,1,0:T(8,128)(2,1)S(1)}, bf16[32,64,512]{2,1,0:T(8,128)(2,1)S(1)}, u32[]{:S(2)}, u32[]{:S(2)}) collective-permute-start(bf16[32,64,512]{2,1,0:T(8,128)(2,1)S(1)} %constant_dynamic-slice_fusion), channel_id=1, source_target_pairs={{0,1},{1,0},{2,3},{3,2},{4,5},{5,4},{6,7},{7,6},{8,9},{9,8},{10,11... | collective-permute-start | bytes 6291464 | tf_op jit(solution)/shard_map/ppermute | solution.py:245
  4.2 26.3 %collective-permute-start = (bf16[8,512,256]{2,1,0:T(8,128)(2,1)}, bf16[8,512,256]{2,1,0:T(8,128)(2,1)}, u32[]{:S(2)}, u32[]{:S(2)}) collective-permute-start(bf16[8,512,256]{2,1,0:T(8,128)(2,1)} %left.7), channel_id=1, source_target_pairs={{0,1},{1,0},{2,3},{3,2},{4,5},{5,4},{6,7},{7,6},{8,9},{9,8},{10,11... | collective-permute-start | bytes 6291464 | tf_op jit(solution)/shard_map/ppermute | solution.py:245
  4.3 15.1 %collective-permute-start.3 = (bf16[8,128,256]{2,1,0:T(8,128)(2,1)S(1)}, bf16[8,128,256]{2,1,0:T(8,128)(2,1)S(1)}, u32[]{:S(2)}, u32[]{:S(2)}) collective-permute-start(bf16[8,128,256]{2,1,0:T(8,128)(2,1)S(1)} %slice.85), channel_id=1, source_target_pairs={{0,4},{1,5},{2,6},{3,7},{4,0},{5,1},{6,2},{7,3},{8,12},{9,13},{10,... | collective-permute-start | bytes 1572872 | tf_op jit(solution)/shard_map/ppermute | solution.py:245
  7.3 14.0 %collective-permute-start.2 = (bf16[8,128,256]{2,1,0:T(8,128)(2,1)S(1)}, bf16[8,128,256]{2,1,0:T(8,128)(2,1)S(1)}, u32[]{:S(2)}, u32[]{:S(2)}) collective-permute-start(bf16[8,128,256]{2,1,0:T(8,128)(2,1)S(1)} %slice.85), channel_id=1, source_target_pairs={{0,2},{1,3},{2,0},{3,1},{4,6},{5,7},{6,4},{7,5},{8,10},{9,11},{10,... | collective-permute-start | bytes 1572872 | tf_op jit(solution)/shard_map/ppermute | solution.py:245
  10.2 14.3 %copy-start.6 = (s32[8]{0:T(128)S(1)}, s32[8]{0:T(128)}, u32[]{:S(2)}) copy-start(s32[8]{0:T(128)} %param.7) | copy-start | bytes 100
  19.4 9.3 %collective-permute-start.6 = (bf16[8,64,256]{2,1,0:T(8,128)(2,1)S(1)}, bf16[8,64,256]{2,1,0:T(8,128)(2,1)S(1)}, u32[]{:S(2)}, u32[]{:S(2)}) collective-permute-start(bf16[8,64,256]{2,1,0:T(8,128)(2,1)S(1)} %slice.90), channel_id=1, source_target_pairs={{0,2},{1,3},{2,0},{3,1},{4,6},{5,7},{6,4},{7,5},{8,10},{9,11},{10,... | collective-permute-start | bytes 786440 | tf_op jit(solution)/shard_map/ppermute | solution.py:245
  21.2 9.3 %collective-permute-start.5 = (bf16[8,64,256]{2,1,0:T(8,128)(2,1)S(1)}, bf16[8,64,256]{2,1,0:T(8,128)(2,1)S(1)}, u32[]{:S(2)}, u32[]{:S(2)}) collective-permute-start(bf16[8,64,256]{2,1,0:T(8,128)(2,1)S(1)} %slice.89), channel_id=1, source_target_pairs={{0,4},{1,5},{2,6},{3,7},{4,0},{5,1},{6,2},{7,3},{8,12},{9,13},{10,... | collective-permute-start | bytes 786440 | tf_op jit(solution)/shard_map/ppermute | solution.py:245
  22.8 16.9 %collective-permute-start.7 = (bf16[8,128,256]{2,1,0:T(8,128)(2,1)S(1)}, bf16[8,128,256]{2,1,0:T(8,128)(2,1)S(1)}, u32[]{:S(2)}, u32[]{:S(2)}) collective-permute-start(bf16[8,128,256]{2,1,0:T(8,128)(2,1)S(1)} %get-tuple-element.89), channel_id=1, source_target_pairs={{0,4},{1,5},{2,6},{3,7},{4,0},{5,1},{6,2},{7,3},{8,12},{9,13},{10,... | collective-permute-start | bytes 1572872 | tf_op jit(solution)/shard_map/ppermute | solution.py:245
  23.3 17.6 %collective-permute-start.4 = (bf16[8,128,256]{2,1,0:T(8,128)(2,1)S(1)}, bf16[8,128,256]{2,1,0:T(8,128)(2,1)S(1)}, u32[]{:S(2)}, u32[]{:S(2)}) collective-permute-start(bf16[8,128,256]{2,1,0:T(8,128)(2,1)S(1)} %get-tuple-element.89), channel_id=1, source_target_pairs={{0,2},{1,3},{2,0},{3,1},{4,6},{5,7},{6,4},{7,5},{8,10},{9,11},{10,... | collective-permute-start | bytes 1572872 | tf_op jit(solution)/shard_map/ppermute | solution.py:245
  35.5 14.7 %collective-permute-start.11 = (bf16[2,2,512,128]{3,2,1,0:T(8,128)(2,1)S(1)}, bf16[2,2,512,128]{3,2,1,0:T(8,128)(2,1)S(1)}, u32[]{:S(2)}, u32[]{:S(2)}) collective-permute-start(bf16[2,2,512,128]{3,2,1,0:T(8,128)(2,1)S(1)} %get-tuple-element.100), channel_id=1, source_target_pairs={{0,8},{8,0},{16,24},{24,16},{1,9},{9,1},{17,25},{25,17},{2,10},{10... | collective-permute-start | bytes 1572872 | tf_op jit(solution)/shard_map/ppermute | solution.py:248
  39.7 9.3 %collective-permute-start.10 = (bf16[8,64,256]{2,1,0:T(8,128)(2,1)S(1)}, bf16[8,64,256]{2,1,0:T(8,128)(2,1)S(1)}, u32[]{:S(2)}, u32[]{:S(2)}) collective-permute-start(bf16[8,64,256]{2,1,0:T(8,128)(2,1)S(1)} %slice.92), channel_id=1, source_target_pairs={{0,2},{1,3},{2,0},{3,1},{4,6},{5,7},{6,4},{7,5},{8,10},{9,11},{10,... | collective-permute-start | bytes 786440 | tf_op jit(solution)/shard_map/ppermute | solution.py:245
  40.9 9.3 %collective-permute-start.9 = (bf16[8,64,256]{2,1,0:T(8,128)(2,1)S(1)}, bf16[8,64,256]{2,1,0:T(8,128)(2,1)S(1)}, u32[]{:S(2)}, u32[]{:S(2)}) collective-permute-start(bf16[8,64,256]{2,1,0:T(8,128)(2,1)S(1)} %slice.91), channel_id=1, source_target_pairs={{0,4},{1,5},{2,6},{3,7},{4,0},{5,1},{6,2},{7,3},{8,12},{9,13},{10,... | collective-permute-start | bytes 786440 | tf_op jit(solution)/shard_map/ppermute | solution.py:245
  41.9 16.2 %collective-permute-start.12 = (bf16[8,128,256]{2,1,0:T(8,128)(2,1)S(1)}, bf16[8,128,256]{2,1,0:T(8,128)(2,1)S(1)}, u32[]{:S(2)}, u32[]{:S(2)}) collective-permute-start(bf16[8,128,256]{2,1,0:T(8,128)(2,1)S(1)} %get-tuple-element.97), channel_id=1, source_target_pairs={{0,4},{1,5},{2,6},{3,7},{4,0},{5,1},{6,2},{7,3},{8,12},{9,13},{10,... | collective-permute-start | bytes 1572872 | tf_op jit(solution)/shard_map/ppermute | solution.py:245
  43.0 16.2 %collective-permute-start.8 = (bf16[8,128,256]{2,1,0:T(8,128)(2,1)S(1)}, bf16[8,128,256]{2,1,0:T(8,128)(2,1)S(1)}, u32[]{:S(2)}, u32[]{:S(2)}) collective-permute-start(bf16[8,128,256]{2,1,0:T(8,128)(2,1)S(1)} %get-tuple-element.97), channel_id=1, source_target_pairs={{0,2},{1,3},{2,0},{3,1},{4,6},{5,7},{6,4},{7,5},{8,10},{9,11},{10,... | collective-permute-start | bytes 1572872 | tf_op jit(solution)/shard_map/ppermute | solution.py:245
  55.3 14.8 %collective-permute-start.16 = (bf16[2,2,512,128]{3,2,1,0:T(8,128)(2,1)S(1)}, bf16[2,2,512,128]{3,2,1,0:T(8,128)(2,1)S(1)}, u32[]{:S(2)}, u32[]{:S(2)}) collective-permute-start(bf16[2,2,512,128]{3,2,1,0:T(8,128)(2,1)S(1)} %get-tuple-element.111), channel_id=1, source_target_pairs={{0,8},{8,0},{16,24},{24,16},{1,9},{9,1},{17,25},{25,17},{2,10},{10... | collective-permute-start | bytes 1572872 | tf_op jit(solution)/shard_map/ppermute | solution.py:248
  58.2 9.3 %collective-permute-start.15 = (bf16[8,64,256]{2,1,0:T(8,128)(2,1)S(1)}, bf16[8,64,256]{2,1,0:T(8,128)(2,1)S(1)}, u32[]{:S(2)}, u32[]{:S(2)}) collective-permute-start(bf16[8,64,256]{2,1,0:T(8,128)(2,1)S(1)} %slice.95), channel_id=1, source_target_pairs={{0,2},{1,3},{2,0},{3,1},{4,6},{5,7},{6,4},{7,5},{8,10},{9,11},{10,... | collective-permute-start | bytes 786440 | tf_op jit(solution)/shard_map/ppermute | solution.py:245
  59.2 10.9 %collective-permute-start.14 = (bf16[8,64,256]{2,1,0:T(8,128)(2,1)S(1)}, bf16[8,64,256]{2,1,0:T(8,128)(2,1)S(1)}, u32[]{:S(2)}, u32[]{:S(2)}) collective-permute-start(bf16[8,64,256]{2,1,0:T(8,128)(2,1)S(1)} %slice.94), channel_id=1, source_target_pairs={{0,4},{1,5},{2,6},{3,7},{4,0},{5,1},{6,2},{7,3},{8,12},{9,13},{10,... | collective-permute-start | bytes 786440 | tf_op jit(solution)/shard_map/ppermute | solution.py:245
  60.9 18.2 %collective-permute-start.18 = (bf16[8,128,256]{2,1,0:T(8,128)(2,1)}, bf16[8,128,256]{2,1,0:T(8,128)(2,1)S(1)}, u32[]{:S(2)}, u32[]{:S(2)}) collective-permute-start(bf16[8,128,256]{2,1,0:T(8,128)(2,1)} %get-tuple-element.108), channel_id=1, source_target_pairs={{0,4},{1,5},{2,6},{3,7},{4,0},{5,1},{6,2},{7,3},{8,12},{9,13},{10,... | collective-permute-start | bytes 1572872 | tf_op jit(solution)/shard_map/ppermute | solution.py:245
  61.3 20.3 %collective-permute-start.13 = (bf16[8,128,256]{2,1,0:T(8,128)(2,1)}, bf16[8,128,256]{2,1,0:T(8,128)(2,1)S(1)}, u32[]{:S(2)}, u32[]{:S(2)}) collective-permute-start(bf16[8,128,256]{2,1,0:T(8,128)(2,1)} %get-tuple-element.108), channel_id=1, source_target_pairs={{0,2},{1,3},{2,0},{3,1},{4,6},{5,7},{6,4},{7,5},{8,10},{9,11},{10,... | collective-permute-start | bytes 1572872 | tf_op jit(solution)/shard_map/ppermute | solution.py:245
  67.5 10.8 %collective-permute-start.17 = (bf16[2,512,128]{2,1,0:T(8,128)(2,1)S(1)}, bf16[2,512,128]{2,1,0:T(8,128)(2,1)S(1)}, u32[]{:S(2)}, u32[]{:S(2)}) collective-permute-start(bf16[2,512,128]{2,1,0:T(8,128)(2,1)S(1)} %fusion.3), channel_id=1, source_target_pairs={{0,16},{8,24},{16,0},{24,8},{1,17},{9,25},{17,1},{25,9},{2,18},{10... | collective-permute-start | bytes 786440 | tf_op jit(solution)/shard_map/ppermute | solution.py:248
  76.6 23.4 %collective-permute-start.21 = (bf16[2,2,512,128]{3,2,1,0:T(8,128)(2,1)}, bf16[2,2,512,128]{3,2,1,0:T(8,128)(2,1)S(1)}, u32[]{:S(2)}, u32[]{:S(2)}) collective-permute-start(bf16[2,2,512,128]{3,2,1,0:T(8,128)(2,1)} %get-tuple-element.129), channel_id=1, source_target_pairs={{0,8},{8,0},{16,24},{24,16},{1,9},{9,1},{17,25},{25,17},{2,10},{10... | collective-permute-start | bytes 1572872 | tf_op jit(solution)/shard_map/ppermute | solution.py:248
  80.7 9.2 %collective-permute-start.20 = (bf16[8,64,256]{2,1,0:T(8,128)(2,1)}, bf16[8,64,256]{2,1,0:T(8,128)(2,1)}, u32[]{:S(2)}, u32[]{:S(2)}) collective-permute-start(bf16[8,64,256]{2,1,0:T(8,128)(2,1)} %slice.98), channel_id=1, source_target_pairs={{0,2},{1,3},{2,0},{3,1},{4,6},{5,7},{6,4},{7,5},{8,10},{9,11},{10,... | collective-permute-start | bytes 786440 | tf_op jit(solution)/shard_map/ppermute | solution.py:245
  83.2 8.3 %collective-permute-start.19 = (bf16[8,64,256]{2,1,0:T(8,128)(2,1)}, bf16[8,64,256]{2,1,0:T(8,128)(2,1)}, u32[]{:S(2)}, u32[]{:S(2)}) collective-permute-start(bf16[8,64,256]{2,1,0:T(8,128)(2,1)} %slice.97), channel_id=1, source_target_pairs={{0,4},{1,5},{2,6},{3,7},{4,0},{5,1},{6,2},{7,3},{8,12},{9,13},{10,... | collective-permute-start | bytes 786440 | tf_op jit(solution)/shard_map/ppermute | solution.py:245
  84.8 16.3 %collective-permute-start.22 = (bf16[2,512,128]{2,1,0:T(8,128)(2,1)}, bf16[2,512,128]{2,1,0:T(8,128)(2,1)S(1)}, u32[]{:S(2)}, u32[]{:S(2)}) collective-permute-start(bf16[2,512,128]{2,1,0:T(8,128)(2,1)} %fusion.2), channel_id=1, source_target_pairs={{0,16},{8,24},{16,0},{24,8},{1,17},{9,25},{17,1},{25,9},{2,18},{10... | collective-permute-start | bytes 786440 | tf_op jit(solution)/shard_map/ppermute | solution.py:248
  86.6 18.2 %collective-permute-start.23 = (bf16[1,64,16,128]{3,2,1,0:T(8,128)(2,1)S(1)}, bf16[1,64,16,128]{3,2,1,0:T(8,128)(2,1)S(1)}, u32[]{:S(2)}, u32[]{:S(2)}) collective-permute-start(bf16[1,64,16,128]{3,2,1,0:T(8,128)(2,1)S(1)} %get-tuple-element.134.refs_0_), channel_id=1, source_target_pairs={{0,2},{1,3},{2,0},{3,1},{4,6},{5,7},{6,4},{7,5},{8,10},{9,11},{10,... | collective-permute-start | bytes 786440 | tf_op jit(solution)/shard_map/ppermute | solution.py:245
  89.9 16.3 %collective-permute-start.24 = (bf16[1,64,16,128]{3,2,1,0:T(8,128)(2,1)S(1)}, bf16[1,64,16,128]{3,2,1,0:T(8,128)(2,1)S(1)}, u32[]{:S(2)}, u32[]{:S(2)}) collective-permute-start(bf16[1,64,16,128]{3,2,1,0:T(8,128)(2,1)S(1)} %get-tuple-element.134.refs_0_), channel_id=1, source_target_pairs={{0,4},{1,5},{2,6},{3,7},{4,0},{5,1},{6,2},{7,3},{8,12},{9,13},{10,... | collective-permute-start | bytes 786440 | tf_op jit(solution)/shard_map/ppermute | solution.py:245
  91.4 15.3 %collective-permute-start.25 = (bf16[1,64,16,128]{3,2,1,0:T(8,128)(2,1)S(1)}, bf16[1,64,16,128]{3,2,1,0:T(8,128)(2,1)S(1)}, u32[]{:S(2)}, u32[]{:S(2)}) collective-permute-start(bf16[1,64,16,128]{3,2,1,0:T(8,128)(2,1)S(1)} %get-tuple-element.134.refs_0_), channel_id=1, source_target_pairs={{0,6},{1,7},{2,4},{3,5},{4,2},{5,3},{6,0},{7,1},{8,14},{9,15},{10,... | collective-permute-start | bytes 786440 | tf_op jit(solution)/shard_map/ppermute | solution.py:245
  92.9 1.0 copy-start.1
  100.0 10.5 %collective-permute-start.26 = (bf16[1,2,512,128]{3,2,1,0:T(8,128)(2,1)S(1)}, bf16[1,2,512,128]{3,2,1,0:T(8,128)(2,1)S(1)}, u32[]{:S(2)}, u32[]{:S(2)}) collective-permute-start(bf16[1,2,512,128]{3,2,1,0:T(8,128)(2,1)S(1)} %get-tuple-element.137), channel_id=1, source_target_pairs={{0,8},{8,0},{16,24},{24,16},{1,9},{9,1},{17,25},{25,17},{2,10},{10... | collective-permute-start | bytes 786440 | tf_op jit(solution)/shard_map/ppermute | solution.py:248
  101.1 9.5 %collective-permute-start.27 = (bf16[2,512,128]{2,1,0:T(8,128)(2,1)S(1)}, bf16[2,512,128]{2,1,0:T(8,128)(2,1)S(1)}, u32[]{:S(2)}, u32[]{:S(2)}) collective-permute-start(bf16[2,512,128]{2,1,0:T(8,128)(2,1)S(1)} %fusion.1), channel_id=1, source_target_pairs={{0,16},{8,24},{16,0},{24,8},{1,17},{9,25},{17,1},{25,9},{2,18},{10... | collective-permute-start | bytes 786440 | tf_op jit(solution)/shard_map/ppermute | solution.py:248
  104.8 9.1 %collective-permute-start.28 = (bf16[1,64,16,128]{3,2,1,0:T(8,128)(2,1)S(1)}, bf16[1,64,16,128]{3,2,1,0:T(8,128)(2,1)S(1)}, u32[]{:S(2)}, u32[]{:S(2)}) collective-permute-start(bf16[1,64,16,128]{3,2,1,0:T(8,128)(2,1)S(1)} %get-tuple-element.142.refs_0_), channel_id=1, source_target_pairs={{0,2},{1,3},{2,0},{3,1},{4,6},{5,7},{6,4},{7,5},{8,10},{9,11},{10,... | collective-permute-start | bytes 786440 | tf_op jit(solution)/shard_map/ppermute | solution.py:245
  106.2 10.2 %collective-permute-start.29 = (bf16[1,64,16,128]{3,2,1,0:T(8,128)(2,1)S(1)}, bf16[1,64,16,128]{3,2,1,0:T(8,128)(2,1)S(1)}, u32[]{:S(2)}, u32[]{:S(2)}) collective-permute-start(bf16[1,64,16,128]{3,2,1,0:T(8,128)(2,1)S(1)} %get-tuple-element.142.refs_0_), channel_id=1, source_target_pairs={{0,4},{1,5},{2,6},{3,7},{4,0},{5,1},{6,2},{7,3},{8,12},{9,13},{10,... | collective-permute-start | bytes 786440 | tf_op jit(solution)/shard_map/ppermute | solution.py:245
  106.8 11.0 %collective-permute-start.30 = (bf16[1,64,16,128]{3,2,1,0:T(8,128)(2,1)S(1)}, bf16[1,64,16,128]{3,2,1,0:T(8,128)(2,1)S(1)}, u32[]{:S(2)}, u32[]{:S(2)}) collective-permute-start(bf16[1,64,16,128]{3,2,1,0:T(8,128)(2,1)S(1)} %get-tuple-element.142.refs_0_), channel_id=1, source_target_pairs={{0,6},{1,7},{2,4},{3,5},{4,2},{5,3},{6,0},{7,1},{8,14},{9,15},{10,... | collective-permute-start | bytes 786440 | tf_op jit(solution)/shard_map/ppermute | solution.py:245
  111.5 10.7 %collective-permute-start.31 = (bf16[1,64,16,128]{3,2,1,0:T(8,128)(2,1)S(1)}, bf16[1,64,16,128]{3,2,1,0:T(8,128)(2,1)S(1)}, u32[]{:S(2)}, u32[]{:S(2)}) collective-permute-start(bf16[1,64,16,128]{3,2,1,0:T(8,128)(2,1)S(1)} %get-tuple-element.145.refs_0_), channel_id=1, source_target_pairs={{0,2},{1,3},{2,0},{3,1},{4,6},{5,7},{6,4},{7,5},{8,10},{9,11},{10,... | collective-permute-start | bytes 786440 | tf_op jit(solution)/shard_map/ppermute | solution.py:245
  113.5 9.2 %collective-permute-start.32 = (bf16[1,64,16,128]{3,2,1,0:T(8,128)(2,1)S(1)}, bf16[1,64,16,128]{3,2,1,0:T(8,128)(2,1)S(1)}, u32[]{:S(2)}, u32[]{:S(2)}) collective-permute-start(bf16[1,64,16,128]{3,2,1,0:T(8,128)(2,1)S(1)} %get-tuple-element.145.refs_0_), channel_id=1, source_target_pairs={{0,4},{1,5},{2,6},{3,7},{4,0},{5,1},{6,2},{7,3},{8,12},{9,13},{10,... | collective-permute-start | bytes 786440 | tf_op jit(solution)/shard_map/ppermute | solution.py:245
  113.9 8.8 %collective-permute-start.33 = (bf16[1,64,16,128]{3,2,1,0:T(8,128)(2,1)S(1)}, bf16[1,64,16,128]{3,2,1,0:T(8,128)(2,1)S(1)}, u32[]{:S(2)}, u32[]{:S(2)}) collective-permute-start(bf16[1,64,16,128]{3,2,1,0:T(8,128)(2,1)S(1)} %get-tuple-element.145.refs_0_), channel_id=1, source_target_pairs={{0,6},{1,7},{2,4},{3,5},{4,2},{5,3},{6,0},{7,1},{8,14},{9,15},{10,... | collective-permute-start | bytes 786440 | tf_op jit(solution)/shard_map/ppermute | solution.py:245
  116.3 8.5 %collective-permute-start.34 = (bf16[1,2,512,128]{3,2,1,0:T(8,128)(2,1)S(1)}, bf16[1,2,512,128]{3,2,1,0:T(8,128)(2,1)S(1)}, u32[]{:S(2)}, u32[]{:S(2)}) collective-permute-start(bf16[1,2,512,128]{3,2,1,0:T(8,128)(2,1)S(1)} %get-tuple-element.149), channel_id=1, source_target_pairs={{0,8},{8,0},{16,24},{24,16},{1,9},{9,1},{17,25},{25,17},{2,10},{10... | collective-permute-start | bytes 786440 | tf_op jit(solution)/shard_map/ppermute | solution.py:248
  117.8 10.1 %collective-permute-start.35 = (bf16[2,512,128]{2,1,0:T(8,128)(2,1)S(1)}, bf16[2,512,128]{2,1,0:T(8,128)(2,1)S(1)}, u32[]{:S(2)}, u32[]{:S(2)}) collective-permute-start(bf16[2,512,128]{2,1,0:T(8,128)(2,1)S(1)} %fusion), channel_id=1, source_target_pairs={{0,16},{8,24},{16,0},{24,8},{1,17},{9,25},{17,1},{25,9},{2,18},{10... | collective-permute-start | bytes 786440 | tf_op jit(solution)/shard_map/ppermute | solution.py:248
  124.8 7.5 %copy-start.5 = (bf16[32,64]{1,0:T(8,128)(2,1)S(1)}, bf16[32,64]{1,0:T(8,128)(2,1)}, u32[]{:S(2)}) copy-start(bf16[32,64]{1,0:T(8,128)(2,1)} %param.9) | copy-start | bytes 12292
  128.7 3.6 %collective-permute-start.36 = (bf16[512,512]{1,0:T(8,128)(2,1)S(1)}, bf16[512,512]{1,0:T(8,128)(2,1)S(1)}, u32[]{:S(2)}, u32[]{:S(2)}) collective-permute-start(bf16[512,512]{1,0:T(8,128)(2,1)S(1)} %get-tuple-element.151), channel_id=1, source_target_pairs={{0,1},{1,0},{2,3},{3,2},{4,5},{5,4},{6,7},{7,6},{8,9},{9,8},{10,11... | collective-permute-start | bytes 1572872 | tf_op jit(solution)/shard_map/ppermute | solution.py:245
  128.8 9.2 %collective-permute-start.37 = (bf16[1,64,16,128]{3,2,1,0:T(8,128)(2,1)S(1)}, bf16[1,64,16,128]{3,2,1,0:T(8,128)(2,1)S(1)}, u32[]{:S(2)}, u32[]{:S(2)}) collective-permute-start(bf16[1,64,16,128]{3,2,1,0:T(8,128)(2,1)S(1)} %get-tuple-element.154.refs_0_), channel_id=1, source_target_pairs={{0,2},{1,3},{2,0},{3,1},{4,6},{5,7},{6,4},{7,5},{8,10},{9,11},{10,... | collective-permute-start | bytes 786440 | tf_op jit(solution)/shard_map/ppermute | solution.py:245
  130.6 14.0 %collective-permute-start.38 = (bf16[1,64,16,128]{3,2,1,0:T(8,128)(2,1)S(1)}, bf16[1,64,16,128]{3,2,1,0:T(8,128)(2,1)S(1)}, u32[]{:S(2)}, u32[]{:S(2)}) collective-permute-start(bf16[1,64,16,128]{3,2,1,0:T(8,128)(2,1)S(1)} %get-tuple-element.154.refs_0_), channel_id=1, source_target_pairs={{0,4},{1,5},{2,6},{3,7},{4,0},{5,1},{6,2},{7,3},{8,12},{9,13},{10,... | collective-permute-start | bytes 786440 | tf_op jit(solution)/shard_map/ppermute | solution.py:245
  130.6 13.9 %collective-permute-start.39 = (bf16[1,64,16,128]{3,2,1,0:T(8,128)(2,1)S(1)}, bf16[1,64,16,128]{3,2,1,0:T(8,128)(2,1)S(1)}, u32[]{:S(2)}, u32[]{:S(2)}) collective-permute-start(bf16[1,64,16,128]{3,2,1,0:T(8,128)(2,1)S(1)} %get-tuple-element.154.refs_0_), channel_id=1, source_target_pairs={{0,6},{1,7},{2,4},{3,5},{4,2},{5,3},{6,0},{7,1},{8,14},{9,15},{10,... | collective-permute-start | bytes 786440 | tf_op jit(solution)/shard_map/ppermute | solution.py:245
  132.4 14.6 %collective-permute-start.40 = (bf16[32,64]{1,0:T(8,128)(2,1)S(1)}, bf16[32,64]{1,0:T(8,128)(2,1)S(1)}, u32[]{:S(2)}, u32[]{:S(2)}) collective-permute-start(bf16[32,64]{1,0:T(8,128)(2,1)S(1)} %copy-done.5), channel_id=1, source_target_pairs={{0,1},{1,0},{2,3},{3,2},{4,5},{5,4},{6,7},{7,6},{8,9},{9,8},{10,11... | collective-permute-start | bytes 12296 | tf_op jit(solution)/shard_map/ppermute | solution.py:245
  147.2 1.2 collective-permute-start.41
  148.9 3.9 %collective-permute-start.42 = (f32[32,64]{0,1:T(8,128)S(1)}, f32[32,64]{0,1:T(8,128)S(1)}, u32[]{:S(2)}, u32[]{:S(2)}) collective-permute-start(f32[32,64]{0,1:T(8,128)S(1)} %fusion.8), channel_id=1, source_target_pairs={{0,8},{8,0},{16,24},{24,16},{1,9},{9,1},{17,25},{25,17},{2,10},{10... | collective-permute-start | bytes 24584 | tf_op jit(solution)/shard_map/ppermute | solution.py:248
  152.9 4.8 %collective-permute-start.43 = (f32[32,64]{0,1:T(8,128)S(1)}, f32[32,64]{0,1:T(8,128)S(1)}, u32[]{:S(2)}, u32[]{:S(2)}) collective-permute-start(f32[32,64]{0,1:T(8,128)S(1)} %add.113), channel_id=1, source_target_pairs={{0,16},{8,24},{16,0},{24,8},{1,17},{9,25},{17,1},{25,9},{2,18},{10... | collective-permute-start | bytes 24584 | tf_op jit(solution)/shard_map/ppermute | solution.py:248
  (3 other events, 2.7 us)

commit v3 on v2

--- a/solution.py
+++ b/solution.py
@@ -10,10 +10,10 @@
 CHUNKS = 4
 GROUPS = ((0,), (1,), (2,), (3,))
 ORDER = (
-    "W0", "M0", "W1", "A1", "P0", "M1", "W2", "A2", "P1", "M2", "C0", "W3", "A3", "M3",
-    "P2", "C1", "F0", "P3", "C2", "F1", "F2", "C3", "R", "F3",
+    "W0", "M0", "W1", "A1", "P0", "M1", "W2", "A2", "P1", "M2", "C0", "W3", "A3", "M3", "P2", "C1", "F0", "P3", "C2", "F1", "F2", "C3", "R", "F3",
 )
 LIMIT = 50 * 2**20
+WEIGHTS = {"M": (2000000000, 2000000000, 2000000000, 2000000000), "C": (1000000, 1000000, 1000000, 1000000), "F": (100000000, 100000000, 100000000, 2000000000), "T": 1000000}
 NT = (((1,), (1,)), ((), ()))
 HBM = pl.BlockSpec(memory_space=pltpu.HBM)
 VMEM = pl.BlockSpec(memory_space=pltpu.VMEM)
@@ -59,7 +59,7 @@
         far[c] = blocks[2].astype(far.dtype)
 
 
-def partial_products(info, left, partner, cols, cuts, nears, *pieces):
+def partial_products(weight, info, left, partner, cols, cuts, nears, *pieces):
     sectors, rows, states = left.shape
 
     block = (2, rows, cols)
@@ -79,7 +79,7 @@
         * nears
         + [jax.ShapeDtypeStruct(block, jnp.float32)] * 2,
         compiler_params=PARAMS,
-        cost_estimate=cost(16 * rows * sectors * states * cols),
+        cost_estimate=cost(weight),
         name="partial_products",
     )(info, left, partner, *pieces)
 
@@ -107,7 +107,7 @@
         copy.wait()
 
 
-def combine(chunk, group, core, mine, near, far, width, pair_cols, held):
+def combine(weight, chunk, group, core, mine, near, far, width, pair_cols, held):
     _, rows, cols = mine.shape
     bf16 = jnp.bfloat16
     block = (width, 2 * rows // width, cols)
@@ -124,7 +124,7 @@
         + [pltpu.VMEM(block, bf16), pltpu.SemaphoreType.DMA((3,))],
         input_output_aliases={4 + i: i for i in range(len(held))},
         compiler_params=PARAMS,
-        cost_estimate=cost(8 * rows * cols),
+        cost_estimate=cost(weight),
         name="combine",
     )(core, mine, near, far, *held)
 
@@ -178,7 +178,7 @@
     fock[...] = acc
 
 
-def fock_terms(first, base, slab, diagonal, *pieces):
+def fock_terms(weight, first, base, slab, diagonal, *pieces):
     width, orbitals, _ = slab.shape
     chunks, _, _, cols = pieces[0].shape
     return pl.pallas_call(
@@ -195,7 +195,7 @@
             pltpu.SemaphoreType.DMA((5,)),
         ],
         compiler_params=PARAMS,
-        cost_estimate=cost(2 * (orbitals + 16) * width * width * chunks * cols),
+        cost_estimate=cost(weight),
         name="fock_terms",
     )(base, slab, diagonal, *pieces)
 
@@ -206,7 +206,7 @@
     o[:, size:] = jnp.swapaxes(b[...].astype(jnp.float32), 0, 1).astype(jnp.bfloat16)
 
 
-def turn(core, slab, received, cols):
+def turn(weight, core, slab, received, cols):
     orbitals, width, total = received.shape
     steps = total // cols
     return pl.pallas_call(
@@ -222,7 +222,7 @@
         ),
         out_shape=jax.ShapeDtypeStruct((width, 2 * orbitals, total), jnp.bfloat16),
         compiler_params=PARAMS,
-        cost_estimate=cost(orbitals * width * total),
+        cost_estimate=cost(weight),
         name="turn",
     )(core, slab, received)
 
@@ -265,7 +265,7 @@
 
     given = lax.dynamic_slice(after(slab, sent), (0, 0, (1 - core) * rows), (general, width, rows))
     received, *waiting[1:] = lax.optimization_barrier((across(given, 1), *waiting[1:]))
-    integrals = turn(number(core), slab, received, cols)
+    integrals = turn(WEIGHTS["T"], number(core), slab, received, cols)
 
     column_ids = z * pair_cols + core * rows + jnp.arange(rows, dtype=jnp.int32)
     diagonal = jnp.broadcast_to(
@@ -279,14 +279,14 @@
         if len(parts) == 4:
             cuts.append((4, (every,), half, 3))
         info = jnp.concatenate([number(chip ^ z), block_sizes])
-        return partial_products(info, amps_left, partner_left, cols, cuts, nears, amps_right, *parts)
+        return partial_products(WEIGHTS["M"][chunk], info, amps_left, partner_left, cols, cuts, nears, amps_right, *parts)
 
     sums, terms, gathered = [None] * CHUNKS, [], {}
 
     def contract(group):
         at = slice(group[0] * cols, (group[-1] + 1) * cols)
         marks = after(diagonal[:, at], state["last"])
-        terms.append(fock_terms(group[0], number(chip), integrals, marks, *gathered[group]))
+        terms.append(fock_terms(WEIGHTS["F"][group[0]], group[0], number(chip), integrals, marks, *gathered[group]))
         state["last"] = terms[-1][0]
 
     if 0 in pieces:
@@ -327,7 +327,7 @@
         group = [g for g in GROUPS if chunk in g][0]
         held = state["held"] if chunk > group[0] else state["held"][:2]
         state["held"] = combine(
-            chunk, group, number(core), after(own, state["last"]), near, far, width, pair_cols, held
+            WEIGHTS["C"][chunk], chunk, group, number(core), after(own, state["last"]), near, far, width, pair_cols, held
         )
         turned = state["held"][2]
         if chunk == group[-1]:

time: 159 us -> 155 us (0.975)
  waiting for transfers between devices: 55.1 us -> 50.3 us
  starting transfers between devices: 51.8 us -> 56.3 us
  local copies, waits for them, and re-layouts: 10.6 us -> 6.92 us
    ppermute x11, waiting for transfers between devices: 11.7 us -> 6.35 us  [along(): return lax.ppermute(value, 'sec', [(i, i ^ flip) for i in range(secs)])]
    ppermute x11, starting transfers between devices: 17 us -> 22.1 us  [along(): return lax.ppermute(value, 'sec', [(i, i ^ flip) for i in range(secs)])]
    unnamed x15, local copies, waits for them, and re-layouts: 4.46 us -> 0.71 us
  transfers between devices with their start and end apart: 44 -> 44, of which waited for: 19 -> 20; matrix products, arithmetic and copies ran while one was open for 2% -> 2% of each run, Pallas kernels for 24% -> 24%
where the time goes in v3:
time: 155 us; the launch traced here: 154 us
  starting transfers between devices  56.3 us (36%)
  waiting for transfers between devices  50.3 us (32%)
  Pallas kernels  38.4 us (25%)
  local copies, waits for them, and re-layouts  6.92 us (4%)
    ppermute x33, waiting for transfers between devices, across(): return lax.ppermute(value, 'gen', [(i, i ^ flip) for i in range(gens)])  43.9 us
    ppermute x33, starting transfers between devices, across(): return lax.ppermute(value, 'gen', [(i, i ^ flip) for i in range(gens)])  34.3 us
    ppermute x11, starting transfers between devices, along(): return lax.ppermute(value, 'sec', [(i, i ^ flip) for i in range(secs)])  22.1 us
    pallas_call x4, Pallas kernels, partial_products(): pl.pallas_call(functools.partial(partial_kernel, cuts, nears), in_specs=[...  20.7 us
    pallas_call x4, Pallas kernels, fock_terms(): pl.pallas_call(functools.partial(fock_kernel, first), in_specs=[SMEM, HBM...  8.47 us
    ppermute x11, waiting for transfers between devices, along(): return lax.ppermute(value, 'sec', [(i, i ^ flip) for i in range(secs)])  6.35 us
    pallas_call x1, Pallas kernels, turn(): pl.pallas_call(turn_kernel, grid_spec=pltpu.PrefetchScalarGridSpec(num_sc...  5.21 us
    pallas_call x4, Pallas kernels, combine(): pl.pallas_call(functools.partial(combine_kernel, chunk, group.index(chunk...  3.23 us
  transfers between devices with their start and end apart: 44, of which 20 were waited for; matrix products, arithmetic and copies ran while one was open for 2% of the time, Pallas kernels for 24%

profile of v3, /device:TPU:0, one launch (start us, length us, event | category | flops | bytes accessed | tf_op | source)
XLA Modules:
  0.0 154.5 jit_solution(10555530582845707995)
XLA Ops:
  1.8 2.0 %constant_dynamic-slice_fusion = bf16[32,64,512]{2,1,0:T(8,128)(2,1)S(1)} fusion(bf16[32,64,1024]{2,1,0:T(8,128)(2,1)} %a.1, s32[]{:T(128)S(6)} %select_n.79), kind=kLoop, calls=%fused_computation.35 | loop fusion | bytes 4194308 | tf_op jit(solution)/shard_map/dynamic_slice | solution.py:266
  4.3 2.9 %collective-permute-start.3 = (bf16[8,128,256]{2,1,0:T(8,128)(2,1)S(1)}, bf16[8,128,256]{2,1,0:T(8,128)(2,1)S(1)}, u32[]{:S(2)}, u32[]{:S(2)}) collective-permute-start(bf16[8,128,256]{2,1,0:T(8,128)(2,1)S(1)} %slice.85), channel_id=1, source_target_pairs={{0,4},{1,5},{2,6},{3,7},{4,0},{5,1},{6,2},{7,3},{8,12},{9,13},{10,... | collective-permute-start | bytes 1572872 | tf_op jit(solution)/shard_map/ppermute | solution.py:245
  7.3 1.5 collective-permute-start.2
  10.2 5.2 %turn.1.slab = bf16[64,64,512]{2,1,0:T(8,128)(2,1)} custom-call(s32[1]{0:T(128)} %bitcast.core, bf16[32,64,1024]{2,1,0:T(8,128)(2,1)} %a.1, bf16[32,64,512]{2,1,0:T(8,128)(2,1)S(1)} %collective-permute-done.1.b), custom_call_target="tpu_custom_call" | custom-call | flops 1000000 | bytes 1 | tf_op jit(solution)/shard_map/turn/pallas_call | solution.py:212
  15.4 4.0 %collective-permute-done.3.refs_2_ = bf16[8,128,256]{2,1,0:T(8,128)(2,1)S(1)} collective-permute-done((bf16[8,128,256]{2,1,0:T(8,128)(2,1)S(1)}, bf16[8,128,256]{2,1,0:T(8,128)(2,1)S(1)}, u32[]{:S(2)}, u32[]{:S(2)}) %collective-permute-start.3) | collective-permute-done | bytes 524320 | tf_op jit(solution)/shard_map/ppermute | solution.py:245
  19.4 1.8 %collective-permute-start.6 = (bf16[8,64,256]{2,1,0:T(8,128)(2,1)S(1)}, bf16[8,64,256]{2,1,0:T(8,128)(2,1)S(1)}, u32[]{:S(2)}, u32[]{:S(2)}) collective-permute-start(bf16[8,64,256]{2,1,0:T(8,128)(2,1)S(1)} %slice.90), channel_id=1, source_target_pairs={{0,2},{1,3},{2,0},{3,1},{4,6},{5,7},{6,4},{7,5},{8,10},{9,11},{10,... | collective-permute-start | bytes 786440 | tf_op jit(solution)/shard_map/ppermute | solution.py:245
  21.2 1.6 %collective-permute-start.5 = (bf16[8,64,256]{2,1,0:T(8,128)(2,1)S(1)}, bf16[8,64,256]{2,1,0:T(8,128)(2,1)S(1)}, u32[]{:S(2)}, u32[]{:S(2)}) collective-permute-start(bf16[8,64,256]{2,1,0:T(8,128)(2,1)S(1)} %slice.89), channel_id=1, source_target_pairs={{0,4},{1,5},{2,6},{3,7},{4,0},{5,1},{6,2},{7,3},{8,12},{9,13},{10,... | collective-permute-start | bytes 786440 | tf_op jit(solution)/shard_map/ppermute | solution.py:245
  24.6 4.2 %collective-permute-done.6.refs_4_ = bf16[8,64,256]{2,1,0:T(8,128)(2,1)S(1)} collective-permute-done((bf16[8,64,256]{2,1,0:T(8,128)(2,1)S(1)}, bf16[8,64,256]{2,1,0:T(8,128)(2,1)S(1)}, u32[]{:S(2)}, u32[]{:S(2)}) %collective-permute-start.6) | collective-permute-done | bytes 262176 | tf_op jit(solution)/shard_map/ppermute | solution.py:245
  28.7 1.8 %collective-permute-done.5.refs_3_ = bf16[8,64,256]{2,1,0:T(8,128)(2,1)S(1)} collective-permute-done((bf16[8,64,256]{2,1,0:T(8,128)(2,1)S(1)}, bf16[8,64,256]{2,1,0:T(8,128)(2,1)S(1)}, u32[]{:S(2)}, u32[]{:S(2)}) %collective-permute-start.5) | collective-permute-done | bytes 262176 | tf_op jit(solution)/shard_map/ppermute | solution.py:245
  30.6 5.0 %partial_products.4 = (bf16[2,2,512,128]{3,2,1,0:T(8,128)(2,1)S(1)}, f32[2,512,128]{2,1,0:T(8,128)S(1)}, f32[2,512,128]{2,1,0:T(8,128)S(1)}) custom-call(s32[9]{0:T(128)S(1)} %pad_add_fusion.info, bf16[8,512,256]{2,1,0:T(8,128)(2,1)} %left.7, bf16[8,512,256]{2,1,0:T(8,128)(2,1)} %collective-permute-done.partner, bf16[8,512,256]{2,1,0:T(8,128)(2,1)} %refs_0_.7, ...), custom_call_target="tpu_custom_call" | custom-call | flops 2000000000 | bytes 1 | tf_op jit(solution)/shard_map/partial_products/pallas_call | solution.py:66
  35.5 1.6 %collective-permute-start.11 = (bf16[2,2,512,128]{3,2,1,0:T(8,128)(2,1)S(1)}, bf16[2,2,512,128]{3,2,1,0:T(8,128)(2,1)S(1)}, u32[]{:S(2)}, u32[]{:S(2)}) collective-permute-start(bf16[2,2,512,128]{3,2,1,0:T(8,128)(2,1)S(1)} %get-tuple-element.100), channel_id=1, source_target_pairs={{0,8},{8,0},{16,24},{24,16},{1,9},{9,1},{17,25},{25,17},{2,10},{10... | collective-permute-start | bytes 1572872 | tf_op jit(solution)/shard_map/ppermute | solution.py:248
  37.2 2.6 %collective-permute-done.7.refs_2_ = bf16[8,128,256]{2,1,0:T(8,128)(2,1)S(1)} collective-permute-done((bf16[8,128,256]{2,1,0:T(8,128)(2,1)S(1)}, bf16[8,128,256]{2,1,0:T(8,128)(2,1)S(1)}, u32[]{:S(2)}, u32[]{:S(2)}) %collective-permute-start.7) | collective-permute-done | bytes 524320 | tf_op jit(solution)/shard_map/ppermute | solution.py:245
  39.7 1.2 collective-permute-start.10
  44.0 5.1 %collective-permute-done.10.refs_4_ = bf16[8,64,256]{2,1,0:T(8,128)(2,1)S(1)} collective-permute-done((bf16[8,64,256]{2,1,0:T(8,128)(2,1)S(1)}, bf16[8,64,256]{2,1,0:T(8,128)(2,1)S(1)}, u32[]{:S(2)}, u32[]{:S(2)}) %collective-permute-start.10) | collective-permute-done | bytes 262176 | tf_op jit(solution)/shard_map/ppermute | solution.py:245
  49.1 1.2 collective-permute-done.9.refs_3_
  50.3 5.0 %partial_products.5 = (bf16[2,2,512,128]{3,2,1,0:T(8,128)(2,1)S(1)}, f32[2,512,128]{2,1,0:T(8,128)S(1)}, f32[2,512,128]{2,1,0:T(8,128)S(1)}) custom-call(s32[9]{0:T(128)S(1)} %pad_add_fusion.info, bf16[8,512,256]{2,1,0:T(8,128)(2,1)} %left.7, bf16[8,512,256]{2,1,0:T(8,128)(2,1)} %collective-permute-done.partner, bf16[8,512,256]{2,1,0:T(8,128)(2,1)} %refs_0_.7, ...), custom_call_target="tpu_custom_call" | custom-call | flops 2000000000 | bytes 1 | tf_op jit(solution)/shard_map/partial_products/pallas_call | solution.py:66
  55.3 1.6 %collective-permute-start.16 = (bf16[2,2,512,128]{3,2,1,0:T(8,128)(2,1)S(1)}, bf16[2,2,512,128]{3,2,1,0:T(8,128)(2,1)S(1)}, u32[]{:S(2)}, u32[]{:S(2)}) collective-permute-start(bf16[2,2,512,128]{3,2,1,0:T(8,128)(2,1)S(1)} %get-tuple-element.111), channel_id=1, source_target_pairs={{0,8},{8,0},{16,24},{24,16},{1,9},{9,1},{17,25},{25,17},{2,10},{10... | collective-permute-start | bytes 1572872 | tf_op jit(solution)/shard_map/ppermute | solution.py:248
  56.9 1.2 collective-permute-done.12.refs_2_
  59.2 1.7 %collective-permute-start.14 = (bf16[8,64,256]{2,1,0:T(8,128)(2,1)S(1)}, bf16[8,64,256]{2,1,0:T(8,128)(2,1)S(1)}, u32[]{:S(2)}, u32[]{:S(2)}) collective-permute-start(bf16[8,64,256]{2,1,0:T(8,128)(2,1)S(1)} %slice.94), channel_id=1, source_target_pairs={{0,4},{1,5},{2,6},{3,7},{4,0},{5,1},{6,2},{7,3},{8,12},{9,13},{10,... | collective-permute-start | bytes 786440 | tf_op jit(solution)/shard_map/ppermute | solution.py:245
  62.4 5.1 %collective-permute-done.15.refs_4_ = bf16[8,64,256]{2,1,0:T(8,128)(2,1)S(1)} collective-permute-done((bf16[8,64,256]{2,1,0:T(8,128)(2,1)S(1)}, bf16[8,64,256]{2,1,0:T(8,128)(2,1)S(1)}, u32[]{:S(2)}, u32[]{:S(2)}) %collective-permute-start.15) | collective-permute-done | bytes 262176 | tf_op jit(solution)/shard_map/ppermute | solution.py:245
  67.5 2.6 %collective-permute-start.17 = (bf16[2,512,128]{2,1,0:T(8,128)(2,1)S(1)}, bf16[2,512,128]{2,1,0:T(8,128)(2,1)S(1)}, u32[]{:S(2)}, u32[]{:S(2)}) collective-permute-start(bf16[2,512,128]{2,1,0:T(8,128)(2,1)S(1)} %fusion.3), channel_id=1, source_target_pairs={{0,16},{8,24},{16,0},{24,8},{1,17},{9,25},{17,1},{25,9},{2,18},{10... | collective-permute-start | bytes 786440 | tf_op jit(solution)/shard_map/ppermute | solution.py:248
  70.8 5.8 %partial_products.6 = (bf16[2,2,512,128]{3,2,1,0:T(8,128)(2,1)}, f32[2,512,128]{2,1,0:T(8,128)S(1)}, f32[2,512,128]{2,1,0:T(8,128)S(1)}) custom-call(s32[9]{0:T(128)S(1)} %pad_add_fusion.info, bf16[8,512,256]{2,1,0:T(8,128)(2,1)} %left.7, bf16[8,512,256]{2,1,0:T(8,128)(2,1)} %collective-permute-done.partner, bf16[8,512,256]{2,1,0:T(8,128)(2,1)} %refs_0_.7, ...), custom_call_target="tpu_custom_call" | custom-call | flops 2000000000 | bytes 1 | tf_op jit(solution)/shard_map/partial_products/pallas_call | solution.py:66
  76.7 1.6 %collective-permute-start.21 = (bf16[2,2,512,128]{3,2,1,0:T(8,128)(2,1)}, bf16[2,2,512,128]{3,2,1,0:T(8,128)(2,1)S(1)}, u32[]{:S(2)}, u32[]{:S(2)}) collective-permute-start(bf16[2,2,512,128]{3,2,1,0:T(8,128)(2,1)} %get-tuple-element.129), channel_id=1, source_target_pairs={{0,8},{8,0},{16,24},{24,16},{1,9},{9,1},{17,25},{25,17},{2,10},{10... | collective-permute-start | bytes 1572872 | tf_op jit(solution)/shard_map/ppermute | solution.py:248
  81.6 1.6 %collective-permute-start.19 = (bf16[8,64,256]{2,1,0:T(8,128)(2,1)}, bf16[8,64,256]{2,1,0:T(8,128)(2,1)}, u32[]{:S(2)}, u32[]{:S(2)}) collective-permute-start(bf16[8,64,256]{2,1,0:T(8,128)(2,1)} %slice.97), channel_id=1, source_target_pairs={{0,4},{1,5},{2,6},{3,7},{4,0},{5,1},{6,2},{7,3},{8,12},{9,13},{10,... | collective-permute-start | bytes 786440 | tf_op jit(solution)/shard_map/ppermute | solution.py:245
  83.2 1.7 %collective-permute-start.22 = (bf16[2,512,128]{2,1,0:T(8,128)(2,1)}, bf16[2,512,128]{2,1,0:T(8,128)(2,1)S(1)}, u32[]{:S(2)}, u32[]{:S(2)}) collective-permute-start(bf16[2,512,128]{2,1,0:T(8,128)(2,1)} %fusion.2), channel_id=1, source_target_pairs={{0,16},{8,24},{16,0},{24,8},{1,17},{9,25},{17,1},{25,9},{2,18},{10... | collective-permute-start | bytes 786440 | tf_op jit(solution)/shard_map/ppermute | solution.py:248
  85.4 3.3 %collective-permute-done.20.refs_4_ = bf16[8,64,256]{2,1,0:T(8,128)(2,1)} collective-permute-done((bf16[8,64,256]{2,1,0:T(8,128)(2,1)}, bf16[8,64,256]{2,1,0:T(8,128)(2,1)}, u32[]{:S(2)}, u32[]{:S(2)}) %collective-permute-start.20) | collective-permute-done | bytes 262176 | tf_op jit(solution)/shard_map/ppermute | solution.py:245
  89.3 1.7 %collective-permute-start.25 = (bf16[1,64,16,128]{3,2,1,0:T(8,128)(2,1)S(1)}, bf16[1,64,16,128]{3,2,1,0:T(8,128)(2,1)S(1)}, u32[]{:S(2)}, u32[]{:S(2)}) collective-permute-start(bf16[1,64,16,128]{3,2,1,0:T(8,128)(2,1)S(1)} %get-tuple-element.134.refs_0_), channel_id=1, source_target_pairs={{0,6},{1,7},{2,4},{3,5},{4,2},{5,3},{6,0},{7,1},{8,14},{9,15},{10,... | collective-permute-start | bytes 786440 | tf_op jit(solution)/shard_map/ppermute | solution.py:245
  91.0 5.0 %partial_products.7 = (bf16[1,2,512,128]{3,2,1,0:T(8,128)(2,1)S(1)}, bf16[1,2,512,128]{3,2,1,0:T(8,128)(2,1)S(1)}, f32[2,512,128]{2,1,0:T(8,128)S(1)}, f32[2,512,128]{2,1,0:T(8,128)S(1)}) custom-call(s32[9]{0:T(128)S(1)} %pad_add_fusion.info, bf16[8,512,256]{2,1,0:T(8,128)(2,1)} %left.7, bf16[8,512,256]{2,1,0:T(8,128)(2,1)} %collective-permute-done.partner, ...), custom_call_target="tpu_custom_call" | custom-call | flops 2000000000 | bytes 1 | tf_op jit(solution)/shard_map/partial_products/pallas_call | solution.py:66
  97.3 2.7 %collective-permute-start.27 = (bf16[2,512,128]{2,1,0:T(8,128)(2,1)S(1)}, bf16[2,512,128]{2,1,0:T(8,128)(2,1)S(1)}, u32[]{:S(2)}, u32[]{:S(2)}) collective-permute-start(bf16[2,512,128]{2,1,0:T(8,128)(2,1)S(1)} %fusion.1), channel_id=1, source_target_pairs={{0,16},{8,24},{16,0},{24,8},{1,17},{9,25},{17,1},{25,9},{2,18},{10... | collective-permute-start | bytes 786440 | tf_op jit(solution)/shard_map/ppermute | solution.py:248
  100.7 1.3 collective-permute-start.28
  102.7 1.7 %collective-permute-start.30 = (bf16[1,64,16,128]{3,2,1,0:T(8,128)(2,1)S(1)}, bf16[1,64,16,128]{3,2,1,0:T(8,128)(2,1)S(1)}, u32[]{:S(2)}, u32[]{:S(2)}) collective-permute-start(bf16[1,64,16,128]{3,2,1,0:T(8,128)(2,1)S(1)} %get-tuple-element.142.refs_0_), channel_id=1, source_target_pairs={{0,6},{1,7},{2,4},{3,5},{4,2},{5,3},{6,0},{7,1},{8,14},{9,15},{10,... | collective-permute-start | bytes 786440 | tf_op jit(solution)/shard_map/ppermute | solution.py:245
  104.4 2.2 %fock_terms.4 = (f32[64,64]{1,0:T(8,128)S(1)}, f32[64,64]{1,0:T(8,128)S(1)}) custom-call(s32[1]{0:T(128)} %bitcast.4.base, bf16[64,64,512]{2,1,0:T(8,128)(2,1)} %turn.1.slab, bf16[16,128]{1,0:T(8,128)(2,1)S(1)} %broadcast_in_dim.18.diagonal, bf16[1,64,16,128]{3,2,1,0:T(8,128)(2,1)S(1)} %get-tuple-element.134.refs_0_, ...), custom_call_target="tpu_custom_call" | custom-call | flops 100000000 | bytes 1 | tf_op jit(solution)/shard_map/fock_terms/pallas_call | solution.py:184
  110.4 1.6 %collective-permute-start.33 = (bf16[1,64,16,128]{3,2,1,0:T(8,128)(2,1)S(1)}, bf16[1,64,16,128]{3,2,1,0:T(8,128)(2,1)S(1)}, u32[]{:S(2)}, u32[]{:S(2)}) collective-permute-start(bf16[1,64,16,128]{3,2,1,0:T(8,128)(2,1)S(1)} %get-tuple-element.145.refs_0_), channel_id=1, source_target_pairs={{0,6},{1,7},{2,4},{3,5},{4,2},{5,3},{6,0},{7,1},{8,14},{9,15},{10,... | collective-permute-start | bytes 786440 | tf_op jit(solution)/shard_map/ppermute | solution.py:245
  112.1 2.6 %collective-permute-done.29.refs_2_ = bf16[1,64,16,128]{3,2,1,0:T(8,128)(2,1)S(1)} collective-permute-done((bf16[1,64,16,128]{3,2,1,0:T(8,128)(2,1)S(1)}, bf16[1,64,16,128]{3,2,1,0:T(8,128)(2,1)S(1)}, u32[]{:S(2)}, u32[]{:S(2)}) %collective-permute-start.29) | collective-permute-done | bytes 262176 | tf_op jit(solution)/shard_map/ppermute | solution.py:245
  115.4 2.9 %collective-permute-start.35 = (bf16[2,512,128]{2,1,0:T(8,128)(2,1)S(1)}, bf16[2,512,128]{2,1,0:T(8,128)(2,1)S(1)}, u32[]{:S(2)}, u32[]{:S(2)}) collective-permute-start(bf16[2,512,128]{2,1,0:T(8,128)(2,1)S(1)} %fusion), channel_id=1, source_target_pairs={{0,16},{8,24},{16,0},{24,8},{1,17},{9,25},{17,1},{25,9},{2,18},{10... | collective-permute-start | bytes 786440 | tf_op jit(solution)/shard_map/ppermute | solution.py:248
  118.2 2.1 %fock_terms.5 = (f32[64,64]{1,0:T(8,128)S(1)}, f32[64,64]{1,0:T(8,128)S(1)}) custom-call(s32[1]{0:T(128)} %bitcast.4.base, bf16[64,64,512]{2,1,0:T(8,128)(2,1)} %turn.1.slab, bf16[16,128]{1,0:T(8,128)(2,1)S(1)} %broadcast_in_dim.17.diagonal, bf16[1,64,16,128]{3,2,1,0:T(8,128)(2,1)S(1)} %get-tuple-element.142.refs_0_, ...), custom_call_target="tpu_custom_call" | custom-call | flops 100000000 | bytes 1 | tf_op jit(solution)/shard_map/fock_terms/pallas_call | solution.py:184
  120.4 2.1 %fock_terms.6 = (f32[64,64]{1,0:T(8,128)S(1)}, f32[64,64]{1,0:T(8,128)S(1)}) custom-call(s32[1]{0:T(128)} %bitcast.4.base, bf16[64,64,512]{2,1,0:T(8,128)(2,1)} %turn.1.slab, bf16[16,128]{1,0:T(8,128)(2,1)S(1)} %broadcast_in_dim.16.diagonal, bf16[1,64,16,128]{3,2,1,0:T(8,128)(2,1)S(1)} %get-tuple-element.145.refs_0_, ...), custom_call_target="tpu_custom_call" | custom-call | flops 100000000 | bytes 1 | tf_op jit(solution)/shard_map/fock_terms/pallas_call | solution.py:184
  122.5 1.3 collective-permute-done.34.a
  124.8 1.2 collective-permute-start.37
  126.4 1.9 %collective-permute-start.39 = (bf16[1,64,16,128]{3,2,1,0:T(8,128)(2,1)S(1)}, bf16[1,64,16,128]{3,2,1,0:T(8,128)(2,1)S(1)}, u32[]{:S(2)}, u32[]{:S(2)}) collective-permute-start(bf16[1,64,16,128]{3,2,1,0:T(8,128)(2,1)S(1)} %get-tuple-element.154.refs_0_), channel_id=1, source_target_pairs={{0,6},{1,7},{2,4},{3,5},{4,2},{5,3},{6,0},{7,1},{8,14},{9,15},{10,... | collective-permute-start | bytes 786440 | tf_op jit(solution)/shard_map/ppermute | solution.py:245
  129.2 4.8 %collective-permute-done.37.refs_1_ = bf16[1,64,16,128]{3,2,1,0:T(8,128)(2,1)S(1)} collective-permute-done((bf16[1,64,16,128]{3,2,1,0:T(8,128)(2,1)S(1)}, bf16[1,64,16,128]{3,2,1,0:T(8,128)(2,1)S(1)}, u32[]{:S(2)}, u32[]{:S(2)}) %collective-permute-start.37) | collective-permute-done | bytes 262176 | tf_op jit(solution)/shard_map/ppermute | solution.py:245
  133.9 6.0 %collective-permute-done.38.refs_2_ = bf16[1,64,16,128]{3,2,1,0:T(8,128)(2,1)S(1)} collective-permute-done((bf16[1,64,16,128]{3,2,1,0:T(8,128)(2,1)S(1)}, bf16[1,64,16,128]{3,2,1,0:T(8,128)(2,1)S(1)}, u32[]{:S(2)}, u32[]{:S(2)}) %collective-permute-start.38) | collective-permute-done | bytes 262176 | tf_op jit(solution)/shard_map/ppermute | solution.py:245
  139.9 2.1 %fock_terms.7 = (f32[64,64]{1,0:T(8,128)S(1)}, f32[64,64]{1,0:T(8,128)S(1)}) custom-call(s32[1]{0:T(128)} %bitcast.4.base, bf16[64,64,512]{2,1,0:T(8,128)(2,1)} %turn.1.slab, bf16[16,128]{1,0:T(8,128)(2,1)S(1)} %broadcast_in_dim.19.diagonal, bf16[1,64,16,128]{3,2,1,0:T(8,128)(2,1)S(1)} %get-tuple-element.154.refs_0_, ...), custom_call_target="tpu_custom_call" | custom-call | flops 2000000000 | bytes 1 | tf_op jit(solution)/shard_map/fock_terms/pallas_call | solution.py:184
  142.6 1.2 collective-permute-done.41
  144.3 2.6 %collective-permute-start.42 = (f32[32,64]{0,1:T(8,128)S(1)}, f32[32,64]{0,1:T(8,128)S(1)}, u32[]{:S(2)}, u32[]{:S(2)}) collective-permute-start(f32[32,64]{0,1:T(8,128)S(1)} %fusion.8), channel_id=1, source_target_pairs={{0,8},{8,0},{16,24},{24,16},{1,9},{9,1},{17,25},{25,17},{2,10},{10... | collective-permute-start | bytes 24584 | tf_op jit(solution)/shard_map/ppermute | solution.py:248
  146.9 1.9 %collective-permute-done.42 = f32[32,64]{0,1:T(8,128)S(1)} collective-permute-done((f32[32,64]{0,1:T(8,128)S(1)}, f32[32,64]{0,1:T(8,128)S(1)}, u32[]{:S(2)}, u32[]{:S(2)}) %collective-permute-start.42) | collective-permute-done | bytes 8224 | tf_op jit(solution)/shard_map/ppermute | solution.py:248
  148.8 2.9 %collective-permute-start.43 = (f32[32,64]{0,1:T(8,128)S(1)}, f32[32,64]{0,1:T(8,128)S(1)}, u32[]{:S(2)}, u32[]{:S(2)}) collective-permute-start(f32[32,64]{0,1:T(8,128)S(1)} %add.113), channel_id=1, source_target_pairs={{0,16},{8,24},{16,0},{24,8},{1,17},{9,25},{17,1},{25,9},{2,18},{10... | collective-permute-start | bytes 24584 | tf_op jit(solution)/shard_map/ppermute | solution.py:248
  151.7 2.0 %collective-permute-done.43 = f32[32,64]{0,1:T(8,128)S(1)} collective-permute-done((f32[32,64]{0,1:T(8,128)S(1)}, f32[32,64]{0,1:T(8,128)S(1)}, u32[]{:S(2)}, u32[]{:S(2)}) %collective-permute-start.43) | collective-permute-done | bytes 8224 | tf_op jit(solution)/shard_map/ppermute | solution.py:248
  (109 shorter events, 26.9 us)
Async XLA Ops:
  1.7 7.0 %copy-start.4 = (bf16[8,512,256]{2,1,0:T(8,128)(2,1)S(1)}, bf16[8,512,256]{2,1,0:T(8,128)(2,1)}, u32[]{:S(2)}) copy-start(bf16[8,512,256]{2,1,0:T(8,128)(2,1)} %refs_0_.7) | copy-start | bytes 6291460
  3.7 6.5 %collective-permute-start.1 = (bf16[32,64,512]{2,1,0:T(8,128)(2,1)S(1)}, bf16[32,64,512]{2,1,0:T(8,128)(2,1)S(1)}, u32[]{:S(2)}, u32[]{:S(2)}) collective-permute-start(bf16[32,64,512]{2,1,0:T(8,128)(2,1)S(1)} %constant_dynamic-slice_fusion), channel_id=1, source_target_pairs={{0,1},{1,0},{2,3},{3,2},{4,5},{5,4},{6,7},{7,6},{8,9},{9,8},{10,11... | collective-permute-start | bytes 6291464 | tf_op jit(solution)/shard_map/ppermute | solution.py:245
  4.2 26.3 %collective-permute-start = (bf16[8,512,256]{2,1,0:T(8,128)(2,1)}, bf16[8,512,256]{2,1,0:T(8,128)(2,1)}, u32[]{:S(2)}, u32[]{:S(2)}) collective-permute-start(bf16[8,512,256]{2,1,0:T(8,128)(2,1)} %left.7), channel_id=1, source_target_pairs={{0,1},{1,0},{2,3},{3,2},{4,5},{5,4},{6,7},{7,6},{8,9},{9,8},{10,11... | collective-permute-start | bytes 6291464 | tf_op jit(solution)/shard_map/ppermute | solution.py:245
  4.3 15.1 %collective-permute-start.3 = (bf16[8,128,256]{2,1,0:T(8,128)(2,1)S(1)}, bf16[8,128,256]{2,1,0:T(8,128)(2,1)S(1)}, u32[]{:S(2)}, u32[]{:S(2)}) collective-permute-start(bf16[8,128,256]{2,1,0:T(8,128)(2,1)S(1)} %slice.85), channel_id=1, source_target_pairs={{0,4},{1,5},{2,6},{3,7},{4,0},{5,1},{6,2},{7,3},{8,12},{9,13},{10,... | collective-permute-start | bytes 1572872 | tf_op jit(solution)/shard_map/ppermute | solution.py:245
  7.3 14.0 %collective-permute-start.2 = (bf16[8,128,256]{2,1,0:T(8,128)(2,1)S(1)}, bf16[8,128,256]{2,1,0:T(8,128)(2,1)S(1)}, u32[]{:S(2)}, u32[]{:S(2)}) collective-permute-start(bf16[8,128,256]{2,1,0:T(8,128)(2,1)S(1)} %slice.85), channel_id=1, source_target_pairs={{0,2},{1,3},{2,0},{3,1},{4,6},{5,7},{6,4},{7,5},{8,10},{9,11},{10,... | collective-permute-start | bytes 1572872 | tf_op jit(solution)/shard_map/ppermute | solution.py:245
  10.2 14.3 %copy-start.6 = (s32[8]{0:T(128)S(1)}, s32[8]{0:T(128)}, u32[]{:S(2)}) copy-start(s32[8]{0:T(128)} %param.7) | copy-start | bytes 100
  19.4 9.3 %collective-permute-start.6 = (bf16[8,64,256]{2,1,0:T(8,128)(2,1)S(1)}, bf16[8,64,256]{2,1,0:T(8,128)(2,1)S(1)}, u32[]{:S(2)}, u32[]{:S(2)}) collective-permute-start(bf16[8,64,256]{2,1,0:T(8,128)(2,1)S(1)} %slice.90), channel_id=1, source_target_pairs={{0,2},{1,3},{2,0},{3,1},{4,6},{5,7},{6,4},{7,5},{8,10},{9,11},{10,... | collective-permute-start | bytes 786440 | tf_op jit(solution)/shard_map/ppermute | solution.py:245
  21.2 9.3 %collective-permute-start.5 = (bf16[8,64,256]{2,1,0:T(8,128)(2,1)S(1)}, bf16[8,64,256]{2,1,0:T(8,128)(2,1)S(1)}, u32[]{:S(2)}, u32[]{:S(2)}) collective-permute-start(bf16[8,64,256]{2,1,0:T(8,128)(2,1)S(1)} %slice.89), channel_id=1, source_target_pairs={{0,4},{1,5},{2,6},{3,7},{4,0},{5,1},{6,2},{7,3},{8,12},{9,13},{10,... | collective-permute-start | bytes 786440 | tf_op jit(solution)/shard_map/ppermute | solution.py:245
  22.8 16.9 %collective-permute-start.7 = (bf16[8,128,256]{2,1,0:T(8,128)(2,1)S(1)}, bf16[8,128,256]{2,1,0:T(8,128)(2,1)S(1)}, u32[]{:S(2)}, u32[]{:S(2)}) collective-permute-start(bf16[8,128,256]{2,1,0:T(8,128)(2,1)S(1)} %get-tuple-element.89), channel_id=1, source_target_pairs={{0,4},{1,5},{2,6},{3,7},{4,0},{5,1},{6,2},{7,3},{8,12},{9,13},{10,... | collective-permute-start | bytes 1572872 | tf_op jit(solution)/shard_map/ppermute | solution.py:245
  23.3 17.6 %collective-permute-start.4 = (bf16[8,128,256]{2,1,0:T(8,128)(2,1)S(1)}, bf16[8,128,256]{2,1,0:T(8,128)(2,1)S(1)}, u32[]{:S(2)}, u32[]{:S(2)}) collective-permute-start(bf16[8,128,256]{2,1,0:T(8,128)(2,1)S(1)} %get-tuple-element.89), channel_id=1, source_target_pairs={{0,2},{1,3},{2,0},{3,1},{4,6},{5,7},{6,4},{7,5},{8,10},{9,11},{10,... | collective-permute-start | bytes 1572872 | tf_op jit(solution)/shard_map/ppermute | solution.py:245
  35.5 14.7 %collective-permute-start.11 = (bf16[2,2,512,128]{3,2,1,0:T(8,128)(2,1)S(1)}, bf16[2,2,512,128]{3,2,1,0:T(8,128)(2,1)S(1)}, u32[]{:S(2)}, u32[]{:S(2)}) collective-permute-start(bf16[2,2,512,128]{3,2,1,0:T(8,128)(2,1)S(1)} %get-tuple-element.100), channel_id=1, source_target_pairs={{0,8},{8,0},{16,24},{24,16},{1,9},{9,1},{17,25},{25,17},{2,10},{10... | collective-permute-start | bytes 1572872 | tf_op jit(solution)/shard_map/ppermute | solution.py:248
  39.7 9.3 %collective-permute-start.10 = (bf16[8,64,256]{2,1,0:T(8,128)(2,1)S(1)}, bf16[8,64,256]{2,1,0:T(8,128)(2,1)S(1)}, u32[]{:S(2)}, u32[]{:S(2)}) collective-permute-start(bf16[8,64,256]{2,1,0:T(8,128)(2,1)S(1)} %slice.92), channel_id=1, source_target_pairs={{0,2},{1,3},{2,0},{3,1},{4,6},{5,7},{6,4},{7,5},{8,10},{9,11},{10,... | collective-permute-start | bytes 786440 | tf_op jit(solution)/shard_map/ppermute | solution.py:245
  40.9 9.3 %collective-permute-start.9 = (bf16[8,64,256]{2,1,0:T(8,128)(2,1)S(1)}, bf16[8,64,256]{2,1,0:T(8,128)(2,1)S(1)}, u32[]{:S(2)}, u32[]{:S(2)}) collective-permute-start(bf16[8,64,256]{2,1,0:T(8,128)(2,1)S(1)} %slice.91), channel_id=1, source_target_pairs={{0,4},{1,5},{2,6},{3,7},{4,0},{5,1},{6,2},{7,3},{8,12},{9,13},{10,... | collective-permute-start | bytes 786440 | tf_op jit(solution)/shard_map/ppermute | solution.py:245
  41.9 16.2 %collective-permute-start.12 = (bf16[8,128,256]{2,1,0:T(8,128)(2,1)S(1)}, bf16[8,128,256]{2,1,0:T(8,128)(2,1)S(1)}, u32[]{:S(2)}, u32[]{:S(2)}) collective-permute-start(bf16[8,128,256]{2,1,0:T(8,128)(2,1)S(1)} %get-tuple-element.97), channel_id=1, source_target_pairs={{0,4},{1,5},{2,6},{3,7},{4,0},{5,1},{6,2},{7,3},{8,12},{9,13},{10,... | collective-permute-start | bytes 1572872 | tf_op jit(solution)/shard_map/ppermute | solution.py:245
  43.0 16.2 %collective-permute-start.8 = (bf16[8,128,256]{2,1,0:T(8,128)(2,1)S(1)}, bf16[8,128,256]{2,1,0:T(8,128)(2,1)S(1)}, u32[]{:S(2)}, u32[]{:S(2)}) collective-permute-start(bf16[8,128,256]{2,1,0:T(8,128)(2,1)S(1)} %get-tuple-element.97), channel_id=1, source_target_pairs={{0,2},{1,3},{2,0},{3,1},{4,6},{5,7},{6,4},{7,5},{8,10},{9,11},{10,... | collective-permute-start | bytes 1572872 | tf_op jit(solution)/shard_map/ppermute | solution.py:245
  55.3 21.4 %copy-start.2 = (f32[2,512,128]{2,1,0:T(8,128)}, f32[2,512,128]{2,1,0:T(8,128)S(1)}, u32[]{:S(2)}) copy-start(f32[2,512,128]{2,1,0:T(8,128)S(1)} %get-tuple-element.130.mine) | copy-start | bytes 1572868
  55.3 14.8 %collective-permute-start.16 = (bf16[2,2,512,128]{3,2,1,0:T(8,128)(2,1)S(1)}, bf16[2,2,512,128]{3,2,1,0:T(8,128)(2,1)S(1)}, u32[]{:S(2)}, u32[]{:S(2)}) collective-permute-start(bf16[2,2,512,128]{3,2,1,0:T(8,128)(2,1)S(1)} %get-tuple-element.111), channel_id=1, source_target_pairs={{0,8},{8,0},{16,24},{24,16},{1,9},{9,1},{17,25},{25,17},{2,10},{10... | collective-permute-start | bytes 1572872 | tf_op jit(solution)/shard_map/ppermute | solution.py:248
  58.2 9.3 %collective-permute-start.15 = (bf16[8,64,256]{2,1,0:T(8,128)(2,1)S(1)}, bf16[8,64,256]{2,1,0:T(8,128)(2,1)S(1)}, u32[]{:S(2)}, u32[]{:S(2)}) collective-permute-start(bf16[8,64,256]{2,1,0:T(8,128)(2,1)S(1)} %slice.95), channel_id=1, source_target_pairs={{0,2},{1,3},{2,0},{3,1},{4,6},{5,7},{6,4},{7,5},{8,10},{9,11},{10,... | collective-permute-start | bytes 786440 | tf_op jit(solution)/shard_map/ppermute | solution.py:245
  59.2 10.9 %collective-permute-start.14 = (bf16[8,64,256]{2,1,0:T(8,128)(2,1)S(1)}, bf16[8,64,256]{2,1,0:T(8,128)(2,1)S(1)}, u32[]{:S(2)}, u32[]{:S(2)}) collective-permute-start(bf16[8,64,256]{2,1,0:T(8,128)(2,1)S(1)} %slice.94), channel_id=1, source_target_pairs={{0,4},{1,5},{2,6},{3,7},{4,0},{5,1},{6,2},{7,3},{8,12},{9,13},{10,... | collective-permute-start | bytes 786440 | tf_op jit(solution)/shard_map/ppermute | solution.py:245
  60.9 18.2 %collective-permute-start.18 = (bf16[8,128,256]{2,1,0:T(8,128)(2,1)}, bf16[8,128,256]{2,1,0:T(8,128)(2,1)S(1)}, u32[]{:S(2)}, u32[]{:S(2)}) collective-permute-start(bf16[8,128,256]{2,1,0:T(8,128)(2,1)} %get-tuple-element.108), channel_id=1, source_target_pairs={{0,4},{1,5},{2,6},{3,7},{4,0},{5,1},{6,2},{7,3},{8,12},{9,13},{10,... | collective-permute-start | bytes 1572872 | tf_op jit(solution)/shard_map/ppermute | solution.py:245
  61.3 19.5 %collective-permute-start.13 = (bf16[8,128,256]{2,1,0:T(8,128)(2,1)}, bf16[8,128,256]{2,1,0:T(8,128)(2,1)S(1)}, u32[]{:S(2)}, u32[]{:S(2)}) collective-permute-start(bf16[8,128,256]{2,1,0:T(8,128)(2,1)} %get-tuple-element.108), channel_id=1, source_target_pairs={{0,2},{1,3},{2,0},{3,1},{4,6},{5,7},{6,4},{7,5},{8,10},{9,11},{10,... | collective-permute-start | bytes 1572872 | tf_op jit(solution)/shard_map/ppermute | solution.py:245
  67.5 10.8 %collective-permute-start.17 = (bf16[2,512,128]{2,1,0:T(8,128)(2,1)S(1)}, bf16[2,512,128]{2,1,0:T(8,128)(2,1)S(1)}, u32[]{:S(2)}, u32[]{:S(2)}) collective-permute-start(bf16[2,512,128]{2,1,0:T(8,128)(2,1)S(1)} %fusion.3), channel_id=1, source_target_pairs={{0,16},{8,24},{16,0},{24,8},{1,17},{9,25},{17,1},{25,9},{2,18},{10... | collective-permute-start | bytes 786440 | tf_op jit(solution)/shard_map/ppermute | solution.py:248
  76.7 19.4 %collective-permute-start.21 = (bf16[2,2,512,128]{3,2,1,0:T(8,128)(2,1)}, bf16[2,2,512,128]{3,2,1,0:T(8,128)(2,1)S(1)}, u32[]{:S(2)}, u32[]{:S(2)}) collective-permute-start(bf16[2,2,512,128]{3,2,1,0:T(8,128)(2,1)} %get-tuple-element.129), channel_id=1, source_target_pairs={{0,8},{8,0},{16,24},{24,16},{1,9},{9,1},{17,25},{25,17},{2,10},{10... | collective-permute-start | bytes 1572872 | tf_op jit(solution)/shard_map/ppermute | solution.py:248
  79.9 8.8 %collective-permute-start.20 = (bf16[8,64,256]{2,1,0:T(8,128)(2,1)}, bf16[8,64,256]{2,1,0:T(8,128)(2,1)}, u32[]{:S(2)}, u32[]{:S(2)}) collective-permute-start(bf16[8,64,256]{2,1,0:T(8,128)(2,1)} %slice.98), channel_id=1, source_target_pairs={{0,2},{1,3},{2,0},{3,1},{4,6},{5,7},{6,4},{7,5},{8,10},{9,11},{10,... | collective-permute-start | bytes 786440 | tf_op jit(solution)/shard_map/ppermute | solution.py:245
  81.6 7.7 %collective-permute-start.19 = (bf16[8,64,256]{2,1,0:T(8,128)(2,1)}, bf16[8,64,256]{2,1,0:T(8,128)(2,1)}, u32[]{:S(2)}, u32[]{:S(2)}) collective-permute-start(bf16[8,64,256]{2,1,0:T(8,128)(2,1)} %slice.97), channel_id=1, source_target_pairs={{0,4},{1,5},{2,6},{3,7},{4,0},{5,1},{6,2},{7,3},{8,12},{9,13},{10,... | collective-permute-start | bytes 786440 | tf_op jit(solution)/shard_map/ppermute | solution.py:245
  83.2 14.0 %collective-permute-start.22 = (bf16[2,512,128]{2,1,0:T(8,128)(2,1)}, bf16[2,512,128]{2,1,0:T(8,128)(2,1)S(1)}, u32[]{:S(2)}, u32[]{:S(2)}) collective-permute-start(bf16[2,512,128]{2,1,0:T(8,128)(2,1)} %fusion.2), channel_id=1, source_target_pairs={{0,16},{8,24},{16,0},{24,8},{1,17},{9,25},{17,1},{25,9},{2,18},{10... | collective-permute-start | bytes 786440 | tf_op jit(solution)/shard_map/ppermute | solution.py:248
  84.9 15.0 %copy-start.3 = (f32[2,512,128]{2,1,0:T(8,128)S(1)}, f32[2,512,128]{2,1,0:T(8,128)}, u32[]{:S(2)}) copy-start(f32[2,512,128]{2,1,0:T(8,128)} %copy-done.2) | copy-start | bytes 1572868
  84.9 15.8 %collective-permute-start.23 = (bf16[1,64,16,128]{3,2,1,0:T(8,128)(2,1)S(1)}, bf16[1,64,16,128]{3,2,1,0:T(8,128)(2,1)S(1)}, u32[]{:S(2)}, u32[]{:S(2)}) collective-permute-start(bf16[1,64,16,128]{3,2,1,0:T(8,128)(2,1)S(1)} %get-tuple-element.134.refs_0_), channel_id=1, source_target_pairs={{0,2},{1,3},{2,0},{3,1},{4,6},{5,7},{6,4},{7,5},{8,10},{9,11},{10,... | collective-permute-start | bytes 786440 | tf_op jit(solution)/shard_map/ppermute | solution.py:245
  88.7 13.7 %collective-permute-start.24 = (bf16[1,64,16,128]{3,2,1,0:T(8,128)(2,1)S(1)}, bf16[1,64,16,128]{3,2,1,0:T(8,128)(2,1)S(1)}, u32[]{:S(2)}, u32[]{:S(2)}) collective-permute-start(bf16[1,64,16,128]{3,2,1,0:T(8,128)(2,1)S(1)} %get-tuple-element.134.refs_0_), channel_id=1, source_target_pairs={{0,4},{1,5},{2,6},{3,7},{4,0},{5,1},{6,2},{7,3},{8,12},{9,13},{10,... | collective-permute-start | bytes 786440 | tf_op jit(solution)/shard_map/ppermute | solution.py:245
  89.3 13.4 %collective-permute-start.25 = (bf16[1,64,16,128]{3,2,1,0:T(8,128)(2,1)S(1)}, bf16[1,64,16,128]{3,2,1,0:T(8,128)(2,1)S(1)}, u32[]{:S(2)}, u32[]{:S(2)}) collective-permute-start(bf16[1,64,16,128]{3,2,1,0:T(8,128)(2,1)S(1)} %get-tuple-element.134.refs_0_), channel_id=1, source_target_pairs={{0,6},{1,7},{2,4},{3,5},{4,2},{5,3},{6,0},{7,1},{8,14},{9,15},{10,... | collective-permute-start | bytes 786440 | tf_op jit(solution)/shard_map/ppermute | solution.py:245
  96.0 10.5 %collective-permute-start.26 = (bf16[1,2,512,128]{3,2,1,0:T(8,128)(2,1)S(1)}, bf16[1,2,512,128]{3,2,1,0:T(8,128)(2,1)S(1)}, u32[]{:S(2)}, u32[]{:S(2)}) collective-permute-start(bf16[1,2,512,128]{3,2,1,0:T(8,128)(2,1)S(1)} %get-tuple-element.137), channel_id=1, source_target_pairs={{0,8},{8,0},{16,24},{24,16},{1,9},{9,1},{17,25},{25,17},{2,10},{10... | collective-permute-start | bytes 786440 | tf_op jit(solution)/shard_map/ppermute | solution.py:248
  97.3 10.4 %collective-permute-start.27 = (bf16[2,512,128]{2,1,0:T(8,128)(2,1)S(1)}, bf16[2,512,128]{2,1,0:T(8,128)(2,1)S(1)}, u32[]{:S(2)}, u32[]{:S(2)}) collective-permute-start(bf16[2,512,128]{2,1,0:T(8,128)(2,1)S(1)} %fusion.1), channel_id=1, source_target_pairs={{0,16},{8,24},{16,0},{24,8},{1,17},{9,25},{17,1},{25,9},{2,18},{10... | collective-permute-start | bytes 786440 | tf_op jit(solution)/shard_map/ppermute | solution.py:248
  100.7 9.7 %collective-permute-start.28 = (bf16[1,64,16,128]{3,2,1,0:T(8,128)(2,1)S(1)}, bf16[1,64,16,128]{3,2,1,0:T(8,128)(2,1)S(1)}, u32[]{:S(2)}, u32[]{:S(2)}) collective-permute-start(bf16[1,64,16,128]{3,2,1,0:T(8,128)(2,1)S(1)} %get-tuple-element.142.refs_0_), channel_id=1, source_target_pairs={{0,2},{1,3},{2,0},{3,1},{4,6},{5,7},{6,4},{7,5},{8,10},{9,11},{10,... | collective-permute-start | bytes 786440 | tf_op jit(solution)/shard_map/ppermute | solution.py:245
  102.3 12.4 %collective-permute-start.29 = (bf16[1,64,16,128]{3,2,1,0:T(8,128)(2,1)S(1)}, bf16[1,64,16,128]{3,2,1,0:T(8,128)(2,1)S(1)}, u32[]{:S(2)}, u32[]{:S(2)}) collective-permute-start(bf16[1,64,16,128]{3,2,1,0:T(8,128)(2,1)S(1)} %get-tuple-element.142.refs_0_), channel_id=1, source_target_pairs={{0,4},{1,5},{2,6},{3,7},{4,0},{5,1},{6,2},{7,3},{8,12},{9,13},{10,... | collective-permute-start | bytes 786440 | tf_op jit(solution)/shard_map/ppermute | solution.py:245
  102.7 12.7 %collective-permute-start.30 = (bf16[1,64,16,128]{3,2,1,0:T(8,128)(2,1)S(1)}, bf16[1,64,16,128]{3,2,1,0:T(8,128)(2,1)S(1)}, u32[]{:S(2)}, u32[]{:S(2)}) collective-permute-start(bf16[1,64,16,128]{3,2,1,0:T(8,128)(2,1)S(1)} %get-tuple-element.142.refs_0_), channel_id=1, source_target_pairs={{0,6},{1,7},{2,4},{3,5},{4,2},{5,3},{6,0},{7,1},{8,14},{9,15},{10,... | collective-permute-start | bytes 786440 | tf_op jit(solution)/shard_map/ppermute | solution.py:245
  108.5 11.9 %collective-permute-start.31 = (bf16[1,64,16,128]{3,2,1,0:T(8,128)(2,1)S(1)}, bf16[1,64,16,128]{3,2,1,0:T(8,128)(2,1)S(1)}, u32[]{:S(2)}, u32[]{:S(2)}) collective-permute-start(bf16[1,64,16,128]{3,2,1,0:T(8,128)(2,1)S(1)} %get-tuple-element.145.refs_0_), channel_id=1, source_target_pairs={{0,2},{1,3},{2,0},{3,1},{4,6},{5,7},{6,4},{7,5},{8,10},{9,11},{10,... | collective-permute-start | bytes 786440 | tf_op jit(solution)/shard_map/ppermute | solution.py:245
  109.7 10.7 %collective-permute-start.32 = (bf16[1,64,16,128]{3,2,1,0:T(8,128)(2,1)S(1)}, bf16[1,64,16,128]{3,2,1,0:T(8,128)(2,1)S(1)}, u32[]{:S(2)}, u32[]{:S(2)}) collective-permute-start(bf16[1,64,16,128]{3,2,1,0:T(8,128)(2,1)S(1)} %get-tuple-element.145.refs_0_), channel_id=1, source_target_pairs={{0,4},{1,5},{2,6},{3,7},{4,0},{5,1},{6,2},{7,3},{8,12},{9,13},{10,... | collective-permute-start | bytes 786440 | tf_op jit(solution)/shard_map/ppermute | solution.py:245
  110.4 10.0 %collective-permute-start.33 = (bf16[1,64,16,128]{3,2,1,0:T(8,128)(2,1)S(1)}, bf16[1,64,16,128]{3,2,1,0:T(8,128)(2,1)S(1)}, u32[]{:S(2)}, u32[]{:S(2)}) collective-permute-start(bf16[1,64,16,128]{3,2,1,0:T(8,128)(2,1)S(1)} %get-tuple-element.145.refs_0_), channel_id=1, source_target_pairs={{0,6},{1,7},{2,4},{3,5},{4,2},{5,3},{6,0},{7,1},{8,14},{9,15},{10,... | collective-permute-start | bytes 786440 | tf_op jit(solution)/shard_map/ppermute | solution.py:245
  114.7 9.2 %collective-permute-start.34 = (bf16[1,2,512,128]{3,2,1,0:T(8,128)(2,1)S(1)}, bf16[1,2,512,128]{3,2,1,0:T(8,128)(2,1)S(1)}, u32[]{:S(2)}, u32[]{:S(2)}) collective-permute-start(bf16[1,2,512,128]{3,2,1,0:T(8,128)(2,1)S(1)} %get-tuple-element.149), channel_id=1, source_target_pairs={{0,8},{8,0},{16,24},{24,16},{1,9},{9,1},{17,25},{25,17},{2,10},{10... | collective-permute-start | bytes 786440 | tf_op jit(solution)/shard_map/ppermute | solution.py:248
  115.4 8.5 %collective-permute-start.35 = (bf16[2,512,128]{2,1,0:T(8,128)(2,1)S(1)}, bf16[2,512,128]{2,1,0:T(8,128)(2,1)S(1)}, u32[]{:S(2)}, u32[]{:S(2)}) collective-permute-start(bf16[2,512,128]{2,1,0:T(8,128)(2,1)S(1)} %fusion), channel_id=1, source_target_pairs={{0,16},{8,24},{16,0},{24,8},{1,17},{9,25},{17,1},{25,9},{2,18},{10... | collective-permute-start | bytes 786440 | tf_op jit(solution)/shard_map/ppermute | solution.py:248
  124.7 3.6 %collective-permute-start.36 = (bf16[512,512]{1,0:T(8,128)(2,1)S(1)}, bf16[512,512]{1,0:T(8,128)(2,1)S(1)}, u32[]{:S(2)}, u32[]{:S(2)}) collective-permute-start(bf16[512,512]{1,0:T(8,128)(2,1)S(1)} %get-tuple-element.151), channel_id=1, source_target_pairs={{0,1},{1,0},{2,3},{3,2},{4,5},{5,4},{6,7},{7,6},{8,9},{9,8},{10,11... | collective-permute-start | bytes 1572872 | tf_op jit(solution)/shard_map/ppermute | solution.py:245
  124.8 9.2 %collective-permute-start.37 = (bf16[1,64,16,128]{3,2,1,0:T(8,128)(2,1)S(1)}, bf16[1,64,16,128]{3,2,1,0:T(8,128)(2,1)S(1)}, u32[]{:S(2)}, u32[]{:S(2)}) collective-permute-start(bf16[1,64,16,128]{3,2,1,0:T(8,128)(2,1)S(1)} %get-tuple-element.154.refs_0_), channel_id=1, source_target_pairs={{0,2},{1,3},{2,0},{3,1},{4,6},{5,7},{6,4},{7,5},{8,10},{9,11},{10,... | collective-permute-start | bytes 786440 | tf_op jit(solution)/shard_map/ppermute | solution.py:245
  125.9 14.0 %collective-permute-start.38 = (bf16[1,64,16,128]{3,2,1,0:T(8,128)(2,1)S(1)}, bf16[1,64,16,128]{3,2,1,0:T(8,128)(2,1)S(1)}, u32[]{:S(2)}, u32[]{:S(2)}) collective-permute-start(bf16[1,64,16,128]{3,2,1,0:T(8,128)(2,1)S(1)} %get-tuple-element.154.refs_0_), channel_id=1, source_target_pairs={{0,4},{1,5},{2,6},{3,7},{4,0},{5,1},{6,2},{7,3},{8,12},{9,13},{10,... | collective-permute-start | bytes 786440 | tf_op jit(solution)/shard_map/ppermute | solution.py:245
  126.4 13.5 %collective-permute-start.39 = (bf16[1,64,16,128]{3,2,1,0:T(8,128)(2,1)S(1)}, bf16[1,64,16,128]{3,2,1,0:T(8,128)(2,1)S(1)}, u32[]{:S(2)}, u32[]{:S(2)}) collective-permute-start(bf16[1,64,16,128]{3,2,1,0:T(8,128)(2,1)S(1)} %get-tuple-element.154.refs_0_), channel_id=1, source_target_pairs={{0,6},{1,7},{2,4},{3,5},{4,2},{5,3},{6,0},{7,1},{8,14},{9,15},{10,... | collective-permute-start | bytes 786440 | tf_op jit(solution)/shard_map/ppermute | solution.py:245
  128.3 14.0 %collective-permute-start.40 = (bf16[32,64]{1,0:T(8,128)(2,1)S(1)}, bf16[32,64]{1,0:T(8,128)(2,1)S(1)}, u32[]{:S(2)}, u32[]{:S(2)}) collective-permute-start(bf16[32,64]{1,0:T(8,128)(2,1)S(1)} %copy-done.5), channel_id=1, source_target_pairs={{0,1},{1,0},{2,3},{3,2},{4,5},{5,4},{6,7},{7,6},{8,9},{9,8},{10,11... | collective-permute-start | bytes 12296 | tf_op jit(solution)/shard_map/ppermute | solution.py:245
  142.6 1.2 collective-permute-start.41
  144.3 4.5 %collective-permute-start.42 = (f32[32,64]{0,1:T(8,128)S(1)}, f32[32,64]{0,1:T(8,128)S(1)}, u32[]{:S(2)}, u32[]{:S(2)}) collective-permute-start(f32[32,64]{0,1:T(8,128)S(1)} %fusion.8), channel_id=1, source_target_pairs={{0,8},{8,0},{16,24},{24,16},{1,9},{9,1},{17,25},{25,17},{2,10},{10... | collective-permute-start | bytes 24584 | tf_op jit(solution)/shard_map/ppermute | solution.py:248
  148.8 5.0 %collective-permute-start.43 = (f32[32,64]{0,1:T(8,128)S(1)}, f32[32,64]{0,1:T(8,128)S(1)}, u32[]{:S(2)}, u32[]{:S(2)}) collective-permute-start(f32[32,64]{0,1:T(8,128)S(1)} %add.113), channel_id=1, source_target_pairs={{0,16},{8,24},{16,0},{24,8},{1,17},{9,25},{17,1},{25,9},{2,18},{10... | collective-permute-start | bytes 24584 | tf_op jit(solution)/shard_map/ppermute | solution.py:248
  (3 other events, 13.3 us)
